TPU v7x, 32 devices: a whole 2x2x4 slice. The times are simulated.
32 devices in a mesh: grp: 2 (over y), site: 4 (over x, core), spin: 4 (over z).
Axes of the slice: x: 2, y: 2, z: 4, core: 2. Of those that a mesh axis runs over, the one named last changes fastest.
Arguments:
- walkers: bfloat16 [8, 512, 256, 256], P(('grp', 'spin'), 'site'), parts along dimension 0, may hold values from -90 to 90
- fields: bfloat16 [8, 1, 512, 256], P(('grp', 'spin'), None, 'site'), parts along dimension 0, may hold values from -3 to 3
- kinetic_x: bfloat16 [512, 512], replicated, may hold values from -0.5 to 1.5
- kinetic_y: bfloat16 [256, 256], replicated, may hold values from -0.5 to 1.5
Outputs:
- orthonormal: bfloat16 [8, 512, 256, 256], P(('grp', 'spin'), 'site'), parts along dimension 0
- triangle: float32 [8, 256, 256], P(('grp', 'spin')), parts along dimension 0
There are 2 independent parts, one for each index of `grp`. A program takes and returns all parts, laid end to end along the dimension named above; an argument that names none is the same for every part. Nothing has to cross between parts.
All inputs are finite; a program needn't handle non-finite values.
Results may differ from a plain program's by a relative error of at most 0.0095.
Values may be sent and summed in bfloat16 or wider, within the bound.
No kernel may reach another device: no remote copies, remote signals or barrier semaphores. Data moves between devices by JAX's collectives and lax.ppermute only.
A program may use at most 128 MiB of HBM per device.

v0:
```python
import functools

import jax
import jax.numpy as jnp
from jax import lax
from jax.experimental import pallas as pl
from jax.experimental.pallas import tpu as pltpu
from jax.sharding import PartitionSpec as P

ROWS = 16
LANES = 128
PAD = 8
BLOCK = 64
VMEM_LIMIT = 32 * 1024 * 1024
VMEM_MOST = 56 * 1024 * 1024


def partner(device, step, count):
    if count & (count - 1) == 0:
        return device ^ step
    return (step - device + count) % count


def trade(piece, step, count):
    if step == 0 and count & (count - 1) == 0:
        return piece
    return lax.ppermute(piece, "site", [(i, partner(i, step, count)) for i in range(count)])


def tie(*arrays):
    return lax.optimization_barrier(arrays)


def settings(limit=VMEM_LIMIT):
    return dict(
        compiler_params=pltpu.CompilerParams(vmem_limit_bytes=limit),
        cost_estimate=pl.CostEstimate(flops=1000, bytes_accessed=1000, transcendentals=0),
    )


def y_kernel(count, band, cuts, window, walkers, kinetic, *rest):
    outs, own, turned = rest[-2 - len(cuts) : -2], rest[-2], rest[-1]
    me = lax.axis_index("site")
    depth = own.shape[0]

    @pl.when(pl.program_id(0) == 0)
    def _():
        row = 0
        for s, first, size in cuts:
            start = pl.multiple_of(partner(me, s, count) * band + first, ROWS)
            own[pl.ds(row, size), :] = kinetic[pl.ds(start, size), :]
            row += size

    for r in range(ROWS):
        line = jnp.dot(own[...], walkers[r], preferred_element_type=jnp.float32)
        for h in range(turned.shape[0]):
            turned[h, pl.ds(r, depth, stride=ROWS + PAD), :] = line[:, h * LANES : (h + 1) * LANES]
    row = 0
    for (s, first, size), out in zip(cuts, outs):
        for h in range(turned.shape[0]):
            piece = turned[h, pl.ds(row * (ROWS + PAD), size * (ROWS + PAD)), :]
            piece = piece.reshape(size, ROWS + PAD, LANES)[:, :ROWS]
            out[:size, :, h * LANES : (h + 1) * LANES] = piece.astype(out.dtype)
        row += size
        if window:
            begin = pl.multiple_of(partner(me, s, count) * band // window * window, LANES)
            across = out.shape[2] // window
            for line in range(0, rest[0].shape[0], ROWS):
                place, part = size + line // ROWS // across, line // ROWS % across
                values = rest[0][pl.ds(line, ROWS), pl.ds(begin, window)]
                out[place, :, part * window : (part + 1) * window] = values


def apply_y(walkers, kinetic_y, count, cuts, sizes, fields=None, window=0):
    lines, width, orbitals = walkers.shape
    depth = sum(size for _, _, size in cuts)
    used = max(sizes)
    extra = fields.size // fields.shape[1] * window // (ROWS * orbitals) if window else 0

    def out_spec(cut, size):
        late = (used - size) // ROWS
        return pl.BlockSpec(
            (cut[2] + extra, ROWS, orbitals), lambda i: (0, jnp.maximum(i - late, 0) if late else i, 0)
        )

    return pl.pallas_call(
        functools.partial(y_kernel, count, width // count, cuts, window),
        grid=(used // ROWS,),
        in_specs=[
            pl.BlockSpec((ROWS, width, orbitals), lambda i: (i, 0, 0)),
            pl.BlockSpec((width, width), lambda i: (0, 0)),
        ]
        + [pl.BlockSpec((lines, width), lambda i: (0, 0))] * (window > 0),
        out_specs=[out_spec(cut, size) for cut, size in zip(cuts, sizes)],
        out_shape=[
            jax.ShapeDtypeStruct((cut[2] + extra, size, orbitals), jnp.bfloat16)
            for cut, size in zip(cuts, sizes)
        ],
        scratch_shapes=[
            pltpu.VMEM((depth, width), jnp.bfloat16),
            pltpu.VMEM((orbitals // LANES, depth * (ROWS + PAD), LANES), jnp.float32),
        ],
        **settings(VMEM_MOST),
    )(walkers, kinetic_y, *([fields] if window else []))


def x_kernel(count, group, *refs):
    pieces, (field, kinetic, before) = refs[: -count - 4], refs[-count - 4 : -count - 1]
    outs, gram = refs[-count - 1 : -1], refs[-1]

    @pl.when(pl.program_id(0) == 0)
    def _():
        gram[...] = before[...]

    factor = jnp.exp(field[0].astype(jnp.float32))
    total = jnp.zeros(gram.shape, jnp.float32)
    for j in range(group):
        lines = jnp.concatenate([piece[j] for piece in pieces], axis=0)
        moved = jnp.dot(kinetic[...], lines, preferred_element_type=jnp.float32)
        moved = moved.astype(jnp.bfloat16).astype(jnp.float32)
        scaled = (factor[:, j : j + 1] * moved).astype(jnp.bfloat16)
        block = scaled.shape[0] // count
        for t in range(count):
            outs[t][j] = scaled[t * block : (t + 1) * block]
        total += lax.dot_general(
            scaled, scaled, (((0,), (0,)), ((), ())), preferred_element_type=jnp.float32
        )
    gram[...] += total


def apply_x(pieces, fields, kinetic_x, gram, count, first, part):
    orbitals = gram.shape[0]
    length = kinetic_x.shape[0]
    group = fields.shape[2]

    def spec(array, begin):
        offset = (first - begin) // group
        return pl.BlockSpec((group,) + array.shape[1:], lambda i: (i + offset, 0, 0))

    square = pl.BlockSpec((orbitals, orbitals), lambda i: (0, 0))
    out = (part, length // count, orbitals)
    results = pl.pallas_call(
        functools.partial(x_kernel, count, group),
        grid=(part // group,),
        in_specs=[spec(*piece) for piece in pieces]
        + [
            pl.BlockSpec((1, length, group), lambda i: (i + first // group, 0, 0)),
            pl.BlockSpec((length, length), lambda i: (0, 0)),
            square,
        ],
        out_specs=[pl.BlockSpec((group,) + out[1:], lambda i: (i, 0, 0))] * count + [square],
        out_shape=[jax.ShapeDtypeStruct(out, jnp.bfloat16)] * count
        + [jax.ShapeDtypeStruct((orbitals, orbitals), jnp.float32)],
        **settings(),
    )(*[array for array, _ in pieces], fields, kinetic_x, gram)
    return results[:count], results[count]


def last_kernel(where, piece, inverse, *rest):
    out, turned = rest[-2], rest[-1]
    part, rows, orbitals = piece.shape
    product = jnp.dot(
        piece[...].reshape(part * rows, orbitals),
        inverse[...],
        preferred_element_type=jnp.float32,
    )
    for h in range(turned.shape[0]):
        for y in range(part):
            lines = product[y * rows : (y + 1) * rows, h * LANES : (h + 1) * LANES]
            turned[h, pl.ds(y * (rows + PAD), rows), :] = lines
        for r in range(rows):
            line = turned[h, pl.ds(r, part, stride=rows + PAD), :]
            out[r, :, h * LANES : (h + 1) * LANES] = line.astype(out.dtype)


def finish(result, piece, inverse, place, width):
    part, lines, orbitals = piece.shape
    begun = result is not None
    rows = 4 * ROWS if lines % (4 * ROWS) == 0 else ROWS
    return pl.pallas_call(
        last_kernel,
        grid_spec=pltpu.PrefetchScalarGridSpec(
            num_scalar_prefetch=1,
            grid=(lines // rows,),
            in_specs=[
                pl.BlockSpec((part, rows, orbitals), lambda i, where: (0, i, 0)),
                pl.BlockSpec((orbitals, orbitals), lambda i, where: (0, 0)),
            ]
            + [pl.BlockSpec(memory_space=pl.ANY)] * begun,
            out_specs=pl.BlockSpec((rows, part, orbitals), lambda i, where: (i, where[0], 0)),
            scratch_shapes=[pltpu.VMEM((orbitals // LANES, part * (rows + PAD), LANES), jnp.float32)],
        ),
        out_shape=jax.ShapeDtypeStruct((lines, width, orbitals), jnp.bfloat16),
        input_output_aliases={3: 0} if begun else {},
        **settings(),
    )(place.reshape(1), piece, inverse, *([result] if begun else []))


def factor_kernel(scale, gram, lower, inverse, work, upper):
    size = gram.shape[0]
    row = lax.broadcasted_iota(jnp.int32, (size, size), 0)
    column = lax.broadcasted_iota(jnp.int32, (size, size), 1)
    work[:, :size] = gram[...] * scale
    work[:, size:] = jnp.where(row == column, 1.0, 0.0)
    line = lax.broadcasted_iota(jnp.int32, (BLOCK, 2 * BLOCK), 0)
    lane = lax.broadcasted_iota(jnp.int32, (BLOCK, 2 * BLOCK), 1)
    identity = jnp.where(lane == line, 1.0, 0.0)[:, :BLOCK]
    dot = functools.partial(
        jnp.dot, precision=lax.Precision.HIGHEST, preferred_element_type=jnp.float32
    )
    for begin in range(0, size, BLOCK):
        end = begin + BLOCK
        both = jnp.concatenate([work[begin:end, begin:end], identity], axis=1)
        for j in range(BLOCK):
            pivot_column = jnp.broadcast_to(both[:, j : j + 1], both.shape)
            pivot = jnp.broadcast_to(pivot_column[j : j + 1], both.shape)
            root = lax.rsqrt(pivot)
            root = root * (1.5 - 0.5 * pivot * root * root)
            pivot_row = jnp.broadcast_to(both[j : j + 1], both.shape) * root
            below = both - pivot_column * root * pivot_row
            both = jnp.where(line > j, below, jnp.where(line == j, pivot_row, both))
        panel = dot(both[:, BLOCK:], work[begin:end, :])
        upper[begin:end, :] = panel[:, :size]
        work[begin:end, size:] = panel[:, size:]
        if end < size:
            work[end:, :] -= dot(panel[:, end:size].T, panel)
    lower[...] = jnp.where(row >= column, upper[...].T, 0.0)
    inverse[...] = work[:, size:].T.astype(inverse.dtype)


def factor(gram, scale):
    size = gram.shape[0]
    return pl.pallas_call(
        functools.partial(factor_kernel, scale),
        out_shape=[
            jax.ShapeDtypeStruct((size, size), jnp.float32),
            jax.ShapeDtypeStruct((size, size), jnp.bfloat16),
        ],
        scratch_shapes=[
            pltpu.VMEM((size, 2 * size), jnp.float32),
            pltpu.VMEM((size, size), jnp.float32),
        ],
        **settings(),
    )(gram)


def one_determinant(walkers, fields, kinetic_x, kinetic_y, count):
    lines, width, orbitals = walkers.shape
    me = lax.axis_index("site")
    band = width // count
    part = ROWS if band % ROWS == 0 else band
    group = 8 if part % 8 == 0 else part
    wide = 2 * part if band % (2 * part) == 0 else band
    steps = range(count)
    order = jnp.stack([partner(me, s, count) for s in steps])

    window = max(LANES, band)
    extra = lines * window // (ROWS * orbitals)
    far = [s for s in steps if s > 1 and lines > ROWS]
    near = [s for s in steps if s not in far]
    head = {}
    if far:
        arrays = apply_y(
            walkers, kinetic_y, count, [(s, 0, band) for s in far], [ROWS] * len(far), fields, window
        )
        kinetic_y, *arrays = tie(kinetic_y, *arrays)
        head = {s: trade(a, s, count) for s, a in zip(far, arrays)}
    cuts = [(s, first, wide) for first in range(0, band, wide) for s in far]
    cuts += [(s, 0, band) for s in near]
    sizes = [lines if s in near else lines - ROWS for s, _, _ in cuts]
    arrays = apply_y(walkers, kinetic_y, count, cuts, sizes)
    tail = {(s, first): a for (s, first, _), a in zip(cuts, arrays)}
    late = [key for key in tail if key[0] in near or key[1] > 0]
    if far:
        held = tie(*[tail[key] for key in late], *[head[s] for s in far])
        tail.update(zip(late, held))
        head.update(zip(far, held[len(late) :]))
    for s in far:
        tail[s, 0] = trade(tail[s, 0], s, count)
    for s in near:
        tail[s, 0] = trade(tail[s, 0], s, count)
    by_band = jnp.take(fields.reshape(lines, count, band), order, axis=1)
    by_band, tail[near[-1], 0] = tie(by_band, tail[near[-1], 0])
    own_fields = {s: trade(by_band[:, s], s, count) for s in near}
    for first in range(wide, band, wide):
        for s in far:
            if first > wide:
                tail[s, first], tail[s, first - 2 * wide] = tie(
                    tail[s, first], tail[s, first - 2 * wide]
                )
            elif s != far[0]:
                tail[s, first], tail[near[-1], 0] = tie(tail[s, first], tail[near[-1], 0])
            tail[s, first] = trade(tail[s, first], s, count)
    for s in far:
        sent = head[s][band:].reshape(extra, ROWS, orbitals // window, window)
        sent = jnp.swapaxes(sent, 1, 2).reshape(lines, window)
        own_fields[s] = lax.dynamic_slice_in_dim(sent, me * band % window, band, 1)
    own_fields = jnp.stack([own_fields[s] for s in steps])
    own_fields = own_fields.reshape(count * lines, band // group, group).swapaxes(0, 1)
    turned_x = kinetic_x.reshape(count, lines, count, lines)
    turned_x = jnp.take(jnp.take(turned_x, order, axis=0), order, axis=2).reshape(kinetic_x.shape)

    gram = jnp.zeros((orbitals, orbitals), jnp.float32)
    ready = []
    for first in range(0, band, part):
        pieces = []
        for s in steps:
            if s in far:
                pieces.append((head[s], 0))
            begin = first // wide * wide if s in far else 0
            pieces.append((tail[s, begin], begin))
        scaled, gram = apply_x(pieces, own_fields, turned_x, gram, count, first, part)
        ready.append(scaled)

    back = []
    half = orbitals // 2
    for c in range(min(2, len(ready))):
        back.append(dict(enumerate(ready[c])))
        for s in far:
            if c == 1 and (s, wide) in tail:
                back[c][s], tail[s, wide] = tie(back[c][s], tail[s, wide])
            if c == 1 and s != far[0]:
                back[c][s], back[0][far[-1]] = tie(back[c][s], back[0][far[-1]])
            back[c][s] = trade(back[c][s], s, count)
    if count & (count - 1) == 0 and count > 1:
        core = me & 1
        if far:
            gram, back[0][far[0]] = tie(gram, back[0][far[0]])
        mine = lax.dynamic_slice_in_dim(gram, core * half, half, 0)
        mine = mine + trade(lax.dynamic_slice_in_dim(gram, (1 - core) * half, half, 0), 1, count)
        step = 2
        while step < count:
            mine = mine + trade(mine, step, count)
            step *= 2
        if len(back) > 1 and far:
            mine, back[1][far[0]] = tie(mine, back[1][far[0]])
        other = trade(mine, 1, count)
        gram = jnp.where(core == 0, jnp.concatenate([mine, other]), jnp.concatenate([other, mine]))
    else:
        gram = lax.psum(gram, "site")
    lower, inverse = factor(gram, 1.0 / (count * lines * width))

    for c in range(2, len(ready)):
        back.append(dict(enumerate(ready[c])))
        for s in far:
            if c == 2:
                back[c][s], back[0][s] = tie(back[c][s], back[0][s])
            else:
                back[c][s], inverse = tie(back[c][s], inverse)
            back[c][s] = trade(back[c][s], s, count)
    for c in range(len(back)):
        for s in near:
            back[c][s], gram = tie(back[c][s], gram)
            back[c][s] = trade(back[c][s], s, count)

    result = None
    for c in range(len(back)):
        for s in steps:
            place = order[s] * (band // part) + c
            result = finish(result, back[c][s], inverse, place, width)
    return result, lower


def per_device(count, walkers, fields, kinetic_x, kinetic_y):
    results = [
        one_determinant(walkers[i], fields[i, 0], kinetic_x, kinetic_y, count)
        for i in range(walkers.shape[0])
    ]
    return tuple(jnp.stack(part) for part in zip(*results))


def solution(mesh):
    placed = (
        P(("grp", "spin"), "site", None, None),
        P(("grp", "spin"), None, "site", None),
        P(),
        P(),
    )
    return jax.shard_map(
        functools.partial(per_device, mesh.shape["site"]),
        mesh=mesh,
        in_specs=placed,
        out_specs=(P(("grp", "spin"), "site", None, None), P(("grp", "spin"), None, None)),
        check_vma=False,
    )
```

profile of v0, /device:TPU:1, one launch (start us, length us, event | category | flops | bytes accessed | tf_op | source)
XLA Modules:
  0.0 378.6 jit_solution(13452958703051515110)
XLA Ops:
  0.6 3.4 shard_map.59
  4.1 2.0 collective-permute-start
  6.7 16.7 %shard_map.60 = (bf16[32,112,256]{2,1,0:T(8,128)(2,1)}, bf16[32,112,256]{2,1,0:T(8,128)(2,1)}, bf16[32,112,256]{2,1,0:T(8,128)(2,1)}, bf16[32,112,256]{2,1,0:T(8...) custom-call(bf16[128,256,256]{2,1,0:T(8,128)(2,1)} %bitcast.72, bf16[256,256]{1,0:T(8,128)(2,1)} %kinetic.2), custom_call_target="tpu_custom_call" | custom-call | flops 1000 | bytes 1000 | tf_op jit(solution)/shard_map/pallas_call | solution.py:86
  23.4 7.8 %collective-permute-done.1.refs_4_ = bf16[68,16,256]{2,1,0:T(8,128)(2,1)S(1)} collective-permute-done((bf16[68,16,256]{2,1,0:T(8,128)(2,1)}, bf16[68,16,256]{2,1,0:T(8,128)(2,1)S(1)}, u32[]{:S(2)}, u32[]{:S(2)}) %collective-permute-start.1) | collective-permute-done | bytes 557088 | tf_op jit(solution)/shard_map/ppermute | solution.py:27
  31.2 1.4 collective-permute-start.6
  36.5 1.5 collective-permute-start.3
  38.6 1.5 collective-permute-start.4
  42.1 30.5 %collective-permute-done.6.refs_3_ = bf16[32,112,256]{2,1,0:T(8,128)(2,1)} collective-permute-done((bf16[32,112,256]{2,1,0:T(8,128)(2,1)}, bf16[32,112,256]{2,1,0:T(8,128)(2,1)}, u32[]{:S(2)}, u32[]{:S(2)}) %collective-permute-start.6) | collective-permute-done | bytes 1835040 | tf_op jit(solution)/shard_map/ppermute | solution.py:27
  72.7 40.8 %collective-permute-done.7.refs_5_ = bf16[32,112,256]{2,1,0:T(8,128)(2,1)} collective-permute-done((bf16[32,112,256]{2,1,0:T(8,128)(2,1)}, bf16[32,112,256]{2,1,0:T(8,128)(2,1)}, u32[]{:S(2)}, u32[]{:S(2)}) %collective-permute-start.7) | collective-permute-done | bytes 1835040 | tf_op jit(solution)/shard_map/ppermute | solution.py:27
  113.5 2.2 copy-done
  115.7 6.7 %shard_map.61 = (bf16[16,128,256]{2,1,0:T(8,128)(2,1)S(1)}, bf16[16,128,256]{2,1,0:T(8,128)(2,1)S(1)}, bf16[16,128,256]{2,1,0:T(8,128)(2,1)}, bf16[16,128,256]{2,1,0:T(8,128)(2,1)}, f32[256,256]{1,0:T(8,128)S(1)}) custom-call(bf16[64,128,256]{2,1,0:T(8,128)(2,1)S(1)} %copy-done, bf16[64,128,256]{2,1,0:T(8,128)(2,1)} %collective-permute-done.2.refs_1_, ...), custom_call_target="tpu_custom_call" | custom-call | flops 1000 | bytes 1000 | tf_op jit(solution)/shard_map/pallas_call | solution.py:142
  124.4 1.5 collective-permute-start.8
  126.0 2.2 copy-done.1
  128.2 6.0 %shard_map.62 = (bf16[16,128,256]{2,1,0:T(8,128)(2,1)S(1)}, bf16[16,128,256]{2,1,0:T(8,128)(2,1)S(1)}, bf16[16,128,256]{2,1,0:T(8,128)(2,1)S(1)}, bf16[16,128,256]{2,1,0:T(8,128)(2,1)S(1)}, f32[256,256]{1,0:T(8,128)S(1)}) custom-call(bf16[64,128,256]{2,1,0:T(8,128)(2,1)S(1)} %copy-done.1, bf16[64,128,256]{2,1,0:T(8,128)(2,1)} %collective-permute-done.2.refs_1_, ...), custom_call_target="tpu_custom_call" | custom-call | flops 1000 | bytes 1000 | tf_op jit(solution)/shard_map/pallas_call | solution.py:142
  136.2 1.1 copy-done.18
  138.2 13.1 %collective-permute-done.3.refs_3_ = bf16[32,112,256]{2,1,0:T(8,128)(2,1)} collective-permute-done((bf16[32,112,256]{2,1,0:T(8,128)(2,1)}, bf16[32,112,256]{2,1,0:T(8,128)(2,1)}, u32[]{:S(2)}, u32[]{:S(2)}) %collective-permute-start.3) | collective-permute-done | bytes 1835040 | tf_op jit(solution)/shard_map/ppermute | solution.py:27
  151.3 40.8 %collective-permute-done.4.refs_5_ = bf16[32,112,256]{2,1,0:T(8,128)(2,1)} collective-permute-done((bf16[32,112,256]{2,1,0:T(8,128)(2,1)}, bf16[32,112,256]{2,1,0:T(8,128)(2,1)}, u32[]{:S(2)}, u32[]{:S(2)}) %collective-permute-start.4) | collective-permute-done | bytes 1835040 | tf_op jit(solution)/shard_map/ppermute | solution.py:27
  192.1 6.0 %shard_map.63 = (bf16[16,128,256]{2,1,0:T(8,128)(2,1)S(1)}, bf16[16,128,256]{2,1,0:T(8,128)(2,1)S(1)}, bf16[16,128,256]{2,1,0:T(8,128)(2,1)S(1)}, bf16[16,128,256]{2,1,0:T(8,128)(2,1)S(1)}, f32[256,256]{1,0:T(8,128)S(1)}) custom-call(bf16[64,128,256]{2,1,0:T(8,128)(2,1)S(1)} %copy-done.1, bf16[64,128,256]{2,1,0:T(8,128)(2,1)} %collective-permute-done.2.refs_1_, ...), custom_call_target="tpu_custom_call" | custom-call | flops 1000 | bytes 1000 | tf_op jit(solution)/shard_map/pallas_call | solution.py:142
  200.1 1.1 copy-done.14
  202.1 6.0 %shard_map.64 = (bf16[16,128,256]{2,1,0:T(8,128)(2,1)S(1)}, bf16[16,128,256]{2,1,0:T(8,128)(2,1)S(1)}, bf16[16,128,256]{2,1,0:T(8,128)(2,1)S(1)}, bf16[16,128,256]{2,1,0:T(8,128)(2,1)S(1)}, f32[256,256]{1,0:T(8,128)S(1)}) custom-call(bf16[64,128,256]{2,1,0:T(8,128)(2,1)S(1)} %copy-done.1, bf16[64,128,256]{2,1,0:T(8,128)(2,1)} %collective-permute-done.2.refs_1_, ...), custom_call_target="tpu_custom_call" | custom-call | flops 1000 | bytes 1000 | tf_op jit(solution)/shard_map/pallas_call | solution.py:142
  213.1 2.3 collective-permute-start.9
  215.4 1.5 collective-permute-start.11
  218.6 18.5 %collective-permute-done.16.piece = bf16[16,128,256]{2,1,0:T(8,128)(2,1)} collective-permute-done((bf16[16,128,256]{2,1,0:T(8,128)(2,1)}, bf16[16,128,256]{2,1,0:T(8,128)(2,1)}, u32[]{:S(2)}, u32[]{:S(2)}) %collective-permute-start.16) | collective-permute-done | bytes 1048608 | tf_op jit(solution)/shard_map/ppermute | solution.py:27
  237.2 23.6 %collective-permute-done.10 = f32[128,256]{1,0:T(8,128)S(1)} collective-permute-done((f32[128,256]{1,0:T(8,128)S(1)}, f32[128,256]{1,0:T(8,128)S(1)}, u32[]{:S(2)}, u32[]{:S(2)}) %collective-permute-start.10) | collective-permute-done | bytes 131104 | tf_op jit(solution)/shard_map/ppermute | solution.py:27
  260.7 2.2 collective-permute-start.19
  263.0 2.2 collective-permute-done.12
  265.3 1.5 collective-permute-start.18
  266.8 38.3 %shard_map.65 = (f32[256,256]{1,0:T(8,128)}, bf16[256,256]{1,0:T(8,128)(2,1)S(1)}) custom-call(f32[256,256]{1,0:T(8,128)S(1)} %maximum_select_fusion.gram), custom_call_target="tpu_custom_call" | custom-call | flops 1000 | bytes 1000 | tf_op jit(solution)/shard_map/pallas_call | solution.py:233
  305.8 1.4 collective-permute-start.14
  307.7 1.2 copy-done.9
  308.9 1.9 shard_map.66.rest_0_
  310.8 2.8 shard_map.67.rest_0_
  313.6 2.8 shard_map.68.rest_0_
  316.5 2.9 shard_map.69.rest_0_
  319.4 1.9 shard_map.70.rest_0_
  321.3 1.9 shard_map.71.rest_0_
  323.1 1.9 shard_map.72.rest_0_
  325.0 2.9 shard_map.73.rest_0_
  328.0 1.9 shard_map.74.rest_0_
  329.8 1.9 shard_map.75.rest_0_
  331.7 2.8 shard_map.76.rest_0_
  334.6 2.9 shard_map.77.rest_0_
  337.5 1.9 shard_map.78.rest_0_
  339.4 2.8 shard_map.79.rest_0_
  342.2 11.1 %collective-permute-done.14.piece = bf16[16,128,256]{2,1,0:T(8,128)(2,1)} collective-permute-done((bf16[16,128,256]{2,1,0:T(8,128)(2,1)}, bf16[16,128,256]{2,1,0:T(8,128)(2,1)}, u32[]{:S(2)}, u32[]{:S(2)}) %collective-permute-start.14) | collective-permute-done | bytes 1048608 | tf_op jit(solution)/shard_map/ppermute | solution.py:27
  353.3 2.8 shard_map.80.rest_0_
  356.2 19.6 %collective-permute-done.13.piece = bf16[16,128,256]{2,1,0:T(8,128)(2,1)} collective-permute-done((bf16[16,128,256]{2,1,0:T(8,128)(2,1)}, bf16[16,128,256]{2,1,0:T(8,128)(2,1)}, u32[]{:S(2)}, u32[]{:S(2)}) %collective-permute-start.13) | collective-permute-done | bytes 1048608 | tf_op jit(solution)/shard_map/ppermute | solution.py:27
  375.8 2.8 shard_map.81
  (96 shorter events, 23.2 us)
Async XLA Ops:
  0.6 32.7 %copy-start.21 = (bf16[1,1,128,256]{3,2,1,0:T(8,128)(2,1)S(1)}, bf16[1,1,128,256]{3,2,1,0:T(8,128)(2,1)}, u32[]{:S(2)}) copy-start(bf16[1,1,128,256]{3,2,1,0:T(8,128)(2,1)} %param.5) | copy-start | bytes 196612
  0.6 32.8 %copy-start.20 = (bf16[512,512]{1,0:T(8,128)(2,1)S(1)}, bf16[512,512]{1,0:T(8,128)(2,1)}, u32[]{:S(2)}) copy-start(bf16[512,512]{1,0:T(8,128)(2,1)} %param.6) | copy-start | bytes 1572868
  4.1 19.3 %collective-permute-start = (bf16[68,16,256]{2,1,0:T(8,128)(2,1)}, bf16[68,16,256]{2,1,0:T(8,128)(2,1)S(1)}, u32[]{:S(2)}, u32[]{:S(2)}) collective-permute-start(bf16[68,16,256]{2,1,0:T(8,128)(2,1)} %get-tuple-element.69), channel_id=1, source_target_pairs={{0,8},{4,12},{8,0},{12,4},{1,9},{5,13},{9,1},{13,5},{2,10},{6,14},... | collective-permute-start | bytes 1671176 | tf_op jit(solution)/shard_map/ppermute | solution.py:27
  6.1 25.0 %collective-permute-start.1 = (bf16[68,16,256]{2,1,0:T(8,128)(2,1)}, bf16[68,16,256]{2,1,0:T(8,128)(2,1)S(1)}, u32[]{:S(2)}, u32[]{:S(2)}) collective-permute-start(bf16[68,16,256]{2,1,0:T(8,128)(2,1)} %get-tuple-element.70), channel_id=1, source_target_pairs={{0,12},{4,8},{8,4},{12,0},{1,13},{5,9},{9,5},{13,1},{2,14},{6,10},... | collective-permute-start | bytes 1671176 | tf_op jit(solution)/shard_map/ppermute | solution.py:27
  31.1 7.5 %collective-permute-start.2 = (bf16[64,128,256]{2,1,0:T(8,128)(2,1)}, bf16[64,128,256]{2,1,0:T(8,128)(2,1)}, u32[]{:S(2)}, u32[]{:S(2)}) collective-permute-start(bf16[64,128,256]{2,1,0:T(8,128)(2,1)} %get-tuple-element.73), channel_id=1, source_target_pairs={{0,4},{4,0},{8,12},{12,8},{1,5},{5,1},{9,13},{13,9},{2,6},{6,2},{1... | collective-permute-start | bytes 12582920 | tf_op jit(solution)/shard_map/ppermute | solution.py:27
  31.2 41.4 %collective-permute-start.6 = (bf16[32,112,256]{2,1,0:T(8,128)(2,1)}, bf16[32,112,256]{2,1,0:T(8,128)(2,1)}, u32[]{:S(2)}, u32[]{:S(2)}) collective-permute-start(bf16[32,112,256]{2,1,0:T(8,128)(2,1)} %get-tuple-element.81), channel_id=1, source_target_pairs={{0,8},{4,12},{8,0},{12,4},{1,9},{5,13},{9,1},{13,5},{2,10},{6,14},... | collective-permute-start | bytes 5505032 | tf_op jit(solution)/shard_map/ppermute | solution.py:27
  32.6 80.9 %collective-permute-start.7 = (bf16[32,112,256]{2,1,0:T(8,128)(2,1)}, bf16[32,112,256]{2,1,0:T(8,128)(2,1)}, u32[]{:S(2)}, u32[]{:S(2)}) collective-permute-start(bf16[32,112,256]{2,1,0:T(8,128)(2,1)} %get-tuple-element.82), channel_id=1, source_target_pairs={{0,12},{4,8},{8,4},{12,0},{1,13},{5,9},{9,5},{13,1},{2,14},{6,10},... | collective-permute-start | bytes 5505032 | tf_op jit(solution)/shard_map/ppermute | solution.py:27
  36.5 114.8 %collective-permute-start.3 = (bf16[32,112,256]{2,1,0:T(8,128)(2,1)}, bf16[32,112,256]{2,1,0:T(8,128)(2,1)}, u32[]{:S(2)}, u32[]{:S(2)}) collective-permute-start(bf16[32,112,256]{2,1,0:T(8,128)(2,1)} %get-tuple-element.77), channel_id=1, source_target_pairs={{0,8},{4,12},{8,0},{12,4},{1,9},{5,13},{9,1},{13,5},{2,10},{6,14},... | collective-permute-start | bytes 5505032 | tf_op jit(solution)/shard_map/ppermute | solution.py:27
  38.6 153.5 %collective-permute-start.4 = (bf16[32,112,256]{2,1,0:T(8,128)(2,1)}, bf16[32,112,256]{2,1,0:T(8,128)(2,1)}, u32[]{:S(2)}, u32[]{:S(2)}) collective-permute-start(bf16[32,112,256]{2,1,0:T(8,128)(2,1)} %get-tuple-element.79), channel_id=1, source_target_pairs={{0,12},{4,8},{8,4},{12,0},{1,13},{5,9},{9,5},{13,1},{2,14},{6,10},... | collective-permute-start | bytes 5505032 | tf_op jit(solution)/shard_map/ppermute | solution.py:27
  40.3 1.3 collective-permute-start.5
  113.5 2.2 copy-start
  122.4 1.0 copy-start.8
  123.4 1.0 copy-start.15
  124.4 88.7 %collective-permute-start.8 = (bf16[16,128,256]{2,1,0:T(8,128)(2,1)}, bf16[16,128,256]{2,1,0:T(8,128)(2,1)}, u32[]{:S(2)}, u32[]{:S(2)}) collective-permute-start(bf16[16,128,256]{2,1,0:T(8,128)(2,1)} %get-tuple-element.89), channel_id=1, source_target_pairs={{0,8},{4,12},{8,0},{12,4},{1,9},{5,13},{9,1},{13,5},{2,10},{6,14},... | collective-permute-start | bytes 3145736 | tf_op jit(solution)/shard_map/ppermute | solution.py:27
  125.9 111.2 %collective-permute-start.16 = (bf16[16,128,256]{2,1,0:T(8,128)(2,1)}, bf16[16,128,256]{2,1,0:T(8,128)(2,1)}, u32[]{:S(2)}, u32[]{:S(2)}) collective-permute-start(bf16[16,128,256]{2,1,0:T(8,128)(2,1)} %get-tuple-element.104), channel_id=1, source_target_pairs={{0,12},{4,8},{8,4},{12,0},{1,13},{5,9},{9,5},{13,1},{2,14},{6,10},... | collective-permute-start | bytes 3145736 | tf_op jit(solution)/shard_map/ppermute | solution.py:27
  126.0 2.2 copy-start.1
  134.2 1.0 copy-start.6
  135.2 1.0 copy-start.16
  136.2 1.1 copy-start.18
  137.2 1.0 copy-start.19
  198.1 1.0 copy-start.4
  199.1 1.0 copy-start.13
  200.1 1.1 copy-start.14
  201.1 1.0 copy-start.17
  208.1 1.0 copy-start.2
  209.1 1.0 copy-start.10
  210.1 1.0 copy-start.11
  211.1 1.0 copy-start.12
  213.1 3.7 collective-permute-start.9
  215.4 47.6 %collective-permute-start.11 = (bf16[16,128,256]{2,1,0:T(8,128)(2,1)}, bf16[16,128,256]{2,1,0:T(8,128)(2,1)S(1)}, u32[]{:S(2)}, u32[]{:S(2)}) collective-permute-start(bf16[16,128,256]{2,1,0:T(8,128)(2,1)} %copy-done.19), channel_id=1, source_target_pairs={{0,8},{4,12},{8,0},{12,4},{1,9},{5,13},{9,1},{13,5},{2,10},{6,14},... | collective-permute-start | bytes 3145736 | tf_op jit(solution)/shard_map/ppermute | solution.py:27
  216.9 43.9 %collective-permute-start.10 = (f32[128,256]{1,0:T(8,128)S(1)}, f32[128,256]{1,0:T(8,128)S(1)}, u32[]{:S(2)}, u32[]{:S(2)}) collective-permute-start(f32[128,256]{1,0:T(8,128)S(1)} %dynamic-slice_add_fusion), channel_id=1, source_target_pairs={{0,8},{4,12},{8,0},{12,4},{1,9},{5,13},{9,1},{13,5},{2,10},{6,14},... | collective-permute-start | bytes 393224 | tf_op jit(solution)/shard_map/ppermute | solution.py:27
  217.9 87.3 %collective-permute-start.21 = (bf16[16,128,256]{2,1,0:T(8,128)(2,1)}, bf16[16,128,256]{2,1,0:T(8,128)(2,1)S(1)}, u32[]{:S(2)}, u32[]{:S(2)}) collective-permute-start(bf16[16,128,256]{2,1,0:T(8,128)(2,1)} %copy-done.18), channel_id=1, source_target_pairs={{0,4},{4,0},{8,12},{12,8},{1,5},{5,1},{9,13},{13,9},{2,6},{6,2},{1... | collective-permute-start | bytes 3145736 | tf_op jit(solution)/shard_map/ppermute | solution.py:27
  218.6 87.0 %collective-permute-start.22 = (bf16[16,128,256]{2,1,0:T(8,128)(2,1)}, bf16[16,128,256]{2,1,0:T(8,128)(2,1)}, u32[]{:S(2)}, u32[]{:S(2)}) collective-permute-start(bf16[16,128,256]{2,1,0:T(8,128)(2,1)} %copy-done.15), channel_id=1, source_target_pairs={{0,4},{4,0},{8,12},{12,8},{1,5},{5,1},{9,13},{13,9},{2,6},{6,2},{1... | collective-permute-start | bytes 3145736 | tf_op jit(solution)/shard_map/ppermute | solution.py:27
  237.1 68.7 %collective-permute-start.20 = (bf16[16,128,256]{2,1,0:T(8,128)(2,1)}, bf16[16,128,256]{2,1,0:T(8,128)(2,1)}, u32[]{:S(2)}, u32[]{:S(2)}) collective-permute-start(bf16[16,128,256]{2,1,0:T(8,128)(2,1)} %copy-done.16), channel_id=1, source_target_pairs={{0,12},{4,8},{8,4},{12,0},{1,13},{5,9},{9,5},{13,1},{2,14},{6,10},... | collective-permute-start | bytes 3145736 | tf_op jit(solution)/shard_map/ppermute | solution.py:27
  260.7 46.4 %collective-permute-start.19 = (bf16[16,128,256]{2,1,0:T(8,128)(2,1)}, bf16[16,128,256]{2,1,0:T(8,128)(2,1)S(1)}, u32[]{:S(2)}, u32[]{:S(2)}) collective-permute-start(bf16[16,128,256]{2,1,0:T(8,128)(2,1)} %copy-done.17), channel_id=1, source_target_pairs={{0,4},{4,0},{8,12},{12,8},{1,5},{5,1},{9,13},{13,9},{2,6},{6,2},{1... | collective-permute-start | bytes 3145736 | tf_op jit(solution)/shard_map/ppermute | solution.py:27
  263.0 2.3 collective-permute-start.12
  265.3 66.4 %collective-permute-start.18 = (bf16[16,128,256]{2,1,0:T(8,128)(2,1)}, bf16[16,128,256]{2,1,0:T(8,128)(2,1)}, u32[]{:S(2)}, u32[]{:S(2)}) collective-permute-start(bf16[16,128,256]{2,1,0:T(8,128)(2,1)} %copy-done.14), channel_id=1, source_target_pairs={{0,8},{4,12},{8,0},{12,4},{1,9},{5,13},{9,1},{13,5},{2,10},{6,14},... | collective-permute-start | bytes 3145736 | tf_op jit(solution)/shard_map/ppermute | solution.py:27
  305.2 29.4 %collective-permute-start.17 = (bf16[16,128,256]{2,1,0:T(8,128)(2,1)}, bf16[16,128,256]{2,1,0:T(8,128)(2,1)}, u32[]{:S(2)}, u32[]{:S(2)}) collective-permute-start(bf16[16,128,256]{2,1,0:T(8,128)(2,1)} %copy-done.13), channel_id=1, source_target_pairs={{0,12},{4,8},{8,4},{12,0},{1,13},{5,9},{9,5},{13,1},{2,14},{6,10},... | collective-permute-start | bytes 3145736 | tf_op jit(solution)/shard_map/ppermute | solution.py:27
  305.6 33.8 %collective-permute-start.15 = (bf16[16,128,256]{2,1,0:T(8,128)(2,1)}, bf16[16,128,256]{2,1,0:T(8,128)(2,1)}, u32[]{:S(2)}, u32[]{:S(2)}) collective-permute-start(bf16[16,128,256]{2,1,0:T(8,128)(2,1)} %copy-done.12), channel_id=1, source_target_pairs={{0,4},{4,0},{8,12},{12,8},{1,5},{5,1},{9,13},{13,9},{2,6},{6,2},{1... | collective-permute-start | bytes 3145736 | tf_op jit(solution)/shard_map/ppermute | solution.py:27
  305.8 47.6 %collective-permute-start.14 = (bf16[16,128,256]{2,1,0:T(8,128)(2,1)}, bf16[16,128,256]{2,1,0:T(8,128)(2,1)}, u32[]{:S(2)}, u32[]{:S(2)}) collective-permute-start(bf16[16,128,256]{2,1,0:T(8,128)(2,1)} %copy-done.11), channel_id=1, source_target_pairs={{0,8},{4,12},{8,0},{12,4},{1,9},{5,13},{9,1},{13,5},{2,10},{6,14},... | collective-permute-start | bytes 3145736 | tf_op jit(solution)/shard_map/ppermute | solution.py:27
  307.1 68.7 %collective-permute-start.13 = (bf16[16,128,256]{2,1,0:T(8,128)(2,1)}, bf16[16,128,256]{2,1,0:T(8,128)(2,1)}, u32[]{:S(2)}, u32[]{:S(2)}) collective-permute-start(bf16[16,128,256]{2,1,0:T(8,128)(2,1)} %copy-done.10), channel_id=1, source_target_pairs={{0,12},{4,8},{8,4},{12,0},{1,13},{5,9},{9,5},{13,1},{2,14},{6,10},... | collective-permute-start | bytes 3145736 | tf_op jit(solution)/shard_map/ppermute | solution.py:27
  307.7 1.2 copy-start.9
  316.5 2.9 copy-start.7
  325.0 2.9 copy-start.5
  334.6 2.9 copy-start.3
where the time goes:
time: 380 us; the launch traced here: 379 us
  waiting for transfers between devices  210 us (55%)
  Pallas kernels  122 us (32%)
  local copies, waits for them, and re-layouts  23.2 us (6%)
  starting transfers between devices  21.7 us (6%)
    ppermute x23, waiting for transfers between devices, trade(): lax.ppermute(piece, 'site', [(i, partner(i, step, count)) for i in range(...  210 us
    pallas_call x16, Pallas kernels, finish(): pl.pallas_call(last_kernel, grid_spec=pltpu.PrefetchScalarGridSpec(num_sc...  38.9 us
    pallas_call x1, Pallas kernels, factor(): pl.pallas_call(functools.partial(factor_kernel, scale), out_shape=[jax.Sh...  38.3 us
    pallas_call x4, Pallas kernels, apply_x(): pl.pallas_call(functools.partial(x_kernel, count, group), grid=(part // g...  24.7 us
    ppermute x23, starting transfers between devices, trade(): lax.ppermute(piece, 'site', [(i, partner(i, step, count)) for i in range(...  21.7 us
    pallas_call x2, Pallas kernels, apply_y(): pl.pallas_call(functools.partial(y_kernel, count, width // count, cuts, w...  20.1 us
    unnamed x46, local copies, waits for them, and re-layouts  19.7 us
  transfers between devices with their start and end apart: 23, of which 13 were waited for; matrix products, arithmetic and copies ran while one was open for 1% of the time, Pallas kernels for 31%

commit v1 on v0

--- a/solution.py
+++ b/solution.py
@@ -11,7 +11,8 @@
 LANES = 128
 PAD = 8
 BLOCK = 64
-VMEM_LIMIT = 32 * 1024 * 1024
+VMEM_LIMIT = 20 * 1024 * 1024
+VMEM_LEAST = 8 * 1024 * 1024
 VMEM_MOST = 56 * 1024 * 1024
 
 
@@ -51,10 +52,22 @@
             own[pl.ds(row, size), :] = kinetic[pl.ds(start, size), :]
             row += size
 
-    for r in range(ROWS):
+    fine = walkers.shape[0]
+    turn = pl.program_id(0) % (ROWS // fine)
+    for r in range(fine):
         line = jnp.dot(own[...], walkers[r], preferred_element_type=jnp.float32)
+        at = turn * fine + r if fine < ROWS else r
         for h in range(turned.shape[0]):
-            turned[h, pl.ds(r, depth, stride=ROWS + PAD), :] = line[:, h * LANES : (h + 1) * LANES]
+            part = line[:, h * LANES : (h + 1) * LANES]
+            turned[h, pl.ds(at, depth, stride=ROWS + PAD), :] = part
+    if fine < ROWS:
+        pl.when(turn == ROWS // fine - 1)(functools.partial(write_cuts, count, band, cuts, window, outs, turned, rest))
+    else:
+        write_cuts(count, band, cuts, window, outs, turned, rest)
+
+
+def write_cuts(count, band, cuts, window, outs, turned, rest):
+    me = lax.axis_index("site")
     row = 0
     for (s, first, size), out in zip(cuts, outs):
         for h in range(turned.shape[0]):
@@ -63,31 +76,39 @@
             out[:size, :, h * LANES : (h + 1) * LANES] = piece.astype(out.dtype)
         row += size
         if window:
-            begin = pl.multiple_of(partner(me, s, count) * band // window * window, LANES)
-            across = out.shape[2] // window
+            begin = partner(me, s, count) * band
+            tile = pl.multiple_of(begin // window * window, LANES)
+            across = out.shape[2] // band
             for line in range(0, rest[0].shape[0], ROWS):
                 place, part = size + line // ROWS // across, line // ROWS % across
-                values = rest[0][pl.ds(line, ROWS), pl.ds(begin, window)]
-                out[place, :, part * window : (part + 1) * window] = values
-
-
-def apply_y(walkers, kinetic_y, count, cuts, sizes, fields=None, window=0):
+                values = rest[0][pl.ds(line, ROWS), pl.ds(tile, window)].astype(jnp.float32)
+                own_values = values[:, :band]
+                for k in range(band, window, band):
+                    own_values = jnp.where(begin - tile == k, values[:, k : k + band], own_values)
+                out[place, :, part * band : (part + 1) * band] = own_values.astype(out.dtype)
+
+
+def rows_for_fields(lines, band, orbitals):
+    return -(-lines * band // (ROWS * orbitals))
+
+
+def apply_y(walkers, kinetic_y, count, cuts, sizes, fine, fields=None, window=0):
     lines, width, orbitals = walkers.shape
     depth = sum(size for _, _, size in cuts)
     used = max(sizes)
-    extra = fields.size // fields.shape[1] * window // (ROWS * orbitals) if window else 0
+    extra = rows_for_fields(lines, width // count, orbitals) if window else 0
 
     def out_spec(cut, size):
         late = (used - size) // ROWS
         return pl.BlockSpec(
-            (cut[2] + extra, ROWS, orbitals), lambda i: (0, jnp.maximum(i - late, 0) if late else i, 0)
+            (cut[2] + extra, ROWS, orbitals), lambda i: (0, jnp.maximum(i * fine // ROWS - late, 0), 0)
         )
 
     return pl.pallas_call(
         functools.partial(y_kernel, count, width // count, cuts, window),
-        grid=(used // ROWS,),
+        grid=(used // fine,),
         in_specs=[
-            pl.BlockSpec((ROWS, width, orbitals), lambda i: (i, 0, 0)),
+            pl.BlockSpec((fine, width, orbitals), lambda i: (i, 0, 0)),
             pl.BlockSpec((width, width), lambda i: (0, 0)),
         ]
         + [pl.BlockSpec((lines, width), lambda i: (0, 0))] * (window > 0),
@@ -156,11 +177,10 @@
     return results[:count], results[count]
 
 
-def last_kernel(where, piece, inverse, *rest):
-    out, turned = rest[-2], rest[-1]
-    part, rows, orbitals = piece.shape
+def times_inverse(piece, inverse, turned, out):
+    part, rows, _ = piece.shape
     product = jnp.dot(
-        piece[...].reshape(part * rows, orbitals),
+        piece[...].reshape(part * rows, piece.shape[2]),
         inverse[...],
         preferred_element_type=jnp.float32,
     )
@@ -171,6 +191,60 @@
         for r in range(rows):
             line = turned[h, pl.ds(r, part, stride=rows + PAD), :]
             out[r, :, h * LANES : (h + 1) * LANES] = line.astype(out.dtype)
+
+
+def last_kernel(where, piece, inverse, *rest):
+    times_inverse(piece, inverse, rest[-1], rest[-2])
+
+
+def split_kernel(piece, inverse, *rest):
+    for k, out in enumerate(rest[:-1]):
+        pl.when(pl.program_id(0) == k)(
+            functools.partial(times_inverse, piece, inverse, rest[-1], out)
+        )
+
+
+def place_kernel(where, piece, result, out):
+    out[...] = piece[...]
+
+
+def split(piece, inverse):
+    part, lines, orbitals = piece.shape
+    rows = 4 * ROWS if lines % (4 * ROWS) == 0 else lines
+    out = (rows, part, orbitals)
+    return pl.pallas_call(
+        split_kernel,
+        grid=(lines // rows,),
+        in_specs=[
+            pl.BlockSpec((part, rows, orbitals), lambda i: (0, i, 0)),
+            pl.BlockSpec((orbitals, orbitals), lambda i: (0, 0)),
+        ],
+        out_specs=[pl.BlockSpec(out, lambda i: (0, 0, 0))] * (lines // rows),
+        out_shape=[jax.ShapeDtypeStruct(out, jnp.bfloat16)] * (lines // rows),
+        scratch_shapes=[pltpu.VMEM((orbitals // LANES, part * (rows + PAD), LANES), jnp.float32)],
+        **settings(VMEM_LEAST),
+    )(piece, inverse)
+
+
+def place(result, piece, begin, where):
+    lines, part, orbitals = piece.shape
+    rows = lines // 2 if begin % (lines // 2) == 0 else lines
+    block = (rows, part, orbitals)
+    return pl.pallas_call(
+        place_kernel,
+        grid_spec=pltpu.PrefetchScalarGridSpec(
+            num_scalar_prefetch=1,
+            grid=(lines // rows,),
+            in_specs=[
+                pl.BlockSpec(block, lambda i, where: (i, 0, 0)),
+                pl.BlockSpec(memory_space=pl.ANY),
+            ],
+            out_specs=pl.BlockSpec(block, lambda i, where: (begin // rows + i, where[0], 0)),
+        ),
+        out_shape=jax.ShapeDtypeStruct(result.shape, result.dtype),
+        input_output_aliases={2: 0},
+        **settings(VMEM_LEAST),
+    )(where.reshape(1), piece, result)
 
 
 def finish(result, piece, inverse, place, width):
@@ -192,15 +266,20 @@
         ),
         out_shape=jax.ShapeDtypeStruct((lines, width, orbitals), jnp.bfloat16),
         input_output_aliases={3: 0} if begun else {},
-        **settings(),
+        **settings(VMEM_LEAST),
     )(place.reshape(1), piece, inverse, *([result] if begun else []))
 
 
-def factor_kernel(scale, gram, lower, inverse, work, upper):
-    size = gram.shape[0]
+def factor_kernel(scale, first, second, lower, inverse, work, upper):
+    size = lower.shape[0]
+    quarter = size // 4
+    upper[3 * quarter :, :] = first[:, :size]
+    upper[:quarter, :quarter] = first[:, size:]
+    upper[2 * quarter : 3 * quarter, : 3 * quarter] = second[:, : 3 * quarter]
+    upper[quarter : 2 * quarter, : 2 * quarter] = second[:, 3 * quarter :]
     row = lax.broadcasted_iota(jnp.int32, (size, size), 0)
     column = lax.broadcasted_iota(jnp.int32, (size, size), 1)
-    work[:, :size] = gram[...] * scale
+    work[:, :size] = jnp.where(row >= column, upper[...], upper[...].T) * scale
     work[:, size:] = jnp.where(row == column, 1.0, 0.0)
     line = lax.broadcasted_iota(jnp.int32, (BLOCK, 2 * BLOCK), 0)
     lane = lax.broadcasted_iota(jnp.int32, (BLOCK, 2 * BLOCK), 1)
@@ -228,8 +307,15 @@
     inverse[...] = work[:, size:].T.astype(inverse.dtype)
 
 
-def factor(gram, scale):
-    size = gram.shape[0]
+def pack(gram):
+    quarter = gram.shape[0] // 4
+    first = [gram[3 * quarter :], gram[:quarter, :quarter]]
+    second = [gram[2 * quarter : 3 * quarter, : 3 * quarter], gram[quarter : 2 * quarter, : 2 * quarter]]
+    return jnp.concatenate(first, axis=1), jnp.concatenate(second, axis=1)
+
+
+def factor(first, second, scale):
+    size = first.shape[0] * 4
     return pl.pallas_call(
         functools.partial(factor_kernel, scale),
         out_shape=[
@@ -240,8 +326,8 @@
             pltpu.VMEM((size, 2 * size), jnp.float32),
             pltpu.VMEM((size, size), jnp.float32),
         ],
-        **settings(),
-    )(gram)
+        **settings(VMEM_LEAST),
+    )(first, second)
 
 
 def one_determinant(walkers, fields, kinetic_x, kinetic_y, count):
@@ -249,26 +335,27 @@
     me = lax.axis_index("site")
     band = width // count
     part = ROWS if band % ROWS == 0 else band
+    chunks = band // part
     group = 8 if part % 8 == 0 else part
     wide = 2 * part if band % (2 * part) == 0 else band
     steps = range(count)
     order = jnp.stack([partner(me, s, count) for s in steps])
 
     window = max(LANES, band)
-    extra = lines * window // (ROWS * orbitals)
+    extra = rows_for_fields(lines, band, orbitals)
     far = [s for s in steps if s > 1 and lines > ROWS]
     near = [s for s in steps if s not in far]
     head = {}
     if far:
         arrays = apply_y(
-            walkers, kinetic_y, count, [(s, 0, band) for s in far], [ROWS] * len(far), fields, window
+            walkers, kinetic_y, count, [(s, 0, band) for s in far], [ROWS] * len(far), ROWS, fields, window
         )
         kinetic_y, *arrays = tie(kinetic_y, *arrays)
         head = {s: trade(a, s, count) for s, a in zip(far, arrays)}
     cuts = [(s, first, wide) for first in range(0, band, wide) for s in far]
     cuts += [(s, 0, band) for s in near]
     sizes = [lines if s in near else lines - ROWS for s, _, _ in cuts]
-    arrays = apply_y(walkers, kinetic_y, count, cuts, sizes)
+    arrays = apply_y(walkers, kinetic_y, count, cuts, sizes, ROWS)
     tail = {(s, first): a for (s, first, _), a in zip(cuts, arrays)}
     late = [key for key in tail if key[0] in near or key[1] > 0]
     if far:
@@ -292,9 +379,8 @@
                 tail[s, first], tail[near[-1], 0] = tie(tail[s, first], tail[near[-1], 0])
             tail[s, first] = trade(tail[s, first], s, count)
     for s in far:
-        sent = head[s][band:].reshape(extra, ROWS, orbitals // window, window)
-        sent = jnp.swapaxes(sent, 1, 2).reshape(lines, window)
-        own_fields[s] = lax.dynamic_slice_in_dim(sent, me * band % window, band, 1)
+        sent = head[s][band:].reshape(extra, ROWS, orbitals // band, band)
+        own_fields[s] = jnp.swapaxes(sent, 1, 2).reshape(-1, band)[:lines]
     own_fields = jnp.stack([own_fields[s] for s in steps])
     own_fields = own_fields.reshape(count * lines, band // group, group).swapaxes(0, 1)
     turned_x = kinetic_x.reshape(count, lines, count, lines)
@@ -313,7 +399,6 @@
         ready.append(scaled)
 
     back = []
-    half = orbitals // 2
     for c in range(min(2, len(ready))):
         back.append(dict(enumerate(ready[c])))
         for s in far:
@@ -326,8 +411,9 @@
         core = me & 1
         if far:
             gram, back[0][far[0]] = tie(gram, back[0][far[0]])
-        mine = lax.dynamic_slice_in_dim(gram, core * half, half, 0)
-        mine = mine + trade(lax.dynamic_slice_in_dim(gram, (1 - core) * half, half, 0), 1, count)
+        first, second = pack(gram)
+        mine = jnp.where(core == 0, first, second)
+        mine = mine + trade(jnp.where(core == 0, second, first), 1, count)
         step = 2
         while step < count:
             mine = mine + trade(mine, step, count)
@@ -335,29 +421,39 @@
         if len(back) > 1 and far:
             mine, back[1][far[0]] = tie(mine, back[1][far[0]])
         other = trade(mine, 1, count)
-        gram = jnp.where(core == 0, jnp.concatenate([mine, other]), jnp.concatenate([other, mine]))
+        first, second = jnp.where(core == 0, mine, other), jnp.where(core == 0, other, mine)
     else:
-        gram = lax.psum(gram, "site")
-    lower, inverse = factor(gram, 1.0 / (count * lines * width))
+        first, second = pack(lax.psum(gram, "site"))
+    lower, inverse = factor(first, second, 1.0 / (count * lines * width))
 
     for c in range(2, len(ready)):
         back.append(dict(enumerate(ready[c])))
         for s in far:
             if c == 2:
                 back[c][s], back[0][s] = tie(back[c][s], back[0][s])
+            elif c < chunks - 1:
+                back[c][s], inverse = tie(back[c][s], inverse)
+            if 2 < c == chunks - 1:
+                back[c][s] = [trade(piece, s, count) for piece in split(back[c][s], inverse)]
             else:
-                back[c][s], inverse = tie(back[c][s], inverse)
-            back[c][s] = trade(back[c][s], s, count)
+                back[c][s] = trade(back[c][s], s, count)
     for c in range(len(back)):
         for s in near:
-            back[c][s], gram = tie(back[c][s], gram)
+            back[c][s], first = tie(back[c][s], first)
             back[c][s] = trade(back[c][s], s, count)
 
     result = None
-    for c in range(len(back)):
+    for c in range(chunks):
         for s in steps:
-            place = order[s] * (band // part) + c
-            result = finish(result, back[c][s], inverse, place, width)
+            if not isinstance(back[c][s], list):
+                where = order[s] * chunks + c
+                result = finish(result, back[c][s], inverse, where, width)
+    for s in far:
+        if isinstance(back[-1][s], list):
+            pieces = back[-1][s]
+            for k, piece in enumerate(pieces):
+                where = order[s] * chunks + chunks - 1
+                result = place(result, piece, k * piece.shape[0], where)
     return result, lower
 
 

time: 380 us -> 375 us (0.987)
  local copies, waits for them, and re-layouts: 23.2 us -> 13.3 us
  Pallas kernels: 122 us -> 128 us
  waiting for transfers between devices: 210 us -> 204 us
  starting transfers between devices: 21.7 us -> 27.4 us
    pallas_call x0 -> x6, Pallas kernels: none -> 11.2 us  [the longest x4 7.04 us: place(): pl.pallas_call(place_kernel, grid_spec=pltpu.PrefetchScalarGridSpec(num_s...]
    unnamed x46 -> x33, local copies, waits for them, and re-layouts: 19.7 us -> 9.79 us
    pallas_call x16 -> x14, Pallas kernels: 38.9 us -> 32 us  [finish(): pl.pallas_call(last_kernel, grid_spec=pltpu.PrefetchScalarGridSpec(num_sc...]
    ppermute x23 -> x25, waiting for transfers between devices: 210 us -> 204 us  [trade(): lax.ppermute(piece, 'site', [(i, partner(i, step, count)) for i in range(...]
    ppermute x23 -> x25, starting transfers between devices: 21.7 us -> 27.4 us  [trade(): lax.ppermute(piece, 'site', [(i, partner(i, step, count)) for i in range(...]
  transfers between devices with their start and end apart: 23 -> 25, of which waited for: 13 -> 14; matrix products, arithmetic and copies ran while one was open for 1% -> 1% of each run, Pallas kernels for 31% -> 33%
where the time goes in v1:
time: 375 us; the launch traced here: 374 us
  waiting for transfers between devices  204 us (54%)
  Pallas kernels  128 us (34%)
  starting transfers between devices  27.4 us (7%)
  local copies, waits for them, and re-layouts  13.3 us (4%)
    ppermute x25, waiting for transfers between devices, trade(): lax.ppermute(piece, 'site', [(i, partner(i, step, count)) for i in range(...  204 us
    pallas_call x1, Pallas kernels, factor(): pl.pallas_call(functools.partial(factor_kernel, scale), out_shape=[jax.Sh...  38.4 us
    pallas_call x14, Pallas kernels, finish(): pl.pallas_call(last_kernel, grid_spec=pltpu.PrefetchScalarGridSpec(num_sc...  32 us
    ppermute x25, starting transfers between devices, trade(): lax.ppermute(piece, 'site', [(i, partner(i, step, count)) for i in range(...  27.4 us
    pallas_call x4, Pallas kernels, apply_x(): pl.pallas_call(functools.partial(x_kernel, count, group), grid=(part // g...  26.1 us
    pallas_call x2, Pallas kernels, apply_y(): pl.pallas_call(functools.partial(y_kernel, count, width // count, cuts, w...  20.2 us
    unnamed x33, local copies, waits for them, and re-layouts  9.79 us
  transfers between devices with their start and end apart: 25, of which 14 were waited for; matrix products, arithmetic and copies ran while one was open for 1% of the time, Pallas kernels for 33%

profile of v1, /device:TPU:1, one launch (start us, length us, event | category | flops | bytes accessed | tf_op | source)
XLA Modules:
  0.0 374.1 jit_solution(4278559943655374466)
XLA Ops:
  0.6 3.4 shard_map.59
  4.0 2.0 collective-permute-start
  6.7 16.8 %shard_map.60 = (bf16[32,112,256]{2,1,0:T(8,128)(2,1)}, bf16[32,112,256]{2,1,0:T(8,128)(2,1)}, bf16[32,112,256]{2,1,0:T(8,128)(2,1)}, bf16[32,112,256]{2,1,0:T(8...) custom-call(bf16[128,256,256]{2,1,0:T(8,128)(2,1)} %bitcast.60, bf16[256,256]{1,0:T(8,128)(2,1)} %kinetic.2), custom_call_target="tpu_custom_call" | custom-call | flops 1000 | bytes 1000 | tf_op jit(solution)/shard_map/pallas_call | solution.py:107
  23.5 6.9 %collective-permute-done.1.refs_4_ = bf16[66,16,256]{2,1,0:T(8,128)(2,1)S(1)} collective-permute-done((bf16[66,16,256]{2,1,0:T(8,128)(2,1)}, bf16[66,16,256]{2,1,0:T(8,128)(2,1)S(1)}, u32[]{:S(2)}, u32[]{:S(2)}) %collective-permute-start.1) | collective-permute-done | bytes 540704 | tf_op jit(solution)/shard_map/ppermute | solution.py:28
  32.6 1.5 collective-permute-start.3
  35.9 2.0 collective-permute-done.2.refs_1_
  42.5 29.4 %collective-permute-done.6.refs_3_ = bf16[32,112,256]{2,1,0:T(8,128)(2,1)} collective-permute-done((bf16[32,112,256]{2,1,0:T(8,128)(2,1)}, bf16[32,112,256]{2,1,0:T(8,128)(2,1)}, u32[]{:S(2)}, u32[]{:S(2)}) %collective-permute-start.6) | collective-permute-done | bytes 1835040 | tf_op jit(solution)/shard_map/ppermute | solution.py:28
  71.9 40.8 %collective-permute-done.7.refs_5_ = bf16[32,112,256]{2,1,0:T(8,128)(2,1)} collective-permute-done((bf16[32,112,256]{2,1,0:T(8,128)(2,1)}, bf16[32,112,256]{2,1,0:T(8,128)(2,1)}, u32[]{:S(2)}, u32[]{:S(2)}) %collective-permute-start.7) | collective-permute-done | bytes 1835040 | tf_op jit(solution)/shard_map/ppermute | solution.py:28
  112.8 2.2 copy-done
  115.0 6.8 %shard_map.61 = (bf16[16,128,256]{2,1,0:T(8,128)(2,1)S(1)}, bf16[16,128,256]{2,1,0:T(8,128)(2,1)}, bf16[16,128,256]{2,1,0:T(8,128)(2,1)}, bf16[16,128,256]{2,1,0:T(8,128)(2,1)}, f32[256,256]{1,0:T(8,128)S(1)}) custom-call(bf16[64,128,256]{2,1,0:T(8,128)(2,1)S(1)} %copy-done, bf16[64,128,256]{2,1,0:T(8,128)(2,1)} %collective-permute-done.2.refs_1_, ...), custom_call_target="tpu_custom_call" | custom-call | flops 1000 | bytes 1000 | tf_op jit(solution)/shard_map/pallas_call | solution.py:163
  123.3 6.7 %shard_map.62 = (bf16[16,128,256]{2,1,0:T(8,128)(2,1)S(1)}, bf16[16,128,256]{2,1,0:T(8,128)(2,1)}, bf16[16,128,256]{2,1,0:T(8,128)(2,1)}, bf16[16,128,256]{2,1,0:T(8,128)(2,1)S(1)}, f32[256,256]{1,0:T(8,128)S(1)}) custom-call(bf16[64,128,256]{2,1,0:T(8,128)(2,1)S(1)} %copy-done, bf16[64,128,256]{2,1,0:T(8,128)(2,1)} %collective-permute-done.2.refs_1_, ...), custom_call_target="tpu_custom_call" | custom-call | flops 1000 | bytes 1000 | tf_op jit(solution)/shard_map/pallas_call | solution.py:163
  132.1 18.5 %collective-permute-done.3.refs_3_ = bf16[32,112,256]{2,1,0:T(8,128)(2,1)} collective-permute-done((bf16[32,112,256]{2,1,0:T(8,128)(2,1)}, bf16[32,112,256]{2,1,0:T(8,128)(2,1)}, u32[]{:S(2)}, u32[]{:S(2)}) %collective-permute-start.3) | collective-permute-done | bytes 1835040 | tf_op jit(solution)/shard_map/ppermute | solution.py:28
  151.9 2.6 collective-permute-start.23
  154.5 36.9 %collective-permute-done.4.refs_5_ = bf16[32,112,256]{2,1,0:T(8,128)(2,1)} collective-permute-done((bf16[32,112,256]{2,1,0:T(8,128)(2,1)}, bf16[32,112,256]{2,1,0:T(8,128)(2,1)}, u32[]{:S(2)}, u32[]{:S(2)}) %collective-permute-start.4) | collective-permute-done | bytes 1835040 | tf_op jit(solution)/shard_map/ppermute | solution.py:28
  191.4 2.2 copy-done.1
  193.6 6.1 %shard_map.63 = (bf16[16,128,256]{2,1,0:T(8,128)(2,1)S(1)}, bf16[16,128,256]{2,1,0:T(8,128)(2,1)S(1)}, bf16[16,128,256]{2,1,0:T(8,128)(2,1)S(1)}, bf16[16,128,256]{2,1,0:T(8,128)(2,1)S(1)}, f32[256,256]{1,0:T(8,128)S(1)}) custom-call(bf16[64,128,256]{2,1,0:T(8,128)(2,1)S(1)} %copy-done.1, bf16[64,128,256]{2,1,0:T(8,128)(2,1)} %collective-permute-done.2.refs_1_, ...), custom_call_target="tpu_custom_call" | custom-call | flops 1000 | bytes 1000 | tf_op jit(solution)/shard_map/pallas_call | solution.py:163
  200.7 6.5 %shard_map.64 = (bf16[16,128,256]{2,1,0:T(8,128)(2,1)S(1)}, bf16[16,128,256]{2,1,0:T(8,128)(2,1)}, bf16[16,128,256]{2,1,0:T(8,128)(2,1)S(1)}, bf16[16,128,256]{2,1,0:T(8,128)(2,1)S(1)}, f32[256,256]{1,0:T(8,128)S(1)}) custom-call(bf16[64,128,256]{2,1,0:T(8,128)(2,1)S(1)} %copy-done.1, bf16[64,128,256]{2,1,0:T(8,128)(2,1)} %collective-permute-done.2.refs_1_, ...), custom_call_target="tpu_custom_call" | custom-call | flops 1000 | bytes 1000 | tf_op jit(solution)/shard_map/pallas_call | solution.py:163
  207.2 5.1 %collective-permute-done.8.piece = bf16[16,128,256]{2,1,0:T(8,128)(2,1)} collective-permute-done((bf16[16,128,256]{2,1,0:T(8,128)(2,1)}, bf16[16,128,256]{2,1,0:T(8,128)(2,1)}, u32[]{:S(2)}, u32[]{:S(2)}) %collective-permute-start.8) | collective-permute-done | bytes 1048608 | tf_op jit(solution)/shard_map/ppermute | solution.py:28
  212.5 2.3 collective-permute-start.9
  215.8 1.5 collective-permute-start.10
  217.3 19.0 %collective-permute-done.18.piece = bf16[16,128,256]{2,1,0:T(8,128)(2,1)} collective-permute-done((bf16[16,128,256]{2,1,0:T(8,128)(2,1)}, bf16[16,128,256]{2,1,0:T(8,128)(2,1)}, u32[]{:S(2)}, u32[]{:S(2)}) %collective-permute-start.18) | collective-permute-done | bytes 1048608 | tf_op jit(solution)/shard_map/ppermute | solution.py:28
  236.5 20.8 %collective-permute-done.11.piece = bf16[16,128,256]{2,1,0:T(8,128)(2,1)} collective-permute-done((bf16[16,128,256]{2,1,0:T(8,128)(2,1)}, bf16[16,128,256]{2,1,0:T(8,128)(2,1)}, u32[]{:S(2)}, u32[]{:S(2)}) %collective-permute-start.11) | collective-permute-done | bytes 1048608 | tf_op jit(solution)/shard_map/ppermute | solution.py:28
  257.3 3.6 collective-permute-start.19
  261.6 2.3 collective-permute-done.12
  264.3 38.4 %shard_map.65 = (f32[256,256]{1,0:T(8,128)}, bf16[256,256]{1,0:T(8,128)(2,1)S(1)}) custom-call(f32[64,320]{1,0:T(8,128)S(1)} %get-tuple-element.123.first, f32[64,320]{1,0:T(8,128)S(1)} %get-tuple-element.122.second), custom_call_target="tpu_custom_call" | custom-call | flops 1000 | bytes 1000 | tf_op jit(solution)/shard_map/pallas_call | solution.py:319
  302.8 2.1 shard_map.67
  304.9 2.1 shard_map.66
  308.5 18.2 %collective-permute-done.20.piece = bf16[16,128,256]{2,1,0:T(8,128)(2,1)S(1)} collective-permute-done((bf16[16,128,256]{2,1,0:T(8,128)(2,1)S(1)}, bf16[16,128,256]{2,1,0:T(8,128)(2,1)S(1)}, u32[]{:S(2)}, u32[]{:S(2)}) %collective-permute-start.20) | collective-permute-done | bytes 1048608 | tf_op jit(solution)/shard_map/ppermute | solution.py:28
  326.7 3.5 collective-permute-start.14
  332.5 1.9 shard_map.68.rest_0_
  334.4 2.8 shard_map.69.rest_0_
  337.3 2.8 shard_map.70.rest_0_
  340.1 2.9 shard_map.71.rest_0_
  343.0 1.9 shard_map.72.rest_0_
  344.9 2.8 shard_map.73.rest_0_
  347.7 2.8 shard_map.74.rest_0_
  350.5 1.9 shard_map.75.rest_0_
  352.4 1.9 shard_map.76.rest_0_
  354.3 1.9 shard_map.77.rest_0_
  356.1 1.9 shard_map.78.rest_0_
  358.0 1.9 shard_map.79.rest_0_
  359.9 1.9 shard_map.80.rest_0_
  361.8 2.8 shard_map.81.result
  364.6 1.8 shard_map.82.result
  366.4 1.8 shard_map.83.result
  368.1 1.8 shard_map.84.result
  369.9 2.5 collective-permute-done.13.piece
  372.4 1.8 shard_map.85
  (97 shorter events, 21.2 us)
Async XLA Ops:
  0.6 33.6 %copy-start.15 = (bf16[1,1,128,256]{3,2,1,0:T(8,128)(2,1)S(1)}, bf16[1,1,128,256]{3,2,1,0:T(8,128)(2,1)}, u32[]{:S(2)}) copy-start(bf16[1,1,128,256]{3,2,1,0:T(8,128)(2,1)} %param.5) | copy-start | bytes 196612
  0.6 33.7 %copy-start.14 = (bf16[512,512]{1,0:T(8,128)(2,1)S(1)}, bf16[512,512]{1,0:T(8,128)(2,1)}, u32[]{:S(2)}) copy-start(bf16[512,512]{1,0:T(8,128)(2,1)} %param.6) | copy-start | bytes 1572868
  4.0 19.4 %collective-permute-start = (bf16[66,16,256]{2,1,0:T(8,128)(2,1)}, bf16[66,16,256]{2,1,0:T(8,128)(2,1)S(1)}, u32[]{:S(2)}, u32[]{:S(2)}) collective-permute-start(bf16[66,16,256]{2,1,0:T(8,128)(2,1)} %get-tuple-element.69), channel_id=1, source_target_pairs={{0,8},{4,12},{8,0},{12,4},{1,9},{5,13},{9,1},{13,5},{2,10},{6,14},... | collective-permute-start | bytes 1622024 | tf_op jit(solution)/shard_map/ppermute | solution.py:28
  6.1 24.3 %collective-permute-start.1 = (bf16[66,16,256]{2,1,0:T(8,128)(2,1)}, bf16[66,16,256]{2,1,0:T(8,128)(2,1)S(1)}, u32[]{:S(2)}, u32[]{:S(2)}) collective-permute-start(bf16[66,16,256]{2,1,0:T(8,128)(2,1)} %get-tuple-element.70), channel_id=1, source_target_pairs={{0,12},{4,8},{8,4},{12,0},{1,13},{5,9},{9,5},{13,1},{2,14},{6,10},... | collective-permute-start | bytes 1622024 | tf_op jit(solution)/shard_map/ppermute | solution.py:28
  30.4 7.5 %collective-permute-start.2 = (bf16[64,128,256]{2,1,0:T(8,128)(2,1)}, bf16[64,128,256]{2,1,0:T(8,128)(2,1)}, u32[]{:S(2)}, u32[]{:S(2)}) collective-permute-start(bf16[64,128,256]{2,1,0:T(8,128)(2,1)} %get-tuple-element.73), channel_id=1, source_target_pairs={{0,4},{4,0},{8,12},{12,8},{1,5},{5,1},{9,13},{13,9},{2,6},{6,2},{1... | collective-permute-start | bytes 12582920 | tf_op jit(solution)/shard_map/ppermute | solution.py:28
  30.5 41.4 %collective-permute-start.6 = (bf16[32,112,256]{2,1,0:T(8,128)(2,1)}, bf16[32,112,256]{2,1,0:T(8,128)(2,1)}, u32[]{:S(2)}, u32[]{:S(2)}) collective-permute-start(bf16[32,112,256]{2,1,0:T(8,128)(2,1)} %get-tuple-element.81), channel_id=1, source_target_pairs={{0,8},{4,12},{8,0},{12,4},{1,9},{5,13},{9,1},{13,5},{2,10},{6,14},... | collective-permute-start | bytes 5505032 | tf_op jit(solution)/shard_map/ppermute | solution.py:28
  31.9 80.9 %collective-permute-start.7 = (bf16[32,112,256]{2,1,0:T(8,128)(2,1)}, bf16[32,112,256]{2,1,0:T(8,128)(2,1)}, u32[]{:S(2)}, u32[]{:S(2)}) collective-permute-start(bf16[32,112,256]{2,1,0:T(8,128)(2,1)} %get-tuple-element.82), channel_id=1, source_target_pairs={{0,12},{4,8},{8,4},{12,0},{1,13},{5,9},{9,5},{13,1},{2,14},{6,10},... | collective-permute-start | bytes 5505032 | tf_op jit(solution)/shard_map/ppermute | solution.py:28
  32.6 117.9 %collective-permute-start.3 = (bf16[32,112,256]{2,1,0:T(8,128)(2,1)}, bf16[32,112,256]{2,1,0:T(8,128)(2,1)}, u32[]{:S(2)}, u32[]{:S(2)}) collective-permute-start(bf16[32,112,256]{2,1,0:T(8,128)(2,1)} %get-tuple-element.77), channel_id=1, source_target_pairs={{0,8},{4,12},{8,0},{12,4},{1,9},{5,13},{9,1},{13,5},{2,10},{6,14},... | collective-permute-start | bytes 5505032 | tf_op jit(solution)/shard_map/ppermute | solution.py:28
  37.9 153.5 %collective-permute-start.4 = (bf16[32,112,256]{2,1,0:T(8,128)(2,1)}, bf16[32,112,256]{2,1,0:T(8,128)(2,1)}, u32[]{:S(2)}, u32[]{:S(2)}) collective-permute-start(bf16[32,112,256]{2,1,0:T(8,128)(2,1)} %get-tuple-element.79), channel_id=1, source_target_pairs={{0,12},{4,8},{8,4},{12,0},{1,13},{5,9},{9,5},{13,1},{2,14},{6,10},... | collective-permute-start | bytes 5505032 | tf_op jit(solution)/shard_map/ppermute | solution.py:28
  40.7 1.2 collective-permute-start.5
  112.8 2.2 copy-start
  121.7 8.3 %copy-start.10 = (bf16[16,128,256]{2,1,0:T(8,128)(2,1)}, bf16[16,128,256]{2,1,0:T(8,128)(2,1)S(1)}, u32[]{:S(2)}) copy-start(bf16[16,128,256]{2,1,0:T(8,128)(2,1)S(1)} %get-tuple-element.120.piece) | copy-start | bytes 3145732
  121.7 90.6 %collective-permute-start.8 = (bf16[16,128,256]{2,1,0:T(8,128)(2,1)}, bf16[16,128,256]{2,1,0:T(8,128)(2,1)}, u32[]{:S(2)}, u32[]{:S(2)}) collective-permute-start(bf16[16,128,256]{2,1,0:T(8,128)(2,1)} %get-tuple-element.88), channel_id=1, source_target_pairs={{0,8},{4,12},{8,0},{12,4},{1,9},{5,13},{9,1},{13,5},{2,10},{6,14},... | collective-permute-start | bytes 3145736 | tf_op jit(solution)/shard_map/ppermute | solution.py:28
  123.2 113.1 %collective-permute-start.18 = (bf16[16,128,256]{2,1,0:T(8,128)(2,1)}, bf16[16,128,256]{2,1,0:T(8,128)(2,1)}, u32[]{:S(2)}, u32[]{:S(2)}) collective-permute-start(bf16[16,128,256]{2,1,0:T(8,128)(2,1)} %get-tuple-element.104), channel_id=1, source_target_pairs={{0,12},{4,8},{8,4},{12,0},{1,13},{5,9},{9,5},{13,1},{2,14},{6,10},... | collective-permute-start | bytes 3145736 | tf_op jit(solution)/shard_map/ppermute | solution.py:28
  130.1 1.0 copy-start.2
  131.1 1.0 copy-start.12
  150.6 106.7 %collective-permute-start.11 = (bf16[16,128,256]{2,1,0:T(8,128)(2,1)}, bf16[16,128,256]{2,1,0:T(8,128)(2,1)}, u32[]{:S(2)}, u32[]{:S(2)}) collective-permute-start(bf16[16,128,256]{2,1,0:T(8,128)(2,1)} %get-tuple-element.91), channel_id=1, source_target_pairs={{0,8},{4,12},{8,0},{12,4},{1,9},{5,13},{9,1},{13,5},{2,10},{6,14},... | collective-permute-start | bytes 3145736 | tf_op jit(solution)/shard_map/ppermute | solution.py:28
  151.9 109.0 %collective-permute-start.23 = (bf16[16,128,256]{2,1,0:T(8,128)(2,1)}, bf16[16,128,256]{2,1,0:T(8,128)(2,1)}, u32[]{:S(2)}, u32[]{:S(2)}) collective-permute-start(bf16[16,128,256]{2,1,0:T(8,128)(2,1)} %get-tuple-element.114), channel_id=1, source_target_pairs={{0,4},{4,0},{8,12},{12,8},{1,5},{5,1},{9,13},{13,9},{2,6},{6,2},{1... | collective-permute-start | bytes 3145736 | tf_op jit(solution)/shard_map/ppermute | solution.py:28
  191.4 70.1 %collective-permute-start.24 = (bf16[16,128,256]{2,1,0:T(8,128)(2,1)}, bf16[16,128,256]{2,1,0:T(8,128)(2,1)}, u32[]{:S(2)}, u32[]{:S(2)}) collective-permute-start(bf16[16,128,256]{2,1,0:T(8,128)(2,1)} %get-tuple-element.118), channel_id=1, source_target_pairs={{0,4},{4,0},{8,12},{12,8},{1,5},{5,1},{9,13},{13,9},{2,6},{6,2},{1... | collective-permute-start | bytes 3145736 | tf_op jit(solution)/shard_map/ppermute | solution.py:28
  191.4 2.2 copy-start.1
  193.6 42.8 %copy-start.13 = (bf16[16,128,256]{2,1,0:T(8,128)(2,1)S(1)}, bf16[16,128,256]{2,1,0:T(8,128)(2,1)}, u32[]{:S(2)}) copy-start(bf16[16,128,256]{2,1,0:T(8,128)(2,1)} %copy-done.12) | copy-start | bytes 3145732
  199.7 1.0 copy-start.6
  207.2 57.1 %copy-start.4 = (bf16[16,128,256]{2,1,0:T(8,128)(2,1)}, bf16[16,128,256]{2,1,0:T(8,128)(2,1)S(1)}, u32[]{:S(2)}) copy-start(bf16[16,128,256]{2,1,0:T(8,128)(2,1)S(1)} %get-tuple-element.100.piece) | copy-start | bytes 3145732
  212.5 3.2 collective-permute-start.9
  215.8 45.1 %collective-permute-start.10 = (f32[64,320]{1,0:T(8,128)S(1)}, f32[64,320]{1,0:T(8,128)S(1)}, u32[]{:S(2)}, u32[]{:S(2)}) collective-permute-start(f32[64,320]{1,0:T(8,128)S(1)} %select_add_fusion), channel_id=1, source_target_pairs={{0,8},{4,12},{8,0},{12,4},{1,9},{5,13},{9,1},{13,5},{2,10},{6,14},... | collective-permute-start | bytes 245768 | tf_op jit(solution)/shard_map/ppermute | solution.py:28
  236.3 70.6 %collective-permute-start.22 = (bf16[16,128,256]{2,1,0:T(8,128)(2,1)S(1)}, bf16[16,128,256]{2,1,0:T(8,128)(2,1)S(1)}, u32[]{:S(2)}, u32[]{:S(2)}) collective-permute-start(bf16[16,128,256]{2,1,0:T(8,128)(2,1)S(1)} %copy-done.13), channel_id=1, source_target_pairs={{0,12},{4,8},{8,4},{12,0},{1,13},{5,9},{9,5},{13,1},{2,14},{6,10},... | collective-permute-start | bytes 3145736 | tf_op jit(solution)/shard_map/ppermute | solution.py:28
  257.3 51.1 %collective-permute-start.19 = (bf16[16,128,256]{2,1,0:T(8,128)(2,1)S(1)}, bf16[16,128,256]{2,1,0:T(8,128)(2,1)S(1)}, u32[]{:S(2)}, u32[]{:S(2)}) collective-permute-start(bf16[16,128,256]{2,1,0:T(8,128)(2,1)S(1)} %get-tuple-element.106), channel_id=1, source_target_pairs={{0,12},{4,8},{8,4},{12,0},{1,13},{5,9},{9,5},{13,1},{2,14},{6,10},... | collective-permute-start | bytes 3145736 | tf_op jit(solution)/shard_map/ppermute | solution.py:28
  260.9 65.8 %collective-permute-start.20 = (bf16[16,128,256]{2,1,0:T(8,128)(2,1)S(1)}, bf16[16,128,256]{2,1,0:T(8,128)(2,1)S(1)}, u32[]{:S(2)}, u32[]{:S(2)}) collective-permute-start(bf16[16,128,256]{2,1,0:T(8,128)(2,1)S(1)} %get-tuple-element.109), channel_id=1, source_target_pairs={{0,8},{4,12},{8,0},{12,4},{1,9},{5,13},{9,1},{13,5},{2,10},{6,14},... | collective-permute-start | bytes 3145736 | tf_op jit(solution)/shard_map/ppermute | solution.py:28
  260.9 69.4 %collective-permute-start.21 = (bf16[16,128,256]{2,1,0:T(8,128)(2,1)S(1)}, bf16[16,128,256]{2,1,0:T(8,128)(2,1)S(1)}, u32[]{:S(2)}, u32[]{:S(2)}) collective-permute-start(bf16[16,128,256]{2,1,0:T(8,128)(2,1)S(1)} %get-tuple-element.110), channel_id=1, source_target_pairs={{0,4},{4,0},{8,12},{12,8},{1,5},{5,1},{9,13},{13,9},{2,6},{6,2},{1... | collective-permute-start | bytes 3145736 | tf_op jit(solution)/shard_map/ppermute | solution.py:28
  261.5 2.4 collective-permute-start.12
  263.9 97.8 %collective-permute-start.17 = (bf16[16,128,256]{2,1,0:T(8,128)(2,1)}, bf16[16,128,256]{2,1,0:T(8,128)(2,1)}, u32[]{:S(2)}, u32[]{:S(2)}) collective-permute-start(bf16[16,128,256]{2,1,0:T(8,128)(2,1)} %get-tuple-element.99), channel_id=1, source_target_pairs={{0,4},{4,0},{8,12},{12,8},{1,5},{5,1},{9,13},{13,9},{2,6},{6,2},{1... | collective-permute-start | bytes 3145736 | tf_op jit(solution)/shard_map/ppermute | solution.py:28
  307.0 57.7 %collective-permute-start.16 = (bf16[64,16,256]{2,1,0:T(8,128)(2,1)}, bf16[64,16,256]{2,1,0:T(8,128)(2,1)}, u32[]{:S(2)}, u32[]{:S(2)}) collective-permute-start(bf16[64,16,256]{2,1,0:T(8,128)(2,1)} %get-tuple-element.98), channel_id=1, source_target_pairs={{0,8},{4,12},{8,0},{12,4},{1,9},{5,13},{9,1},{13,5},{2,10},{6,14},... | collective-permute-start | bytes 1572872 | tf_op jit(solution)/shard_map/ppermute | solution.py:28
  308.4 57.9 %collective-permute-start.15 = (bf16[64,16,256]{2,1,0:T(8,128)(2,1)}, bf16[64,16,256]{2,1,0:T(8,128)(2,1)}, u32[]{:S(2)}, u32[]{:S(2)}) collective-permute-start(bf16[64,16,256]{2,1,0:T(8,128)(2,1)} %get-tuple-element.97), channel_id=1, source_target_pairs={{0,8},{4,12},{8,0},{12,4},{1,9},{5,13},{9,1},{13,5},{2,10},{6,14},... | collective-permute-start | bytes 1572872 | tf_op jit(solution)/shard_map/ppermute | solution.py:28
  326.7 41.4 %collective-permute-start.14 = (bf16[64,16,256]{2,1,0:T(8,128)(2,1)}, bf16[64,16,256]{2,1,0:T(8,128)(2,1)}, u32[]{:S(2)}, u32[]{:S(2)}) collective-permute-start(bf16[64,16,256]{2,1,0:T(8,128)(2,1)} %get-tuple-element.95), channel_id=1, source_target_pairs={{0,12},{4,8},{8,4},{12,0},{1,13},{5,9},{9,5},{13,1},{2,14},{6,10},... | collective-permute-start | bytes 1572872 | tf_op jit(solution)/shard_map/ppermute | solution.py:28
  330.3 1.0 copy-start.8
  331.3 41.1 %collective-permute-start.13 = (bf16[64,16,256]{2,1,0:T(8,128)(2,1)}, bf16[64,16,256]{2,1,0:T(8,128)(2,1)}, u32[]{:S(2)}, u32[]{:S(2)}) collective-permute-start(bf16[64,16,256]{2,1,0:T(8,128)(2,1)} %get-tuple-element.94), channel_id=1, source_target_pairs={{0,12},{4,8},{8,4},{12,0},{1,13},{5,9},{9,5},{13,1},{2,14},{6,10},... | collective-permute-start | bytes 1572872 | tf_op jit(solution)/shard_map/ppermute | solution.py:28
  331.3 1.2 copy-start.11
  340.1 2.9 copy-start.3
  350.5 1.9 copy-start.7
  352.4 1.9 copy-start.9
  358.0 1.9 copy-start.5

commit v2 on v1

--- a/solution.py
+++ b/solution.py
@@ -39,7 +39,7 @@
     )
 
 
-def y_kernel(count, band, cuts, window, walkers, kinetic, *rest):
+def y_kernel(count, band, cuts, carry, walkers, kinetic, *rest):
     outs, own, turned = rest[-2 - len(cuts) : -2], rest[-2], rest[-1]
     me = lax.axis_index("site")
     depth = own.shape[0]
@@ -52,22 +52,11 @@
             own[pl.ds(row, size), :] = kinetic[pl.ds(start, size), :]
             row += size
 
-    fine = walkers.shape[0]
-    turn = pl.program_id(0) % (ROWS // fine)
-    for r in range(fine):
+    for r in range(ROWS):
         line = jnp.dot(own[...], walkers[r], preferred_element_type=jnp.float32)
-        at = turn * fine + r if fine < ROWS else r
         for h in range(turned.shape[0]):
             part = line[:, h * LANES : (h + 1) * LANES]
-            turned[h, pl.ds(at, depth, stride=ROWS + PAD), :] = part
-    if fine < ROWS:
-        pl.when(turn == ROWS // fine - 1)(functools.partial(write_cuts, count, band, cuts, window, outs, turned, rest))
-    else:
-        write_cuts(count, band, cuts, window, outs, turned, rest)
-
-
-def write_cuts(count, band, cuts, window, outs, turned, rest):
-    me = lax.axis_index("site")
+            turned[h, pl.ds(r, depth, stride=ROWS + PAD), :] = part
     row = 0
     for (s, first, size), out in zip(cuts, outs):
         for h in range(turned.shape[0]):
@@ -75,7 +64,8 @@
             piece = piece.reshape(size, ROWS + PAD, LANES)[:, :ROWS]
             out[:size, :, h * LANES : (h + 1) * LANES] = piece.astype(out.dtype)
         row += size
-        if window:
+        if s in carry and first == 0:
+            window = max(LANES, band)
             begin = partner(me, s, count) * band
             tile = pl.multiple_of(begin // window * window, LANES)
             across = out.shape[2] // band
@@ -92,29 +82,33 @@
     return -(-lines * band // (ROWS * orbitals))
 
 
-def apply_y(walkers, kinetic_y, count, cuts, sizes, fine, fields=None, window=0):
+def apply_y(walkers, kinetic_y, fields, count, cuts, sizes, carry):
     lines, width, orbitals = walkers.shape
     depth = sum(size for _, _, size in cuts)
     used = max(sizes)
-    extra = rows_for_fields(lines, width // count, orbitals) if window else 0
+    extra = rows_for_fields(lines, width // count, orbitals)
+
+    def out_rows(cut):
+        return cut[2] + (extra if cut[0] in carry and cut[1] == 0 else 0)
 
     def out_spec(cut, size):
         late = (used - size) // ROWS
         return pl.BlockSpec(
-            (cut[2] + extra, ROWS, orbitals), lambda i: (0, jnp.maximum(i * fine // ROWS - late, 0), 0)
+            (out_rows(cut), ROWS, orbitals),
+            lambda i: (0, jnp.maximum(i - late, 0) if late else i, 0),
         )
 
     return pl.pallas_call(
-        functools.partial(y_kernel, count, width // count, cuts, window),
-        grid=(used // fine,),
+        functools.partial(y_kernel, count, width // count, cuts, carry),
+        grid=(used // ROWS,),
         in_specs=[
-            pl.BlockSpec((fine, width, orbitals), lambda i: (i, 0, 0)),
+            pl.BlockSpec((ROWS, width, orbitals), lambda i: (i, 0, 0)),
             pl.BlockSpec((width, width), lambda i: (0, 0)),
-        ]
-        + [pl.BlockSpec((lines, width), lambda i: (0, 0))] * (window > 0),
+            pl.BlockSpec((lines, width), lambda i: (0, 0)),
+        ],
         out_specs=[out_spec(cut, size) for cut, size in zip(cuts, sizes)],
         out_shape=[
-            jax.ShapeDtypeStruct((cut[2] + extra, size, orbitals), jnp.bfloat16)
+            jax.ShapeDtypeStruct((out_rows(cut), size, orbitals), jnp.bfloat16)
             for cut, size in zip(cuts, sizes)
         ],
         scratch_shapes=[
@@ -122,7 +116,7 @@
             pltpu.VMEM((orbitals // LANES, depth * (ROWS + PAD), LANES), jnp.float32),
         ],
         **settings(VMEM_MOST),
-    )(walkers, kinetic_y, *([fields] if window else []))
+    )(walkers, kinetic_y, fields)
 
 
 def x_kernel(count, group, *refs):
@@ -341,47 +335,50 @@
     steps = range(count)
     order = jnp.stack([partner(me, s, count) for s in steps])
 
-    window = max(LANES, band)
     extra = rows_for_fields(lines, band, orbitals)
     far = [s for s in steps if s > 1 and lines > ROWS]
     near = [s for s in steps if s not in far]
     head = {}
     if far:
-        arrays = apply_y(
-            walkers, kinetic_y, count, [(s, 0, band) for s in far], [ROWS] * len(far), ROWS, fields, window
-        )
+        cuts = [(s, 0, band) for s in far]
+        arrays = apply_y(walkers, kinetic_y, fields, count, cuts, [ROWS] * len(far), far)
         kinetic_y, *arrays = tie(kinetic_y, *arrays)
         head = {s: trade(a, s, count) for s, a in zip(far, arrays)}
+    near_cuts = [(0, part), (part, part), (2 * part, band - 2 * part)] if chunks >= 4 else [(0, band)]
     cuts = [(s, first, wide) for first in range(0, band, wide) for s in far]
-    cuts += [(s, 0, band) for s in near]
+    cuts += [(s, *cut) for s in near for cut in ([(0, band)] if s == 0 or not far else near_cuts)]
     sizes = [lines if s in near else lines - ROWS for s, _, _ in cuts]
-    arrays = apply_y(walkers, kinetic_y, count, cuts, sizes, ROWS)
+    arrays = apply_y(walkers, kinetic_y, fields, count, cuts, sizes, near)
     tail = {(s, first): a for (s, first, _), a in zip(cuts, arrays)}
-    late = [key for key in tail if key[0] in near or key[1] > 0]
-    if far:
-        held = tie(*[tail[key] for key in late], *[head[s] for s in far])
-        tail.update(zip(late, held))
-        head.update(zip(far, held[len(late) :]))
+    def hold(key, *keys):
+        held = tie(tail[key], *[tail[k] if isinstance(k, tuple) else head[k] for k in keys])
+        tail[key] = held[0]
+        for k, array in zip(keys, held[1:]):
+            (tail if isinstance(k, tuple) else head)[k] = array
+
+    sent = set()
+
+    def go(key):
+        tail[key] = trade(tail[key], key[0], count)
+        sent.add(key)
+
     for s in far:
-        tail[s, 0] = trade(tail[s, 0], s, count)
-    for s in near:
-        tail[s, 0] = trade(tail[s, 0], s, count)
-    by_band = jnp.take(fields.reshape(lines, count, band), order, axis=1)
-    by_band, tail[near[-1], 0] = tie(by_band, tail[near[-1], 0])
-    own_fields = {s: trade(by_band[:, s], s, count) for s in near}
-    for first in range(wide, band, wide):
-        for s in far:
-            if first > wide:
-                tail[s, first], tail[s, first - 2 * wide] = tie(
-                    tail[s, first], tail[s, first - 2 * wide]
-                )
-            elif s != far[0]:
-                tail[s, first], tail[near[-1], 0] = tie(tail[s, first], tail[near[-1], 0])
-            tail[s, first] = trade(tail[s, first], s, count)
-    for s in far:
-        sent = head[s][band:].reshape(extra, ROWS, orbitals // band, band)
-        own_fields[s] = jnp.swapaxes(sent, 1, 2).reshape(-1, band)[:lines]
-    own_fields = jnp.stack([own_fields[s] for s in steps])
+        go((s, 0))
+    if far and chunks >= 4:
+        y, z = (near[-1], 0), (near[-1], part)
+        hold(y, *far)
+        go(y)
+        hold(z, y, *[(s, 0) for s in far])
+        go(z)
+    for key in tail:
+        if key not in sent:
+            go(key)
+    own_fields = []
+    for s in steps:
+        sent = (head[s] if s in far else tail[s, 0])[-extra:, :ROWS]
+        sent = sent.reshape(extra, ROWS, orbitals // band, band)
+        own_fields.append(jnp.swapaxes(sent, 1, 2).reshape(-1, band)[:lines])
+    own_fields = jnp.stack(own_fields)
     own_fields = own_fields.reshape(count * lines, band // group, group).swapaxes(0, 1)
     turned_x = kinetic_x.reshape(count, lines, count, lines)
     turned_x = jnp.take(jnp.take(turned_x, order, axis=0), order, axis=2).reshape(kinetic_x.shape)
@@ -393,7 +390,7 @@
         for s in steps:
             if s in far:
                 pieces.append((head[s], 0))
-            begin = first // wide * wide if s in far else 0
+            begin = max(at for step, at in tail if step == s and at <= first)
             pieces.append((tail[s, begin], begin))
         scaled, gram = apply_x(pieces, own_fields, turned_x, gram, count, first, part)
         ready.append(scaled)

time: 375 us -> 372 us (level)
  waiting for transfers between devices: 204 us -> 194 us
    ppermute x25 -> x26, waiting for transfers between devices: 204 us -> 194 us  [trade(): lax.ppermute(piece, 'site', [(i, partner(i, step, count)) for i in range(...]
    ppermute x25 -> x26, starting transfers between devices: 27.4 us -> 30 us  [trade(): lax.ppermute(piece, 'site', [(i, partner(i, step, count)) for i in range(...]
    unnamed x33 -> x34, local copies, waits for them, and re-layouts: 9.79 us -> 11.9 us
  transfers between devices with their start and end apart: 25 -> 26, of which waited for: 14 -> 13; matrix products, arithmetic and copies ran while one was open for 1% -> 2% of each run, Pallas kernels for 33% -> 33%
where the time goes in v2:
time: 372 us; the launch traced here: 371 us
  waiting for transfers between devices  194 us (52%)
  Pallas kernels  128 us (34%)
  starting transfers between devices  30 us (8%)
  local copies, waits for them, and re-layouts  16.7 us (4%)
    ppermute x26, waiting for transfers between devices, trade(): lax.ppermute(piece, 'site', [(i, partner(i, step, count)) for i in range(...  194 us
    pallas_call x1, Pallas kernels, factor(): pl.pallas_call(functools.partial(factor_kernel, scale), out_shape=[jax.Sh...  38.4 us
    pallas_call x14, Pallas kernels, finish(): pl.pallas_call(last_kernel, grid_spec=pltpu.PrefetchScalarGridSpec(num_sc...  32.1 us
    ppermute x26, starting transfers between devices, trade(): lax.ppermute(piece, 'site', [(i, partner(i, step, count)) for i in range(...  30 us
    pallas_call x4, Pallas kernels, apply_x(): pl.pallas_call(functools.partial(x_kernel, count, group), grid=(part // g...  26.1 us
    pallas_call x2, Pallas kernels, apply_y(): pl.pallas_call(functools.partial(y_kernel, count, width // count, cuts, c...  20.2 us
    unnamed x34, local copies, waits for them, and re-layouts  11.9 us
  transfers between devices with their start and end apart: 26, of which 13 were waited for; matrix products, arithmetic and copies ran while one was open for 2% of the time, Pallas kernels for 33%

profile of v2, /device:TPU:1, one launch (start us, length us, event | category | flops | bytes accessed | tf_op | source)
XLA Modules:
  0.0 371.4 jit_solution(16590389631377582990)
XLA Ops:
  0.6 3.4 shard_map.59
  4.0 2.0 collective-permute-start.1
  6.6 16.9 %shard_map.60 = (bf16[32,112,256]{2,1,0:T(8,128)(2,1)}, bf16[32,112,256]{2,1,0:T(8,128)(2,1)}, bf16[32,112,256]{2,1,0:T(8,128)(2,1)}, bf16[32,112,256]{2,1,0:T(8...) custom-call(bf16[128,256,256]{2,1,0:T(8,128)(2,1)} %bitcast.58, ...), custom_call_target="tpu_custom_call" | custom-call | flops 1000 | bytes 1000 | tf_op jit(solution)/shard_map/pallas_call | solution.py:101
  23.5 1.7 collective-permute-start.6
  25.5 5.7 %collective-permute-done.2.refs_4_ = bf16[66,16,256]{2,1,0:T(8,128)(2,1)S(1)} collective-permute-done((bf16[66,16,256]{2,1,0:T(8,128)(2,1)}, bf16[66,16,256]{2,1,0:T(8,128)(2,1)S(1)}, u32[]{:S(2)}, u32[]{:S(2)}) %collective-permute-start.2) | collective-permute-done | bytes 540704 | tf_op jit(solution)/shard_map/ppermute | solution.py:28
  39.3 29.9 %collective-permute-done.6.refs_3_ = bf16[32,112,256]{2,1,0:T(8,128)(2,1)} collective-permute-done((bf16[32,112,256]{2,1,0:T(8,128)(2,1)}, bf16[32,112,256]{2,1,0:T(8,128)(2,1)}, u32[]{:S(2)}, u32[]{:S(2)}) %collective-permute-start.6) | collective-permute-done | bytes 1835040 | tf_op jit(solution)/shard_map/ppermute | solution.py:28
  69.3 40.7 %collective-permute-done.7.refs_5_ = bf16[32,112,256]{2,1,0:T(8,128)(2,1)} collective-permute-done((bf16[32,112,256]{2,1,0:T(8,128)(2,1)}, bf16[32,112,256]{2,1,0:T(8,128)(2,1)}, u32[]{:S(2)}, u32[]{:S(2)}) %collective-permute-start.7) | collective-permute-done | bytes 1835040 | tf_op jit(solution)/shard_map/ppermute | solution.py:28
  111.5 2.2 copy-done
  115.0 6.7 %shard_map.61 = (bf16[16,128,256]{2,1,0:T(8,128)(2,1)S(1)}, bf16[16,128,256]{2,1,0:T(8,128)(2,1)}, bf16[16,128,256]{2,1,0:T(8,128)(2,1)}, bf16[16,128,256]{2,1,0:T(8,128)(2,1)}, f32[256,256]{1,0:T(8,128)S(1)}) custom-call(bf16[66,128,256]{2,1,0:T(8,128)(2,1)S(1)} %copy-done, bf16[18,128,256]{2,1,0:T(8,128)(2,1)S(1)} %copy-done.3, ...), custom_call_target="tpu_custom_call" | custom-call | flops 1000 | bytes 1000 | tf_op jit(solution)/shard_map/pallas_call | solution.py:157
  124.2 23.7 %collective-permute-done.3.refs_3_ = bf16[32,112,256]{2,1,0:T(8,128)(2,1)} collective-permute-done((bf16[32,112,256]{2,1,0:T(8,128)(2,1)}, bf16[32,112,256]{2,1,0:T(8,128)(2,1)}, u32[]{:S(2)}, u32[]{:S(2)}) %collective-permute-start.3) | collective-permute-done | bytes 1835040 | tf_op jit(solution)/shard_map/ppermute | solution.py:28
  147.9 3.7 %collective-permute-start.19 = (bf16[16,128,256]{2,1,0:T(8,128)(2,1)}, bf16[16,128,256]{2,1,0:T(8,128)(2,1)}, u32[]{:S(2)}, u32[]{:S(2)}) collective-permute-start(bf16[16,128,256]{2,1,0:T(8,128)(2,1)} %get-tuple-element.102), channel_id=1, source_target_pairs={{0,12},{4,8},{8,4},{12,0},{1,13},{5,9},{9,5},{13,1},{2,14},{6,10},... | collective-permute-start | bytes 3145736 | tf_op jit(solution)/shard_map/ppermute | solution.py:28
  151.7 6.8 %shard_map.62 = (bf16[16,128,256]{2,1,0:T(8,128)(2,1)S(1)}, bf16[16,128,256]{2,1,0:T(8,128)(2,1)}, bf16[16,128,256]{2,1,0:T(8,128)(2,1)}, bf16[16,128,256]{2,1,0:T(8,128)(2,1)S(1)}, f32[256,256]{1,0:T(8,128)S(1)}) custom-call(bf16[66,128,256]{2,1,0:T(8,128)(2,1)S(1)} %copy-done, bf16[16,128,256]{2,1,0:T(8,128)(2,1)} %collective-permute-done.8.refs_1_, ...), custom_call_target="tpu_custom_call" | custom-call | flops 1000 | bytes 1000 | tf_op jit(solution)/shard_map/pallas_call | solution.py:157
  160.4 28.2 %collective-permute-done.4.refs_5_ = bf16[32,112,256]{2,1,0:T(8,128)(2,1)} collective-permute-done((bf16[32,112,256]{2,1,0:T(8,128)(2,1)}, bf16[32,112,256]{2,1,0:T(8,128)(2,1)}, u32[]{:S(2)}, u32[]{:S(2)}) %collective-permute-start.4) | collective-permute-done | bytes 1835040 | tf_op jit(solution)/shard_map/ppermute | solution.py:28
  188.6 1.8 collective-permute-start.12
  190.4 2.2 copy-done.1
  192.6 6.1 %shard_map.63 = (bf16[16,128,256]{2,1,0:T(8,128)(2,1)S(1)}, bf16[16,128,256]{2,1,0:T(8,128)(2,1)S(1)}, bf16[16,128,256]{2,1,0:T(8,128)(2,1)S(1)}, bf16[16,128,256]{2,1,0:T(8,128)(2,1)S(1)}, f32[256,256]{1,0:T(8,128)S(1)}) custom-call(bf16[66,128,256]{2,1,0:T(8,128)(2,1)S(1)} %copy-done.1, bf16[32,128,256]{2,1,0:T(8,128)(2,1)} %collective-permute-done.refs_1_, ...), custom_call_target="tpu_custom_call" | custom-call | flops 1000 | bytes 1000 | tf_op jit(solution)/shard_map/pallas_call | solution.py:157
  199.7 6.6 %shard_map.64 = (bf16[16,128,256]{2,1,0:T(8,128)(2,1)S(1)}, bf16[16,128,256]{2,1,0:T(8,128)(2,1)}, bf16[16,128,256]{2,1,0:T(8,128)(2,1)S(1)}, bf16[16,128,256]{2,1,0:T(8,128)(2,1)S(1)}, f32[256,256]{1,0:T(8,128)S(1)}) custom-call(bf16[66,128,256]{2,1,0:T(8,128)(2,1)S(1)} %copy-done.1, bf16[32,128,256]{2,1,0:T(8,128)(2,1)} %collective-permute-done.refs_1_, ...), custom_call_target="tpu_custom_call" | custom-call | flops 1000 | bytes 1000 | tf_op jit(solution)/shard_map/pallas_call | solution.py:157
  206.2 3.5 collective-permute-done.9.piece
  209.8 2.1 collective-permute-start.10
  213.0 1.8 collective-permute-start.11
  214.8 18.7 %collective-permute-done.19.piece = bf16[16,128,256]{2,1,0:T(8,128)(2,1)} collective-permute-done((bf16[16,128,256]{2,1,0:T(8,128)(2,1)}, bf16[16,128,256]{2,1,0:T(8,128)(2,1)}, u32[]{:S(2)}, u32[]{:S(2)}) %collective-permute-start.19) | collective-permute-done | bytes 1048608 | tf_op jit(solution)/shard_map/ppermute | solution.py:28
  235.3 21.4 %collective-permute-done.11 = f32[64,320]{1,0:T(8,128)S(1)} collective-permute-done((f32[64,320]{1,0:T(8,128)S(1)}, f32[64,320]{1,0:T(8,128)S(1)}, u32[]{:S(2)}, u32[]{:S(2)}) %collective-permute-start.11) | collective-permute-done | bytes 81952 | tf_op jit(solution)/shard_map/ppermute | solution.py:28
  257.9 2.9 collective-permute-start.22
  260.9 2.3 collective-permute-done.13
  263.6 38.4 %shard_map.65 = (f32[256,256]{1,0:T(8,128)}, bf16[256,256]{1,0:T(8,128)(2,1)S(1)}) custom-call(f32[64,320]{1,0:T(8,128)S(1)} %get-tuple-element.121.first, f32[64,320]{1,0:T(8,128)S(1)} %get-tuple-element.120.second), custom_call_target="tpu_custom_call" | custom-call | flops 1000 | bytes 1000 | tf_op jit(solution)/shard_map/pallas_call | solution.py:313
  302.1 2.1 shard_map.67
  304.1 2.0 shard_map.66
  307.6 16.4 %collective-permute-done.21.piece = bf16[16,128,256]{2,1,0:T(8,128)(2,1)S(1)} collective-permute-done((bf16[16,128,256]{2,1,0:T(8,128)(2,1)S(1)}, bf16[16,128,256]{2,1,0:T(8,128)(2,1)S(1)}, u32[]{:S(2)}, u32[]{:S(2)}) %collective-permute-start.21) | collective-permute-done | bytes 1048608 | tf_op jit(solution)/shard_map/ppermute | solution.py:28
  324.1 3.7 %collective-permute-start.15 = (bf16[64,16,256]{2,1,0:T(8,128)(2,1)}, bf16[64,16,256]{2,1,0:T(8,128)(2,1)}, u32[]{:S(2)}, u32[]{:S(2)}) collective-permute-start(bf16[64,16,256]{2,1,0:T(8,128)(2,1)} %get-tuple-element.93), channel_id=1, source_target_pairs={{0,12},{4,8},{8,4},{12,0},{1,13},{5,9},{9,5},{13,1},{2,14},{6,10},... | collective-permute-start | bytes 1572872 | tf_op jit(solution)/shard_map/ppermute | solution.py:28
  330.0 1.9 shard_map.68.rest_0_
  331.9 2.8 shard_map.69.rest_0_
  334.7 2.8 shard_map.70.rest_0_
  337.5 2.9 shard_map.71.rest_0_
  340.5 1.9 shard_map.72.rest_0_
  342.3 2.8 shard_map.73.rest_0_
  345.2 2.8 shard_map.74.rest_0_
  348.0 1.9 shard_map.75.rest_0_
  349.9 1.9 shard_map.76.rest_0_
  351.8 1.9 shard_map.77.rest_0_
  353.6 1.9 shard_map.78.rest_0_
  355.5 1.9 shard_map.79.rest_0_
  357.4 1.9 shard_map.80.rest_0_
  359.2 2.8 shard_map.81.result
  362.1 1.8 shard_map.82.result
  363.9 1.8 shard_map.83.result
  365.6 1.8 shard_map.84.result
  367.4 2.3 collective-permute-done.14.piece
  369.7 1.8 shard_map.85
  (101 shorter events, 25.4 us)
Async XLA Ops:
  0.6 32.8 %copy-start.16 = (bf16[512,512]{1,0:T(8,128)(2,1)S(1)}, bf16[512,512]{1,0:T(8,128)(2,1)}, u32[]{:S(2)}) copy-start(bf16[512,512]{1,0:T(8,128)(2,1)} %param.6) | copy-start | bytes 1572868
  4.0 21.5 %collective-permute-start.1 = (bf16[66,16,256]{2,1,0:T(8,128)(2,1)}, bf16[66,16,256]{2,1,0:T(8,128)(2,1)S(1)}, u32[]{:S(2)}, u32[]{:S(2)}) collective-permute-start(bf16[66,16,256]{2,1,0:T(8,128)(2,1)} %get-tuple-element.67), channel_id=1, source_target_pairs={{0,8},{4,12},{8,0},{12,4},{1,9},{5,13},{9,1},{13,5},{2,10},{6,14},... | collective-permute-start | bytes 1622024 | tf_op jit(solution)/shard_map/ppermute | solution.py:28
  6.1 25.2 %collective-permute-start.2 = (bf16[66,16,256]{2,1,0:T(8,128)(2,1)}, bf16[66,16,256]{2,1,0:T(8,128)(2,1)S(1)}, u32[]{:S(2)}, u32[]{:S(2)}) collective-permute-start(bf16[66,16,256]{2,1,0:T(8,128)(2,1)} %get-tuple-element.68), channel_id=1, source_target_pairs={{0,12},{4,8},{8,4},{12,0},{1,13},{5,9},{9,5},{13,1},{2,14},{6,10},... | collective-permute-start | bytes 1622024 | tf_op jit(solution)/shard_map/ppermute | solution.py:28
  23.5 45.8 %collective-permute-start.6 = (bf16[32,112,256]{2,1,0:T(8,128)(2,1)}, bf16[32,112,256]{2,1,0:T(8,128)(2,1)}, u32[]{:S(2)}, u32[]{:S(2)}) collective-permute-start(bf16[32,112,256]{2,1,0:T(8,128)(2,1)} %get-tuple-element.75), channel_id=1, source_target_pairs={{0,8},{4,12},{8,0},{12,4},{1,9},{5,13},{9,1},{13,5},{2,10},{6,14},... | collective-permute-start | bytes 5505032 | tf_op jit(solution)/shard_map/ppermute | solution.py:28
  25.2 84.7 %collective-permute-start.7 = (bf16[32,112,256]{2,1,0:T(8,128)(2,1)}, bf16[32,112,256]{2,1,0:T(8,128)(2,1)}, u32[]{:S(2)}, u32[]{:S(2)}) collective-permute-start(bf16[32,112,256]{2,1,0:T(8,128)(2,1)} %get-tuple-element.76), channel_id=1, source_target_pairs={{0,12},{4,8},{8,4},{12,0},{1,13},{5,9},{9,5},{13,1},{2,14},{6,10},... | collective-permute-start | bytes 5505032 | tf_op jit(solution)/shard_map/ppermute | solution.py:28
  31.2 3.1 collective-permute-start.5
  31.6 116.3 %collective-permute-start.3 = (bf16[32,112,256]{2,1,0:T(8,128)(2,1)}, bf16[32,112,256]{2,1,0:T(8,128)(2,1)}, u32[]{:S(2)}, u32[]{:S(2)}) collective-permute-start(bf16[32,112,256]{2,1,0:T(8,128)(2,1)} %get-tuple-element.70), channel_id=1, source_target_pairs={{0,8},{4,12},{8,0},{12,4},{1,9},{5,13},{9,1},{13,5},{2,10},{6,14},... | collective-permute-start | bytes 5505032 | tf_op jit(solution)/shard_map/ppermute | solution.py:28
  33.0 155.6 %collective-permute-start.4 = (bf16[32,112,256]{2,1,0:T(8,128)(2,1)}, bf16[32,112,256]{2,1,0:T(8,128)(2,1)}, u32[]{:S(2)}, u32[]{:S(2)}) collective-permute-start(bf16[32,112,256]{2,1,0:T(8,128)(2,1)} %get-tuple-element.72), channel_id=1, source_target_pairs={{0,12},{4,8},{8,4},{12,0},{1,13},{5,9},{9,5},{13,1},{2,14},{6,10},... | collective-permute-start | bytes 5505032 | tf_op jit(solution)/shard_map/ppermute | solution.py:28
  34.3 76.6 %copy-start.2 = (bf16[18,128,256]{2,1,0:T(8,128)(2,1)}, bf16[18,128,256]{2,1,0:T(8,128)(2,1)S(1)}, u32[]{:S(2)}) copy-start(bf16[18,128,256]{2,1,0:T(8,128)(2,1)S(1)} %collective-permute-done.5.refs_1_) | copy-start | bytes 3538948
  34.3 156.1 %collective-permute-start = (bf16[32,128,256]{2,1,0:T(8,128)(2,1)}, bf16[32,128,256]{2,1,0:T(8,128)(2,1)}, u32[]{:S(2)}, u32[]{:S(2)}) collective-permute-start(bf16[32,128,256]{2,1,0:T(8,128)(2,1)} %get-tuple-element.65), channel_id=1, source_target_pairs={{0,4},{4,0},{8,12},{12,8},{1,5},{5,1},{9,13},{13,9},{2,6},{6,2},{1... | collective-permute-start | bytes 6291464 | tf_op jit(solution)/shard_map/ppermute | solution.py:28
  110.0 41.7 %collective-permute-start.8 = (bf16[16,128,256]{2,1,0:T(8,128)(2,1)}, bf16[16,128,256]{2,1,0:T(8,128)(2,1)}, u32[]{:S(2)}, u32[]{:S(2)}) collective-permute-start(bf16[16,128,256]{2,1,0:T(8,128)(2,1)} %get-tuple-element.78), channel_id=1, source_target_pairs={{0,4},{4,0},{8,12},{12,8},{1,5},{5,1},{9,13},{13,9},{2,6},{6,2},{1... | collective-permute-start | bytes 3145736 | tf_op jit(solution)/shard_map/ppermute | solution.py:28
  111.5 2.2 copy-start
  113.7 1.3 copy-start.3
  121.7 1.0 copy-start.12
  122.7 87.0 %collective-permute-start.9 = (bf16[16,128,256]{2,1,0:T(8,128)(2,1)}, bf16[16,128,256]{2,1,0:T(8,128)(2,1)}, u32[]{:S(2)}, u32[]{:S(2)}) collective-permute-start(bf16[16,128,256]{2,1,0:T(8,128)(2,1)} %get-tuple-element.86), channel_id=1, source_target_pairs={{0,8},{4,12},{8,0},{12,4},{1,9},{5,13},{9,1},{13,5},{2,10},{6,14},... | collective-permute-start | bytes 3145736 | tf_op jit(solution)/shard_map/ppermute | solution.py:28
  147.9 85.6 %collective-permute-start.19 = (bf16[16,128,256]{2,1,0:T(8,128)(2,1)}, bf16[16,128,256]{2,1,0:T(8,128)(2,1)}, u32[]{:S(2)}, u32[]{:S(2)}) collective-permute-start(bf16[16,128,256]{2,1,0:T(8,128)(2,1)} %get-tuple-element.102), channel_id=1, source_target_pairs={{0,12},{4,8},{8,4},{12,0},{1,13},{5,9},{9,5},{13,1},{2,14},{6,10},... | collective-permute-start | bytes 3145736 | tf_op jit(solution)/shard_map/ppermute | solution.py:28
  151.7 82.0 %collective-permute-start.25 = (bf16[16,128,256]{2,1,0:T(8,128)(2,1)}, bf16[16,128,256]{2,1,0:T(8,128)(2,1)}, u32[]{:S(2)}, u32[]{:S(2)}) collective-permute-start(bf16[16,128,256]{2,1,0:T(8,128)(2,1)} %get-tuple-element.116), channel_id=1, source_target_pairs={{0,4},{4,0},{8,12},{12,8},{1,5},{5,1},{9,13},{13,9},{2,6},{6,2},{1... | collective-permute-start | bytes 3145736 | tf_op jit(solution)/shard_map/ppermute | solution.py:28
  158.4 1.0 copy-start.4
  159.4 1.0 copy-start.14
  188.6 69.3 %collective-permute-start.12 = (bf16[16,128,256]{2,1,0:T(8,128)(2,1)}, bf16[16,128,256]{2,1,0:T(8,128)(2,1)}, u32[]{:S(2)}, u32[]{:S(2)}) collective-permute-start(bf16[16,128,256]{2,1,0:T(8,128)(2,1)} %get-tuple-element.89), channel_id=1, source_target_pairs={{0,8},{4,12},{8,0},{12,4},{1,9},{5,13},{9,1},{13,5},{2,10},{6,14},... | collective-permute-start | bytes 3145736 | tf_op jit(solution)/shard_map/ppermute | solution.py:28
  190.4 70.4 %collective-permute-start.24 = (bf16[16,128,256]{2,1,0:T(8,128)(2,1)}, bf16[16,128,256]{2,1,0:T(8,128)(2,1)}, u32[]{:S(2)}, u32[]{:S(2)}) collective-permute-start(bf16[16,128,256]{2,1,0:T(8,128)(2,1)} %get-tuple-element.112), channel_id=1, source_target_pairs={{0,4},{4,0},{8,12},{12,8},{1,5},{5,1},{9,13},{13,9},{2,6},{6,2},{1... | collective-permute-start | bytes 3145736 | tf_op jit(solution)/shard_map/ppermute | solution.py:28
  190.4 2.2 copy-start.1
  192.6 40.9 %copy-start.15 = (bf16[16,128,256]{2,1,0:T(8,128)(2,1)S(1)}, bf16[16,128,256]{2,1,0:T(8,128)(2,1)}, u32[]{:S(2)}) copy-start(bf16[16,128,256]{2,1,0:T(8,128)(2,1)} %copy-done.14) | copy-start | bytes 3145732
  198.7 1.0 copy-start.8
  206.2 57.4 %copy-start.6 = (bf16[16,128,256]{2,1,0:T(8,128)(2,1)}, bf16[16,128,256]{2,1,0:T(8,128)(2,1)S(1)}, u32[]{:S(2)}) copy-start(bf16[16,128,256]{2,1,0:T(8,128)(2,1)S(1)} %get-tuple-element.98.piece) | copy-start | bytes 3145732
  209.8 3.1 collective-permute-start.10
  213.0 43.7 %collective-permute-start.11 = (f32[64,320]{1,0:T(8,128)S(1)}, f32[64,320]{1,0:T(8,128)S(1)}, u32[]{:S(2)}, u32[]{:S(2)}) collective-permute-start(f32[64,320]{1,0:T(8,128)S(1)} %select_add_fusion), channel_id=1, source_target_pairs={{0,8},{4,12},{8,0},{12,4},{1,9},{5,13},{9,1},{13,5},{2,10},{6,14},... | collective-permute-start | bytes 245768 | tf_op jit(solution)/shard_map/ppermute | solution.py:28
  233.6 72.6 %collective-permute-start.23 = (bf16[16,128,256]{2,1,0:T(8,128)(2,1)S(1)}, bf16[16,128,256]{2,1,0:T(8,128)(2,1)S(1)}, u32[]{:S(2)}, u32[]{:S(2)}) collective-permute-start(bf16[16,128,256]{2,1,0:T(8,128)(2,1)S(1)} %copy-done.15), channel_id=1, source_target_pairs={{0,12},{4,8},{8,4},{12,0},{1,13},{5,9},{9,5},{13,1},{2,14},{6,10},... | collective-permute-start | bytes 3145736 | tf_op jit(solution)/shard_map/ppermute | solution.py:28
  233.6 72.6 %collective-permute-start.20 = (bf16[16,128,256]{2,1,0:T(8,128)(2,1)S(1)}, bf16[16,128,256]{2,1,0:T(8,128)(2,1)S(1)}, u32[]{:S(2)}, u32[]{:S(2)}) collective-permute-start(bf16[16,128,256]{2,1,0:T(8,128)(2,1)S(1)} %get-tuple-element.104), channel_id=1, source_target_pairs={{0,12},{4,8},{8,4},{12,0},{1,13},{5,9},{9,5},{13,1},{2,14},{6,10},... | collective-permute-start | bytes 3145736 | tf_op jit(solution)/shard_map/ppermute | solution.py:28
  256.7 67.4 %collective-permute-start.21 = (bf16[16,128,256]{2,1,0:T(8,128)(2,1)S(1)}, bf16[16,128,256]{2,1,0:T(8,128)(2,1)S(1)}, u32[]{:S(2)}, u32[]{:S(2)}) collective-permute-start(bf16[16,128,256]{2,1,0:T(8,128)(2,1)S(1)} %get-tuple-element.107), channel_id=1, source_target_pairs={{0,8},{4,12},{8,0},{12,4},{1,9},{5,13},{9,1},{13,5},{2,10},{6,14},... | collective-permute-start | bytes 3145736 | tf_op jit(solution)/shard_map/ppermute | solution.py:28
  257.9 69.9 %collective-permute-start.22 = (bf16[16,128,256]{2,1,0:T(8,128)(2,1)S(1)}, bf16[16,128,256]{2,1,0:T(8,128)(2,1)S(1)}, u32[]{:S(2)}, u32[]{:S(2)}) collective-permute-start(bf16[16,128,256]{2,1,0:T(8,128)(2,1)S(1)} %get-tuple-element.108), channel_id=1, source_target_pairs={{0,4},{4,0},{8,12},{12,8},{1,5},{5,1},{9,13},{13,9},{2,6},{6,2},{1... | collective-permute-start | bytes 3145736 | tf_op jit(solution)/shard_map/ppermute | solution.py:28
  260.8 2.4 collective-permute-start.13
  263.2 96.0 %collective-permute-start.18 = (bf16[16,128,256]{2,1,0:T(8,128)(2,1)}, bf16[16,128,256]{2,1,0:T(8,128)(2,1)}, u32[]{:S(2)}, u32[]{:S(2)}) collective-permute-start(bf16[16,128,256]{2,1,0:T(8,128)(2,1)} %get-tuple-element.97), channel_id=1, source_target_pairs={{0,4},{4,0},{8,12},{12,8},{1,5},{5,1},{9,13},{13,9},{2,6},{6,2},{1... | collective-permute-start | bytes 3145736 | tf_op jit(solution)/shard_map/ppermute | solution.py:28
  306.2 55.9 %collective-permute-start.17 = (bf16[64,16,256]{2,1,0:T(8,128)(2,1)}, bf16[64,16,256]{2,1,0:T(8,128)(2,1)}, u32[]{:S(2)}, u32[]{:S(2)}) collective-permute-start(bf16[64,16,256]{2,1,0:T(8,128)(2,1)} %get-tuple-element.96), channel_id=1, source_target_pairs={{0,8},{4,12},{8,0},{12,4},{1,9},{5,13},{9,1},{13,5},{2,10},{6,14},... | collective-permute-start | bytes 1572872 | tf_op jit(solution)/shard_map/ppermute | solution.py:28
  306.2 57.7 %collective-permute-start.16 = (bf16[64,16,256]{2,1,0:T(8,128)(2,1)}, bf16[64,16,256]{2,1,0:T(8,128)(2,1)}, u32[]{:S(2)}, u32[]{:S(2)}) collective-permute-start(bf16[64,16,256]{2,1,0:T(8,128)(2,1)} %get-tuple-element.95), channel_id=1, source_target_pairs={{0,8},{4,12},{8,0},{12,4},{1,9},{5,13},{9,1},{13,5},{2,10},{6,14},... | collective-permute-start | bytes 1572872 | tf_op jit(solution)/shard_map/ppermute | solution.py:28
  324.1 41.5 %collective-permute-start.15 = (bf16[64,16,256]{2,1,0:T(8,128)(2,1)}, bf16[64,16,256]{2,1,0:T(8,128)(2,1)}, u32[]{:S(2)}, u32[]{:S(2)}) collective-permute-start(bf16[64,16,256]{2,1,0:T(8,128)(2,1)} %get-tuple-element.93), channel_id=1, source_target_pairs={{0,12},{4,8},{8,4},{12,0},{1,13},{5,9},{9,5},{13,1},{2,14},{6,10},... | collective-permute-start | bytes 1572872 | tf_op jit(solution)/shard_map/ppermute | solution.py:28
  327.8 1.0 copy-start.10
  328.8 40.9 %collective-permute-start.14 = (bf16[64,16,256]{2,1,0:T(8,128)(2,1)}, bf16[64,16,256]{2,1,0:T(8,128)(2,1)}, u32[]{:S(2)}, u32[]{:S(2)}) collective-permute-start(bf16[64,16,256]{2,1,0:T(8,128)(2,1)} %get-tuple-element.92), channel_id=1, source_target_pairs={{0,12},{4,8},{8,4},{12,0},{1,13},{5,9},{9,5},{13,1},{2,14},{6,10},... | collective-permute-start | bytes 1572872 | tf_op jit(solution)/shard_map/ppermute | solution.py:28
  328.8 1.2 copy-start.13
  337.5 2.9 copy-start.5
  348.0 1.9 copy-start.9
  349.9 1.9 copy-start.11
  355.5 1.9 copy-start.7

commit v3 on v2

--- a/solution.py
+++ b/solution.py
@@ -113,7 +113,7 @@
         ],
         scratch_shapes=[
             pltpu.VMEM((depth, width), jnp.bfloat16),
-            pltpu.VMEM((orbitals // LANES, depth * (ROWS + PAD), LANES), jnp.float32),
+            pltpu.VMEM((orbitals // LANES, (depth + 1) * (ROWS + PAD), LANES), jnp.float32),
         ],
         **settings(VMEM_MOST),
     )(walkers, kinetic_y, fields)
@@ -215,7 +215,7 @@
         ],
         out_specs=[pl.BlockSpec(out, lambda i: (0, 0, 0))] * (lines // rows),
         out_shape=[jax.ShapeDtypeStruct(out, jnp.bfloat16)] * (lines // rows),
-        scratch_shapes=[pltpu.VMEM((orbitals // LANES, part * (rows + PAD), LANES), jnp.float32)],
+        scratch_shapes=[pltpu.VMEM((orbitals // LANES, (part + 1) * (rows + PAD), LANES), jnp.float32)],
         **settings(VMEM_LEAST),
     )(piece, inverse)
 
@@ -256,7 +256,7 @@
             ]
             + [pl.BlockSpec(memory_space=pl.ANY)] * begun,
             out_specs=pl.BlockSpec((rows, part, orbitals), lambda i, where: (i, where[0], 0)),
-            scratch_shapes=[pltpu.VMEM((orbitals // LANES, part * (rows + PAD), LANES), jnp.float32)],
+            scratch_shapes=[pltpu.VMEM((orbitals // LANES, (part + 1) * (rows + PAD), LANES), jnp.float32)],
         ),
         out_shape=jax.ShapeDtypeStruct((lines, width, orbitals), jnp.bfloat16),
         input_output_aliases={3: 0} if begun else {},

time: 372 us -> 372 us (level)
  no operation moved by 1% of the time
where the time goes in v3:
time: 372 us; the launch traced here: 371 us
  waiting for transfers between devices  194 us (52%)
  Pallas kernels  128 us (34%)
  starting transfers between devices  30 us (8%)
  local copies, waits for them, and re-layouts  16.7 us (4%)
    ppermute x26, waiting for transfers between devices, trade(): lax.ppermute(piece, 'site', [(i, partner(i, step, count)) for i in range(...  194 us
    pallas_call x1, Pallas kernels, factor(): pl.pallas_call(functools.partial(factor_kernel, scale), out_shape=[jax.Sh...  38.4 us
    pallas_call x14, Pallas kernels, finish(): pl.pallas_call(last_kernel, grid_spec=pltpu.PrefetchScalarGridSpec(num_sc...  32 us
    ppermute x26, starting transfers between devices, trade(): lax.ppermute(piece, 'site', [(i, partner(i, step, count)) for i in range(...  30 us
    pallas_call x4, Pallas kernels, apply_x(): pl.pallas_call(functools.partial(x_kernel, count, group), grid=(part // g...  26.1 us
    pallas_call x2, Pallas kernels, apply_y(): pl.pallas_call(functools.partial(y_kernel, count, width // count, cuts, c...  20.3 us
    unnamed x34, local copies, waits for them, and re-layouts  11.9 us
  transfers between devices with their start and end apart: 26, of which 13 were waited for; matrix products, arithmetic and copies ran while one was open for 2% of the time, Pallas kernels for 33%

profile of v3, /device:TPU:1, one launch (start us, length us, event | category | flops | bytes accessed | tf_op | source)
XLA Modules:
  0.0 371.4 jit_solution(714407413133947256)
XLA Ops:
  0.6 3.4 shard_map.59
  4.0 2.0 collective-permute-start.1
  6.7 16.9 %shard_map.60 = (bf16[32,112,256]{2,1,0:T(8,128)(2,1)}, bf16[32,112,256]{2,1,0:T(8,128)(2,1)}, bf16[32,112,256]{2,1,0:T(8,128)(2,1)}, bf16[32,112,256]{2,1,0:T(8...) custom-call(bf16[128,256,256]{2,1,0:T(8,128)(2,1)} %bitcast.58, ...), custom_call_target="tpu_custom_call" | custom-call | flops 1000 | bytes 1000 | tf_op jit(solution)/shard_map/pallas_call | solution.py:101
  23.6 1.7 collective-permute-start.6
  25.6 5.6 %collective-permute-done.2.refs_4_ = bf16[66,16,256]{2,1,0:T(8,128)(2,1)S(1)} collective-permute-done((bf16[66,16,256]{2,1,0:T(8,128)(2,1)}, bf16[66,16,256]{2,1,0:T(8,128)(2,1)S(1)}, u32[]{:S(2)}, u32[]{:S(2)}) %collective-permute-start.2) | collective-permute-done | bytes 540704 | tf_op jit(solution)/shard_map/ppermute | solution.py:28
  39.4 29.9 %collective-permute-done.6.refs_3_ = bf16[32,112,256]{2,1,0:T(8,128)(2,1)} collective-permute-done((bf16[32,112,256]{2,1,0:T(8,128)(2,1)}, bf16[32,112,256]{2,1,0:T(8,128)(2,1)}, u32[]{:S(2)}, u32[]{:S(2)}) %collective-permute-start.6) | collective-permute-done | bytes 1835040 | tf_op jit(solution)/shard_map/ppermute | solution.py:28
  69.3 40.7 %collective-permute-done.7.refs_5_ = bf16[32,112,256]{2,1,0:T(8,128)(2,1)} collective-permute-done((bf16[32,112,256]{2,1,0:T(8,128)(2,1)}, bf16[32,112,256]{2,1,0:T(8,128)(2,1)}, u32[]{:S(2)}, u32[]{:S(2)}) %collective-permute-start.7) | collective-permute-done | bytes 1835040 | tf_op jit(solution)/shard_map/ppermute | solution.py:28
  111.5 2.2 copy-done
  115.0 6.7 %shard_map.61 = (bf16[16,128,256]{2,1,0:T(8,128)(2,1)S(1)}, bf16[16,128,256]{2,1,0:T(8,128)(2,1)}, bf16[16,128,256]{2,1,0:T(8,128)(2,1)}, bf16[16,128,256]{2,1,0:T(8,128)(2,1)}, f32[256,256]{1,0:T(8,128)S(1)}) custom-call(bf16[66,128,256]{2,1,0:T(8,128)(2,1)S(1)} %copy-done, bf16[18,128,256]{2,1,0:T(8,128)(2,1)S(1)} %copy-done.3, ...), custom_call_target="tpu_custom_call" | custom-call | flops 1000 | bytes 1000 | tf_op jit(solution)/shard_map/pallas_call | solution.py:157
  124.2 23.7 %collective-permute-done.3.refs_3_ = bf16[32,112,256]{2,1,0:T(8,128)(2,1)} collective-permute-done((bf16[32,112,256]{2,1,0:T(8,128)(2,1)}, bf16[32,112,256]{2,1,0:T(8,128)(2,1)}, u32[]{:S(2)}, u32[]{:S(2)}) %collective-permute-start.3) | collective-permute-done | bytes 1835040 | tf_op jit(solution)/shard_map/ppermute | solution.py:28
  147.9 3.7 %collective-permute-start.19 = (bf16[16,128,256]{2,1,0:T(8,128)(2,1)}, bf16[16,128,256]{2,1,0:T(8,128)(2,1)}, u32[]{:S(2)}, u32[]{:S(2)}) collective-permute-start(bf16[16,128,256]{2,1,0:T(8,128)(2,1)} %get-tuple-element.102), channel_id=1, source_target_pairs={{0,12},{4,8},{8,4},{12,0},{1,13},{5,9},{9,5},{13,1},{2,14},{6,10},... | collective-permute-start | bytes 3145736 | tf_op jit(solution)/shard_map/ppermute | solution.py:28
  151.7 6.8 %shard_map.62 = (bf16[16,128,256]{2,1,0:T(8,128)(2,1)S(1)}, bf16[16,128,256]{2,1,0:T(8,128)(2,1)}, bf16[16,128,256]{2,1,0:T(8,128)(2,1)}, bf16[16,128,256]{2,1,0:T(8,128)(2,1)S(1)}, f32[256,256]{1,0:T(8,128)S(1)}) custom-call(bf16[66,128,256]{2,1,0:T(8,128)(2,1)S(1)} %copy-done, bf16[16,128,256]{2,1,0:T(8,128)(2,1)} %collective-permute-done.8.refs_1_, ...), custom_call_target="tpu_custom_call" | custom-call | flops 1000 | bytes 1000 | tf_op jit(solution)/shard_map/pallas_call | solution.py:157
  160.5 28.2 %collective-permute-done.4.refs_5_ = bf16[32,112,256]{2,1,0:T(8,128)(2,1)} collective-permute-done((bf16[32,112,256]{2,1,0:T(8,128)(2,1)}, bf16[32,112,256]{2,1,0:T(8,128)(2,1)}, u32[]{:S(2)}, u32[]{:S(2)}) %collective-permute-start.4) | collective-permute-done | bytes 1835040 | tf_op jit(solution)/shard_map/ppermute | solution.py:28
  188.6 1.8 collective-permute-start.12
  190.4 2.2 copy-done.1
  192.7 6.1 %shard_map.63 = (bf16[16,128,256]{2,1,0:T(8,128)(2,1)S(1)}, bf16[16,128,256]{2,1,0:T(8,128)(2,1)S(1)}, bf16[16,128,256]{2,1,0:T(8,128)(2,1)S(1)}, bf16[16,128,256]{2,1,0:T(8,128)(2,1)S(1)}, f32[256,256]{1,0:T(8,128)S(1)}) custom-call(bf16[66,128,256]{2,1,0:T(8,128)(2,1)S(1)} %copy-done.1, bf16[32,128,256]{2,1,0:T(8,128)(2,1)} %collective-permute-done.refs_1_, ...), custom_call_target="tpu_custom_call" | custom-call | flops 1000 | bytes 1000 | tf_op jit(solution)/shard_map/pallas_call | solution.py:157
  199.7 6.6 %shard_map.64 = (bf16[16,128,256]{2,1,0:T(8,128)(2,1)S(1)}, bf16[16,128,256]{2,1,0:T(8,128)(2,1)}, bf16[16,128,256]{2,1,0:T(8,128)(2,1)S(1)}, bf16[16,128,256]{2,1,0:T(8,128)(2,1)S(1)}, f32[256,256]{1,0:T(8,128)S(1)}) custom-call(bf16[66,128,256]{2,1,0:T(8,128)(2,1)S(1)} %copy-done.1, bf16[32,128,256]{2,1,0:T(8,128)(2,1)} %collective-permute-done.refs_1_, ...), custom_call_target="tpu_custom_call" | custom-call | flops 1000 | bytes 1000 | tf_op jit(solution)/shard_map/pallas_call | solution.py:157
  206.3 3.5 collective-permute-done.9.piece
  209.9 2.1 collective-permute-start.10
  213.0 1.8 collective-permute-start.11
  214.9 18.7 %collective-permute-done.19.piece = bf16[16,128,256]{2,1,0:T(8,128)(2,1)} collective-permute-done((bf16[16,128,256]{2,1,0:T(8,128)(2,1)}, bf16[16,128,256]{2,1,0:T(8,128)(2,1)}, u32[]{:S(2)}, u32[]{:S(2)}) %collective-permute-start.19) | collective-permute-done | bytes 1048608 | tf_op jit(solution)/shard_map/ppermute | solution.py:28
  235.3 21.4 %collective-permute-done.11 = f32[64,320]{1,0:T(8,128)S(1)} collective-permute-done((f32[64,320]{1,0:T(8,128)S(1)}, f32[64,320]{1,0:T(8,128)S(1)}, u32[]{:S(2)}, u32[]{:S(2)}) %collective-permute-start.11) | collective-permute-done | bytes 81952 | tf_op jit(solution)/shard_map/ppermute | solution.py:28
  257.9 2.9 collective-permute-start.22
  260.9 2.3 collective-permute-done.13
  263.6 38.4 %shard_map.65 = (f32[256,256]{1,0:T(8,128)}, bf16[256,256]{1,0:T(8,128)(2,1)S(1)}) custom-call(f32[64,320]{1,0:T(8,128)S(1)} %get-tuple-element.121.first, f32[64,320]{1,0:T(8,128)S(1)} %get-tuple-element.120.second), custom_call_target="tpu_custom_call" | custom-call | flops 1000 | bytes 1000 | tf_op jit(solution)/shard_map/pallas_call | solution.py:313
  302.1 2.1 shard_map.67
  304.2 2.0 shard_map.66
  307.7 16.4 %collective-permute-done.21.piece = bf16[16,128,256]{2,1,0:T(8,128)(2,1)S(1)} collective-permute-done((bf16[16,128,256]{2,1,0:T(8,128)(2,1)S(1)}, bf16[16,128,256]{2,1,0:T(8,128)(2,1)S(1)}, u32[]{:S(2)}, u32[]{:S(2)}) %collective-permute-start.21) | collective-permute-done | bytes 1048608 | tf_op jit(solution)/shard_map/ppermute | solution.py:28
  324.1 3.7 %collective-permute-start.15 = (bf16[64,16,256]{2,1,0:T(8,128)(2,1)}, bf16[64,16,256]{2,1,0:T(8,128)(2,1)}, u32[]{:S(2)}, u32[]{:S(2)}) collective-permute-start(bf16[64,16,256]{2,1,0:T(8,128)(2,1)} %get-tuple-element.93), channel_id=1, source_target_pairs={{0,12},{4,8},{8,4},{12,0},{1,13},{5,9},{9,5},{13,1},{2,14},{6,10},... | collective-permute-start | bytes 1572872 | tf_op jit(solution)/shard_map/ppermute | solution.py:28
  330.0 1.9 shard_map.68.rest_0_
  331.9 2.8 shard_map.69.rest_0_
  334.7 2.8 shard_map.70.rest_0_
  337.6 2.9 shard_map.71.rest_0_
  340.5 1.9 shard_map.72.rest_0_
  342.4 2.8 shard_map.73.rest_0_
  345.2 2.8 shard_map.74.rest_0_
  348.0 1.9 shard_map.75.rest_0_
  349.9 1.9 shard_map.76.rest_0_
  351.8 1.9 shard_map.77.rest_0_
  353.6 1.9 shard_map.78.rest_0_
  355.5 1.9 shard_map.79.rest_0_
  357.4 1.9 shard_map.80.rest_0_
  359.3 2.8 shard_map.81.result
  362.1 1.8 shard_map.82.result
  363.9 1.8 shard_map.83.result
  365.6 1.8 shard_map.84.result
  367.4 2.3 collective-permute-done.14.piece
  369.7 1.8 shard_map.85
  (101 shorter events, 25.5 us)
Async XLA Ops:
  0.6 32.8 %copy-start.16 = (bf16[512,512]{1,0:T(8,128)(2,1)S(1)}, bf16[512,512]{1,0:T(8,128)(2,1)}, u32[]{:S(2)}) copy-start(bf16[512,512]{1,0:T(8,128)(2,1)} %param.6) | copy-start | bytes 1572868
  4.0 21.6 %collective-permute-start.1 = (bf16[66,16,256]{2,1,0:T(8,128)(2,1)}, bf16[66,16,256]{2,1,0:T(8,128)(2,1)S(1)}, u32[]{:S(2)}, u32[]{:S(2)}) collective-permute-start(bf16[66,16,256]{2,1,0:T(8,128)(2,1)} %get-tuple-element.67), channel_id=1, source_target_pairs={{0,8},{4,12},{8,0},{12,4},{1,9},{5,13},{9,1},{13,5},{2,10},{6,14},... | collective-permute-start | bytes 1622024 | tf_op jit(solution)/shard_map/ppermute | solution.py:28
  6.1 25.2 %collective-permute-start.2 = (bf16[66,16,256]{2,1,0:T(8,128)(2,1)}, bf16[66,16,256]{2,1,0:T(8,128)(2,1)S(1)}, u32[]{:S(2)}, u32[]{:S(2)}) collective-permute-start(bf16[66,16,256]{2,1,0:T(8,128)(2,1)} %get-tuple-element.68), channel_id=1, source_target_pairs={{0,12},{4,8},{8,4},{12,0},{1,13},{5,9},{9,5},{13,1},{2,14},{6,10},... | collective-permute-start | bytes 1622024 | tf_op jit(solution)/shard_map/ppermute | solution.py:28
  23.6 45.7 %collective-permute-start.6 = (bf16[32,112,256]{2,1,0:T(8,128)(2,1)}, bf16[32,112,256]{2,1,0:T(8,128)(2,1)}, u32[]{:S(2)}, u32[]{:S(2)}) collective-permute-start(bf16[32,112,256]{2,1,0:T(8,128)(2,1)} %get-tuple-element.75), channel_id=1, source_target_pairs={{0,8},{4,12},{8,0},{12,4},{1,9},{5,13},{9,1},{13,5},{2,10},{6,14},... | collective-permute-start | bytes 5505032 | tf_op jit(solution)/shard_map/ppermute | solution.py:28
  25.3 84.7 %collective-permute-start.7 = (bf16[32,112,256]{2,1,0:T(8,128)(2,1)}, bf16[32,112,256]{2,1,0:T(8,128)(2,1)}, u32[]{:S(2)}, u32[]{:S(2)}) collective-permute-start(bf16[32,112,256]{2,1,0:T(8,128)(2,1)} %get-tuple-element.76), channel_id=1, source_target_pairs={{0,12},{4,8},{8,4},{12,0},{1,13},{5,9},{9,5},{13,1},{2,14},{6,10},... | collective-permute-start | bytes 5505032 | tf_op jit(solution)/shard_map/ppermute | solution.py:28
  31.2 3.1 collective-permute-start.5
  31.6 116.3 %collective-permute-start.3 = (bf16[32,112,256]{2,1,0:T(8,128)(2,1)}, bf16[32,112,256]{2,1,0:T(8,128)(2,1)}, u32[]{:S(2)}, u32[]{:S(2)}) collective-permute-start(bf16[32,112,256]{2,1,0:T(8,128)(2,1)} %get-tuple-element.70), channel_id=1, source_target_pairs={{0,8},{4,12},{8,0},{12,4},{1,9},{5,13},{9,1},{13,5},{2,10},{6,14},... | collective-permute-start | bytes 5505032 | tf_op jit(solution)/shard_map/ppermute | solution.py:28
  33.0 155.6 %collective-permute-start.4 = (bf16[32,112,256]{2,1,0:T(8,128)(2,1)}, bf16[32,112,256]{2,1,0:T(8,128)(2,1)}, u32[]{:S(2)}, u32[]{:S(2)}) collective-permute-start(bf16[32,112,256]{2,1,0:T(8,128)(2,1)} %get-tuple-element.72), channel_id=1, source_target_pairs={{0,12},{4,8},{8,4},{12,0},{1,13},{5,9},{9,5},{13,1},{2,14},{6,10},... | collective-permute-start | bytes 5505032 | tf_op jit(solution)/shard_map/ppermute | solution.py:28
  34.3 76.6 %copy-start.2 = (bf16[18,128,256]{2,1,0:T(8,128)(2,1)}, bf16[18,128,256]{2,1,0:T(8,128)(2,1)S(1)}, u32[]{:S(2)}) copy-start(bf16[18,128,256]{2,1,0:T(8,128)(2,1)S(1)} %collective-permute-done.5.refs_1_) | copy-start | bytes 3538948
  34.3 156.1 %collective-permute-start = (bf16[32,128,256]{2,1,0:T(8,128)(2,1)}, bf16[32,128,256]{2,1,0:T(8,128)(2,1)}, u32[]{:S(2)}, u32[]{:S(2)}) collective-permute-start(bf16[32,128,256]{2,1,0:T(8,128)(2,1)} %get-tuple-element.65), channel_id=1, source_target_pairs={{0,4},{4,0},{8,12},{12,8},{1,5},{5,1},{9,13},{13,9},{2,6},{6,2},{1... | collective-permute-start | bytes 6291464 | tf_op jit(solution)/shard_map/ppermute | solution.py:28
  110.0 41.7 %collective-permute-start.8 = (bf16[16,128,256]{2,1,0:T(8,128)(2,1)}, bf16[16,128,256]{2,1,0:T(8,128)(2,1)}, u32[]{:S(2)}, u32[]{:S(2)}) collective-permute-start(bf16[16,128,256]{2,1,0:T(8,128)(2,1)} %get-tuple-element.78), channel_id=1, source_target_pairs={{0,4},{4,0},{8,12},{12,8},{1,5},{5,1},{9,13},{13,9},{2,6},{6,2},{1... | collective-permute-start | bytes 3145736 | tf_op jit(solution)/shard_map/ppermute | solution.py:28
  111.5 2.2 copy-start
  113.7 1.3 copy-start.3
  121.7 1.0 copy-start.12
  122.7 87.0 %collective-permute-start.9 = (bf16[16,128,256]{2,1,0:T(8,128)(2,1)}, bf16[16,128,256]{2,1,0:T(8,128)(2,1)}, u32[]{:S(2)}, u32[]{:S(2)}) collective-permute-start(bf16[16,128,256]{2,1,0:T(8,128)(2,1)} %get-tuple-element.86), channel_id=1, source_target_pairs={{0,8},{4,12},{8,0},{12,4},{1,9},{5,13},{9,1},{13,5},{2,10},{6,14},... | collective-permute-start | bytes 3145736 | tf_op jit(solution)/shard_map/ppermute | solution.py:28
  147.9 85.6 %collective-permute-start.19 = (bf16[16,128,256]{2,1,0:T(8,128)(2,1)}, bf16[16,128,256]{2,1,0:T(8,128)(2,1)}, u32[]{:S(2)}, u32[]{:S(2)}) collective-permute-start(bf16[16,128,256]{2,1,0:T(8,128)(2,1)} %get-tuple-element.102), channel_id=1, source_target_pairs={{0,12},{4,8},{8,4},{12,0},{1,13},{5,9},{9,5},{13,1},{2,14},{6,10},... | collective-permute-start | bytes 3145736 | tf_op jit(solution)/shard_map/ppermute | solution.py:28
  151.7 82.0 %collective-permute-start.25 = (bf16[16,128,256]{2,1,0:T(8,128)(2,1)}, bf16[16,128,256]{2,1,0:T(8,128)(2,1)}, u32[]{:S(2)}, u32[]{:S(2)}) collective-permute-start(bf16[16,128,256]{2,1,0:T(8,128)(2,1)} %get-tuple-element.116), channel_id=1, source_target_pairs={{0,4},{4,0},{8,12},{12,8},{1,5},{5,1},{9,13},{13,9},{2,6},{6,2},{1... | collective-permute-start | bytes 3145736 | tf_op jit(solution)/shard_map/ppermute | solution.py:28
  158.5 1.0 copy-start.4
  159.4 1.0 copy-start.14
  188.6 69.3 %collective-permute-start.12 = (bf16[16,128,256]{2,1,0:T(8,128)(2,1)}, bf16[16,128,256]{2,1,0:T(8,128)(2,1)}, u32[]{:S(2)}, u32[]{:S(2)}) collective-permute-start(bf16[16,128,256]{2,1,0:T(8,128)(2,1)} %get-tuple-element.89), channel_id=1, source_target_pairs={{0,8},{4,12},{8,0},{12,4},{1,9},{5,13},{9,1},{13,5},{2,10},{6,14},... | collective-permute-start | bytes 3145736 | tf_op jit(solution)/shard_map/ppermute | solution.py:28
  190.4 70.4 %collective-permute-start.24 = (bf16[16,128,256]{2,1,0:T(8,128)(2,1)}, bf16[16,128,256]{2,1,0:T(8,128)(2,1)}, u32[]{:S(2)}, u32[]{:S(2)}) collective-permute-start(bf16[16,128,256]{2,1,0:T(8,128)(2,1)} %get-tuple-element.112), channel_id=1, source_target_pairs={{0,4},{4,0},{8,12},{12,8},{1,5},{5,1},{9,13},{13,9},{2,6},{6,2},{1... | collective-permute-start | bytes 3145736 | tf_op jit(solution)/shard_map/ppermute | solution.py:28
  190.4 2.2 copy-start.1
  192.7 40.9 %copy-start.15 = (bf16[16,128,256]{2,1,0:T(8,128)(2,1)S(1)}, bf16[16,128,256]{2,1,0:T(8,128)(2,1)}, u32[]{:S(2)}) copy-start(bf16[16,128,256]{2,1,0:T(8,128)(2,1)} %copy-done.14) | copy-start | bytes 3145732
  198.7 1.0 copy-start.8
  206.3 57.4 %copy-start.6 = (bf16[16,128,256]{2,1,0:T(8,128)(2,1)}, bf16[16,128,256]{2,1,0:T(8,128)(2,1)S(1)}, u32[]{:S(2)}) copy-start(bf16[16,128,256]{2,1,0:T(8,128)(2,1)S(1)} %get-tuple-element.98.piece) | copy-start | bytes 3145732
  209.9 3.1 collective-permute-start.10
  213.0 43.7 %collective-permute-start.11 = (f32[64,320]{1,0:T(8,128)S(1)}, f32[64,320]{1,0:T(8,128)S(1)}, u32[]{:S(2)}, u32[]{:S(2)}) collective-permute-start(f32[64,320]{1,0:T(8,128)S(1)} %select_add_fusion), channel_id=1, source_target_pairs={{0,8},{4,12},{8,0},{12,4},{1,9},{5,13},{9,1},{13,5},{2,10},{6,14},... | collective-permute-start | bytes 245768 | tf_op jit(solution)/shard_map/ppermute | solution.py:28
  233.6 72.6 %collective-permute-start.23 = (bf16[16,128,256]{2,1,0:T(8,128)(2,1)S(1)}, bf16[16,128,256]{2,1,0:T(8,128)(2,1)S(1)}, u32[]{:S(2)}, u32[]{:S(2)}) collective-permute-start(bf16[16,128,256]{2,1,0:T(8,128)(2,1)S(1)} %copy-done.15), channel_id=1, source_target_pairs={{0,12},{4,8},{8,4},{12,0},{1,13},{5,9},{9,5},{13,1},{2,14},{6,10},... | collective-permute-start | bytes 3145736 | tf_op jit(solution)/shard_map/ppermute | solution.py:28
  233.6 72.6 %collective-permute-start.20 = (bf16[16,128,256]{2,1,0:T(8,128)(2,1)S(1)}, bf16[16,128,256]{2,1,0:T(8,128)(2,1)S(1)}, u32[]{:S(2)}, u32[]{:S(2)}) collective-permute-start(bf16[16,128,256]{2,1,0:T(8,128)(2,1)S(1)} %get-tuple-element.104), channel_id=1, source_target_pairs={{0,12},{4,8},{8,4},{12,0},{1,13},{5,9},{9,5},{13,1},{2,14},{6,10},... | collective-permute-start | bytes 3145736 | tf_op jit(solution)/shard_map/ppermute | solution.py:28
  256.7 67.4 %collective-permute-start.21 = (bf16[16,128,256]{2,1,0:T(8,128)(2,1)S(1)}, bf16[16,128,256]{2,1,0:T(8,128)(2,1)S(1)}, u32[]{:S(2)}, u32[]{:S(2)}) collective-permute-start(bf16[16,128,256]{2,1,0:T(8,128)(2,1)S(1)} %get-tuple-element.107), channel_id=1, source_target_pairs={{0,8},{4,12},{8,0},{12,4},{1,9},{5,13},{9,1},{13,5},{2,10},{6,14},... | collective-permute-start | bytes 3145736 | tf_op jit(solution)/shard_map/ppermute | solution.py:28
  257.9 69.9 %collective-permute-start.22 = (bf16[16,128,256]{2,1,0:T(8,128)(2,1)S(1)}, bf16[16,128,256]{2,1,0:T(8,128)(2,1)S(1)}, u32[]{:S(2)}, u32[]{:S(2)}) collective-permute-start(bf16[16,128,256]{2,1,0:T(8,128)(2,1)S(1)} %get-tuple-element.108), channel_id=1, source_target_pairs={{0,4},{4,0},{8,12},{12,8},{1,5},{5,1},{9,13},{13,9},{2,6},{6,2},{1... | collective-permute-start | bytes 3145736 | tf_op jit(solution)/shard_map/ppermute | solution.py:28
  260.8 2.4 collective-permute-start.13
  263.2 96.0 %collective-permute-start.18 = (bf16[16,128,256]{2,1,0:T(8,128)(2,1)}, bf16[16,128,256]{2,1,0:T(8,128)(2,1)}, u32[]{:S(2)}, u32[]{:S(2)}) collective-permute-start(bf16[16,128,256]{2,1,0:T(8,128)(2,1)} %get-tuple-element.97), channel_id=1, source_target_pairs={{0,4},{4,0},{8,12},{12,8},{1,5},{5,1},{9,13},{13,9},{2,6},{6,2},{1... | collective-permute-start | bytes 3145736 | tf_op jit(solution)/shard_map/ppermute | solution.py:28
  306.2 55.9 %collective-permute-start.17 = (bf16[64,16,256]{2,1,0:T(8,128)(2,1)}, bf16[64,16,256]{2,1,0:T(8,128)(2,1)}, u32[]{:S(2)}, u32[]{:S(2)}) collective-permute-start(bf16[64,16,256]{2,1,0:T(8,128)(2,1)} %get-tuple-element.96), channel_id=1, source_target_pairs={{0,8},{4,12},{8,0},{12,4},{1,9},{5,13},{9,1},{13,5},{2,10},{6,14},... | collective-permute-start | bytes 1572872 | tf_op jit(solution)/shard_map/ppermute | solution.py:28
  306.2 57.6 %collective-permute-start.16 = (bf16[64,16,256]{2,1,0:T(8,128)(2,1)}, bf16[64,16,256]{2,1,0:T(8,128)(2,1)}, u32[]{:S(2)}, u32[]{:S(2)}) collective-permute-start(bf16[64,16,256]{2,1,0:T(8,128)(2,1)} %get-tuple-element.95), channel_id=1, source_target_pairs={{0,8},{4,12},{8,0},{12,4},{1,9},{5,13},{9,1},{13,5},{2,10},{6,14},... | collective-permute-start | bytes 1572872 | tf_op jit(solution)/shard_map/ppermute | solution.py:28
  324.1 41.5 %collective-permute-start.15 = (bf16[64,16,256]{2,1,0:T(8,128)(2,1)}, bf16[64,16,256]{2,1,0:T(8,128)(2,1)}, u32[]{:S(2)}, u32[]{:S(2)}) collective-permute-start(bf16[64,16,256]{2,1,0:T(8,128)(2,1)} %get-tuple-element.93), channel_id=1, source_target_pairs={{0,12},{4,8},{8,4},{12,0},{1,13},{5,9},{9,5},{13,1},{2,14},{6,10},... | collective-permute-start | bytes 1572872 | tf_op jit(solution)/shard_map/ppermute | solution.py:28
  327.8 1.0 copy-start.10
  328.8 40.9 %collective-permute-start.14 = (bf16[64,16,256]{2,1,0:T(8,128)(2,1)}, bf16[64,16,256]{2,1,0:T(8,128)(2,1)}, u32[]{:S(2)}, u32[]{:S(2)}) collective-permute-start(bf16[64,16,256]{2,1,0:T(8,128)(2,1)} %get-tuple-element.92), channel_id=1, source_target_pairs={{0,12},{4,8},{8,4},{12,0},{1,13},{5,9},{9,5},{13,1},{2,14},{6,10},... | collective-permute-start | bytes 1572872 | tf_op jit(solution)/shard_map/ppermute | solution.py:28
  328.8 1.2 copy-start.13
  337.6 2.9 copy-start.5
  348.0 1.9 copy-start.9
  349.9 1.9 copy-start.11
  355.5 1.9 copy-start.7

commit v4 on v3

--- a/solution.py
+++ b/solution.py
@@ -10,6 +10,7 @@
 ROWS = 16
 LANES = 128
 PAD = 8
+PARTS = 2
 BLOCK = 64
 VMEM_LIMIT = 20 * 1024 * 1024
 VMEM_LEAST = 8 * 1024 * 1024
@@ -198,8 +199,24 @@
         )
 
 
-def place_kernel(where, piece, result, out):
-    out[...] = piece[...]
+def place_kernel(begin, step, count, chunk, chunks, piece, result, out, held, got, put):
+    lines, part, _ = piece.shape
+    rows = lines // got.shape[0]
+    where = partner(lax.axis_index("site"), step, count) * chunks + chunk
+    y = pl.ds(pl.multiple_of(where * part, ROWS), part)
+    reads, writes = [], []
+    for k in range(got.shape[0]):
+        x = pl.ds(k * rows, rows)
+        reads.append(pltpu.make_async_copy(piece.at[x], held.at[x], got.at[k]))
+        target = out.at[pl.ds(begin + k * rows, rows), y, :]
+        writes.append(pltpu.make_async_copy(held.at[x], target, put.at[k]))
+    for read in reads:
+        read.start()
+    for read, write in zip(reads, writes):
+        read.wait()
+        write.start()
+    for write in writes:
+        write.wait()
 
 
 def split(piece, inverse):
@@ -220,25 +237,22 @@
     )(piece, inverse)
 
 
-def place(result, piece, begin, where):
-    lines, part, orbitals = piece.shape
-    rows = lines // 2 if begin % (lines // 2) == 0 else lines
-    block = (rows, part, orbitals)
+def place(result, piece, begin, step, count, chunk, chunks):
+    parts = PARTS if piece.shape[0] % PARTS == 0 else 1
+    anywhere = pl.BlockSpec(memory_space=pl.ANY)
     return pl.pallas_call(
-        place_kernel,
-        grid_spec=pltpu.PrefetchScalarGridSpec(
-            num_scalar_prefetch=1,
-            grid=(lines // rows,),
-            in_specs=[
-                pl.BlockSpec(block, lambda i, where: (i, 0, 0)),
-                pl.BlockSpec(memory_space=pl.ANY),
-            ],
-            out_specs=pl.BlockSpec(block, lambda i, where: (begin // rows + i, where[0], 0)),
-        ),
+        functools.partial(place_kernel, begin, step, count, chunk, chunks),
+        in_specs=[anywhere, anywhere],
+        out_specs=anywhere,
         out_shape=jax.ShapeDtypeStruct(result.shape, result.dtype),
-        input_output_aliases={2: 0},
+        scratch_shapes=[
+            pltpu.VMEM(piece.shape, jnp.bfloat16),
+            pltpu.SemaphoreType.DMA((parts,)),
+            pltpu.SemaphoreType.DMA((parts,)),
+        ],
+        input_output_aliases={1: 0},
         **settings(VMEM_LEAST),
-    )(where.reshape(1), piece, result)
+    )(piece, result)
 
 
 def finish(result, piece, inverse, place, width):
@@ -449,8 +463,8 @@
         if isinstance(back[-1][s], list):
             pieces = back[-1][s]
             for k, piece in enumerate(pieces):
-                where = order[s] * chunks + chunks - 1
-                result = place(result, piece, k * piece.shape[0], where)
+                at = k * piece.shape[0]
+                result = place(result, piece, at, s, count, chunks - 1, chunks)
     return result, lower
 
 

time: 372 us -> 373 us (level)
  no operation moved by 1% of the time
where the time goes in v4:
time: 373 us; the launch traced here: 372 us
  waiting for transfers between devices  194 us (52%)
  Pallas kernels  128 us (34%)
  starting transfers between devices  30 us (8%)
  local copies, waits for them, and re-layouts  16.6 us (4%)
    ppermute x26, waiting for transfers between devices, trade(): lax.ppermute(piece, 'site', [(i, partner(i, step, count)) for i in range(...  194 us
    pallas_call x1, Pallas kernels, factor(): pl.pallas_call(functools.partial(factor_kernel, scale), out_shape=[jax.Sh...  38.4 us
    pallas_call x14, Pallas kernels, finish(): pl.pallas_call(last_kernel, grid_spec=pltpu.PrefetchScalarGridSpec(num_sc...  32 us
    ppermute x26, starting transfers between devices, trade(): lax.ppermute(piece, 'site', [(i, partner(i, step, count)) for i in range(...  30 us
    pallas_call x4, Pallas kernels, apply_x(): pl.pallas_call(functools.partial(x_kernel, count, group), grid=(part // g...  26.1 us
    pallas_call x2, Pallas kernels, apply_y(): pl.pallas_call(functools.partial(y_kernel, count, width // count, cuts, c...  20.3 us
    unnamed x34, local copies, waits for them, and re-layouts  11.8 us
  transfers between devices with their start and end apart: 26, of which 13 were waited for; matrix products, arithmetic and copies ran while one was open for 2% of the time, Pallas kernels for 33%

profile of v4, /device:TPU:1, one launch (start us, length us, event | category | flops | bytes accessed | tf_op | source)
XLA Modules:
  0.0 371.6 jit_solution(2954459049355858257)
XLA Ops:
  0.6 3.4 shard_map.59
  4.0 2.0 collective-permute-start.1
  6.7 16.9 %shard_map.60 = (bf16[32,112,256]{2,1,0:T(8,128)(2,1)}, bf16[32,112,256]{2,1,0:T(8,128)(2,1)}, bf16[32,112,256]{2,1,0:T(8,128)(2,1)}, bf16[32,112,256]{2,1,0:T(8...) custom-call(bf16[128,256,256]{2,1,0:T(8,128)(2,1)} %bitcast.56, ...), custom_call_target="tpu_custom_call" | custom-call | flops 1000 | bytes 1000 | tf_op jit(solution)/shard_map/pallas_call | solution.py:102
  23.6 1.7 collective-permute-start.6
  25.6 5.6 %collective-permute-done.2.refs_4_ = bf16[66,16,256]{2,1,0:T(8,128)(2,1)S(1)} collective-permute-done((bf16[66,16,256]{2,1,0:T(8,128)(2,1)}, bf16[66,16,256]{2,1,0:T(8,128)(2,1)S(1)}, u32[]{:S(2)}, u32[]{:S(2)}) %collective-permute-start.2) | collective-permute-done | bytes 540704 | tf_op jit(solution)/shard_map/ppermute | solution.py:29
  39.4 29.9 %collective-permute-done.6.refs_3_ = bf16[32,112,256]{2,1,0:T(8,128)(2,1)} collective-permute-done((bf16[32,112,256]{2,1,0:T(8,128)(2,1)}, bf16[32,112,256]{2,1,0:T(8,128)(2,1)}, u32[]{:S(2)}, u32[]{:S(2)}) %collective-permute-start.6) | collective-permute-done | bytes 1835040 | tf_op jit(solution)/shard_map/ppermute | solution.py:29
  69.3 40.7 %collective-permute-done.7.refs_5_ = bf16[32,112,256]{2,1,0:T(8,128)(2,1)} collective-permute-done((bf16[32,112,256]{2,1,0:T(8,128)(2,1)}, bf16[32,112,256]{2,1,0:T(8,128)(2,1)}, u32[]{:S(2)}, u32[]{:S(2)}) %collective-permute-start.7) | collective-permute-done | bytes 1835040 | tf_op jit(solution)/shard_map/ppermute | solution.py:29
  111.5 2.2 copy-done
  115.0 6.7 %shard_map.61 = (bf16[16,128,256]{2,1,0:T(8,128)(2,1)S(1)}, bf16[16,128,256]{2,1,0:T(8,128)(2,1)}, bf16[16,128,256]{2,1,0:T(8,128)(2,1)}, bf16[16,128,256]{2,1,0:T(8,128)(2,1)}, f32[256,256]{1,0:T(8,128)S(1)}) custom-call(bf16[66,128,256]{2,1,0:T(8,128)(2,1)S(1)} %copy-done, bf16[18,128,256]{2,1,0:T(8,128)(2,1)S(1)} %copy-done.3, ...), custom_call_target="tpu_custom_call" | custom-call | flops 1000 | bytes 1000 | tf_op jit(solution)/shard_map/pallas_call | solution.py:158
  124.2 23.7 %collective-permute-done.3.refs_3_ = bf16[32,112,256]{2,1,0:T(8,128)(2,1)} collective-permute-done((bf16[32,112,256]{2,1,0:T(8,128)(2,1)}, bf16[32,112,256]{2,1,0:T(8,128)(2,1)}, u32[]{:S(2)}, u32[]{:S(2)}) %collective-permute-start.3) | collective-permute-done | bytes 1835040 | tf_op jit(solution)/shard_map/ppermute | solution.py:29
  148.0 3.7 %collective-permute-start.19 = (bf16[16,128,256]{2,1,0:T(8,128)(2,1)}, bf16[16,128,256]{2,1,0:T(8,128)(2,1)}, u32[]{:S(2)}, u32[]{:S(2)}) collective-permute-start(bf16[16,128,256]{2,1,0:T(8,128)(2,1)} %get-tuple-element.102), channel_id=1, source_target_pairs={{0,12},{4,8},{8,4},{12,0},{1,13},{5,9},{9,5},{13,1},{2,14},{6,10},... | collective-permute-start | bytes 3145736 | tf_op jit(solution)/shard_map/ppermute | solution.py:29
  151.7 6.7 %shard_map.62 = (bf16[16,128,256]{2,1,0:T(8,128)(2,1)S(1)}, bf16[16,128,256]{2,1,0:T(8,128)(2,1)}, bf16[16,128,256]{2,1,0:T(8,128)(2,1)}, bf16[16,128,256]{2,1,0:T(8,128)(2,1)S(1)}, f32[256,256]{1,0:T(8,128)S(1)}) custom-call(bf16[66,128,256]{2,1,0:T(8,128)(2,1)S(1)} %copy-done, bf16[16,128,256]{2,1,0:T(8,128)(2,1)} %collective-permute-done.8.refs_1_, ...), custom_call_target="tpu_custom_call" | custom-call | flops 1000 | bytes 1000 | tf_op jit(solution)/shard_map/pallas_call | solution.py:158
  160.4 28.3 %collective-permute-done.4.refs_5_ = bf16[32,112,256]{2,1,0:T(8,128)(2,1)} collective-permute-done((bf16[32,112,256]{2,1,0:T(8,128)(2,1)}, bf16[32,112,256]{2,1,0:T(8,128)(2,1)}, u32[]{:S(2)}, u32[]{:S(2)}) %collective-permute-start.4) | collective-permute-done | bytes 1835040 | tf_op jit(solution)/shard_map/ppermute | solution.py:29
  188.6 1.8 collective-permute-start.12
  190.4 2.2 copy-done.1
  192.7 6.1 %shard_map.63 = (bf16[16,128,256]{2,1,0:T(8,128)(2,1)S(1)}, bf16[16,128,256]{2,1,0:T(8,128)(2,1)S(1)}, bf16[16,128,256]{2,1,0:T(8,128)(2,1)S(1)}, bf16[16,128,256]{2,1,0:T(8,128)(2,1)S(1)}, f32[256,256]{1,0:T(8,128)S(1)}) custom-call(bf16[66,128,256]{2,1,0:T(8,128)(2,1)S(1)} %copy-done.1, bf16[32,128,256]{2,1,0:T(8,128)(2,1)} %collective-permute-done.refs_1_, ...), custom_call_target="tpu_custom_call" | custom-call | flops 1000 | bytes 1000 | tf_op jit(solution)/shard_map/pallas_call | solution.py:158
  199.7 6.5 %shard_map.64 = (bf16[16,128,256]{2,1,0:T(8,128)(2,1)S(1)}, bf16[16,128,256]{2,1,0:T(8,128)(2,1)}, bf16[16,128,256]{2,1,0:T(8,128)(2,1)S(1)}, bf16[16,128,256]{2,1,0:T(8,128)(2,1)S(1)}, f32[256,256]{1,0:T(8,128)S(1)}) custom-call(bf16[66,128,256]{2,1,0:T(8,128)(2,1)S(1)} %copy-done.1, bf16[32,128,256]{2,1,0:T(8,128)(2,1)} %collective-permute-done.refs_1_, ...), custom_call_target="tpu_custom_call" | custom-call | flops 1000 | bytes 1000 | tf_op jit(solution)/shard_map/pallas_call | solution.py:158
  206.2 3.5 collective-permute-done.9.piece
  209.9 2.1 collective-permute-start.10
  213.0 1.8 collective-permute-start.11
  214.9 18.7 %collective-permute-done.19.piece = bf16[16,128,256]{2,1,0:T(8,128)(2,1)} collective-permute-done((bf16[16,128,256]{2,1,0:T(8,128)(2,1)}, bf16[16,128,256]{2,1,0:T(8,128)(2,1)}, u32[]{:S(2)}, u32[]{:S(2)}) %collective-permute-start.19) | collective-permute-done | bytes 1048608 | tf_op jit(solution)/shard_map/ppermute | solution.py:29
  235.3 21.4 %collective-permute-done.11 = f32[64,320]{1,0:T(8,128)S(1)} collective-permute-done((f32[64,320]{1,0:T(8,128)S(1)}, f32[64,320]{1,0:T(8,128)S(1)}, u32[]{:S(2)}, u32[]{:S(2)}) %collective-permute-start.11) | collective-permute-done | bytes 81952 | tf_op jit(solution)/shard_map/ppermute | solution.py:29
  257.9 2.9 collective-permute-start.22
  260.9 2.3 collective-permute-done.13
  263.6 38.4 %shard_map.65 = (f32[256,256]{1,0:T(8,128)}, bf16[256,256]{1,0:T(8,128)(2,1)S(1)}) custom-call(f32[64,320]{1,0:T(8,128)S(1)} %get-tuple-element.121.first, f32[64,320]{1,0:T(8,128)S(1)} %get-tuple-element.120.second), custom_call_target="tpu_custom_call" | custom-call | flops 1000 | bytes 1000 | tf_op jit(solution)/shard_map/pallas_call | solution.py:327
  302.1 2.0 shard_map.67
  304.1 2.1 shard_map.66
  307.7 16.4 %collective-permute-done.21.piece = bf16[16,128,256]{2,1,0:T(8,128)(2,1)S(1)} collective-permute-done((bf16[16,128,256]{2,1,0:T(8,128)(2,1)S(1)}, bf16[16,128,256]{2,1,0:T(8,128)(2,1)S(1)}, u32[]{:S(2)}, u32[]{:S(2)}) %collective-permute-start.21) | collective-permute-done | bytes 1048608 | tf_op jit(solution)/shard_map/ppermute | solution.py:29
  324.1 3.7 %collective-permute-start.15 = (bf16[64,16,256]{2,1,0:T(8,128)(2,1)}, bf16[64,16,256]{2,1,0:T(8,128)(2,1)}, u32[]{:S(2)}, u32[]{:S(2)}) collective-permute-start(bf16[64,16,256]{2,1,0:T(8,128)(2,1)} %get-tuple-element.93), channel_id=1, source_target_pairs={{0,12},{4,8},{8,4},{12,0},{1,13},{5,9},{9,5},{13,1},{2,14},{6,10},... | collective-permute-start | bytes 1572872 | tf_op jit(solution)/shard_map/ppermute | solution.py:29
  330.0 1.9 shard_map.68.rest_0_
  331.9 2.8 shard_map.69.rest_0_
  334.7 2.8 shard_map.70.rest_0_
  337.6 2.9 shard_map.71.rest_0_
  340.5 1.9 shard_map.72.rest_0_
  342.4 2.8 shard_map.73.rest_0_
  345.2 2.8 shard_map.74.rest_0_
  348.0 1.9 shard_map.75.rest_0_
  349.9 1.9 shard_map.76.rest_0_
  351.8 1.9 shard_map.77.rest_0_
  353.6 1.9 shard_map.78.rest_0_
  355.5 1.9 shard_map.79.rest_0_
  357.4 1.9 shard_map.80.rest_0_
  359.2 2.8 shard_map.81.result
  362.1 1.8 shard_map.82.result
  363.9 1.8 shard_map.83.result
  365.7 1.8 shard_map.84.result
  367.5 2.2 collective-permute-done.14.piece
  369.7 1.8 shard_map.85
  (101 shorter events, 25.4 us)
Async XLA Ops:
  0.6 32.8 %copy-start.16 = (bf16[512,512]{1,0:T(8,128)(2,1)S(1)}, bf16[512,512]{1,0:T(8,128)(2,1)}, u32[]{:S(2)}) copy-start(bf16[512,512]{1,0:T(8,128)(2,1)} %param.6) | copy-start | bytes 1572868
  4.0 21.6 %collective-permute-start.1 = (bf16[66,16,256]{2,1,0:T(8,128)(2,1)}, bf16[66,16,256]{2,1,0:T(8,128)(2,1)S(1)}, u32[]{:S(2)}, u32[]{:S(2)}) collective-permute-start(bf16[66,16,256]{2,1,0:T(8,128)(2,1)} %get-tuple-element.67), channel_id=1, source_target_pairs={{0,8},{4,12},{8,0},{12,4},{1,9},{5,13},{9,1},{13,5},{2,10},{6,14},... | collective-permute-start | bytes 1622024 | tf_op jit(solution)/shard_map/ppermute | solution.py:29
  6.1 25.2 %collective-permute-start.2 = (bf16[66,16,256]{2,1,0:T(8,128)(2,1)}, bf16[66,16,256]{2,1,0:T(8,128)(2,1)S(1)}, u32[]{:S(2)}, u32[]{:S(2)}) collective-permute-start(bf16[66,16,256]{2,1,0:T(8,128)(2,1)} %get-tuple-element.68), channel_id=1, source_target_pairs={{0,12},{4,8},{8,4},{12,0},{1,13},{5,9},{9,5},{13,1},{2,14},{6,10},... | collective-permute-start | bytes 1622024 | tf_op jit(solution)/shard_map/ppermute | solution.py:29
  23.6 45.7 %collective-permute-start.6 = (bf16[32,112,256]{2,1,0:T(8,128)(2,1)}, bf16[32,112,256]{2,1,0:T(8,128)(2,1)}, u32[]{:S(2)}, u32[]{:S(2)}) collective-permute-start(bf16[32,112,256]{2,1,0:T(8,128)(2,1)} %get-tuple-element.75), channel_id=1, source_target_pairs={{0,8},{4,12},{8,0},{12,4},{1,9},{5,13},{9,1},{13,5},{2,10},{6,14},... | collective-permute-start | bytes 5505032 | tf_op jit(solution)/shard_map/ppermute | solution.py:29
  25.3 84.7 %collective-permute-start.7 = (bf16[32,112,256]{2,1,0:T(8,128)(2,1)}, bf16[32,112,256]{2,1,0:T(8,128)(2,1)}, u32[]{:S(2)}, u32[]{:S(2)}) collective-permute-start(bf16[32,112,256]{2,1,0:T(8,128)(2,1)} %get-tuple-element.76), channel_id=1, source_target_pairs={{0,12},{4,8},{8,4},{12,0},{1,13},{5,9},{9,5},{13,1},{2,14},{6,10},... | collective-permute-start | bytes 5505032 | tf_op jit(solution)/shard_map/ppermute | solution.py:29
  31.2 3.1 collective-permute-start.5
  31.6 116.3 %collective-permute-start.3 = (bf16[32,112,256]{2,1,0:T(8,128)(2,1)}, bf16[32,112,256]{2,1,0:T(8,128)(2,1)}, u32[]{:S(2)}, u32[]{:S(2)}) collective-permute-start(bf16[32,112,256]{2,1,0:T(8,128)(2,1)} %get-tuple-element.70), channel_id=1, source_target_pairs={{0,8},{4,12},{8,0},{12,4},{1,9},{5,13},{9,1},{13,5},{2,10},{6,14},... | collective-permute-start | bytes 5505032 | tf_op jit(solution)/shard_map/ppermute | solution.py:29
  33.0 155.6 %collective-permute-start.4 = (bf16[32,112,256]{2,1,0:T(8,128)(2,1)}, bf16[32,112,256]{2,1,0:T(8,128)(2,1)}, u32[]{:S(2)}, u32[]{:S(2)}) collective-permute-start(bf16[32,112,256]{2,1,0:T(8,128)(2,1)} %get-tuple-element.72), channel_id=1, source_target_pairs={{0,12},{4,8},{8,4},{12,0},{1,13},{5,9},{9,5},{13,1},{2,14},{6,10},... | collective-permute-start | bytes 5505032 | tf_op jit(solution)/shard_map/ppermute | solution.py:29
  34.3 76.6 %copy-start.2 = (bf16[18,128,256]{2,1,0:T(8,128)(2,1)}, bf16[18,128,256]{2,1,0:T(8,128)(2,1)S(1)}, u32[]{:S(2)}) copy-start(bf16[18,128,256]{2,1,0:T(8,128)(2,1)S(1)} %collective-permute-done.5.refs_1_) | copy-start | bytes 3538948
  34.3 156.1 %collective-permute-start = (bf16[32,128,256]{2,1,0:T(8,128)(2,1)}, bf16[32,128,256]{2,1,0:T(8,128)(2,1)}, u32[]{:S(2)}, u32[]{:S(2)}) collective-permute-start(bf16[32,128,256]{2,1,0:T(8,128)(2,1)} %get-tuple-element.65), channel_id=1, source_target_pairs={{0,4},{4,0},{8,12},{12,8},{1,5},{5,1},{9,13},{13,9},{2,6},{6,2},{1... | collective-permute-start | bytes 6291464 | tf_op jit(solution)/shard_map/ppermute | solution.py:29
  110.0 41.7 %collective-permute-start.8 = (bf16[16,128,256]{2,1,0:T(8,128)(2,1)}, bf16[16,128,256]{2,1,0:T(8,128)(2,1)}, u32[]{:S(2)}, u32[]{:S(2)}) collective-permute-start(bf16[16,128,256]{2,1,0:T(8,128)(2,1)} %get-tuple-element.78), channel_id=1, source_target_pairs={{0,4},{4,0},{8,12},{12,8},{1,5},{5,1},{9,13},{13,9},{2,6},{6,2},{1... | collective-permute-start | bytes 3145736 | tf_op jit(solution)/shard_map/ppermute | solution.py:29
  111.5 2.2 copy-start
  113.7 1.3 copy-start.3
  121.7 1.0 copy-start.12
  122.7 87.0 %collective-permute-start.9 = (bf16[16,128,256]{2,1,0:T(8,128)(2,1)}, bf16[16,128,256]{2,1,0:T(8,128)(2,1)}, u32[]{:S(2)}, u32[]{:S(2)}) collective-permute-start(bf16[16,128,256]{2,1,0:T(8,128)(2,1)} %get-tuple-element.86), channel_id=1, source_target_pairs={{0,8},{4,12},{8,0},{12,4},{1,9},{5,13},{9,1},{13,5},{2,10},{6,14},... | collective-permute-start | bytes 3145736 | tf_op jit(solution)/shard_map/ppermute | solution.py:29
  148.0 85.6 %collective-permute-start.19 = (bf16[16,128,256]{2,1,0:T(8,128)(2,1)}, bf16[16,128,256]{2,1,0:T(8,128)(2,1)}, u32[]{:S(2)}, u32[]{:S(2)}) collective-permute-start(bf16[16,128,256]{2,1,0:T(8,128)(2,1)} %get-tuple-element.102), channel_id=1, source_target_pairs={{0,12},{4,8},{8,4},{12,0},{1,13},{5,9},{9,5},{13,1},{2,14},{6,10},... | collective-permute-start | bytes 3145736 | tf_op jit(solution)/shard_map/ppermute | solution.py:29
  151.7 82.0 %collective-permute-start.25 = (bf16[16,128,256]{2,1,0:T(8,128)(2,1)}, bf16[16,128,256]{2,1,0:T(8,128)(2,1)}, u32[]{:S(2)}, u32[]{:S(2)}) collective-permute-start(bf16[16,128,256]{2,1,0:T(8,128)(2,1)} %get-tuple-element.116), channel_id=1, source_target_pairs={{0,4},{4,0},{8,12},{12,8},{1,5},{5,1},{9,13},{13,9},{2,6},{6,2},{1... | collective-permute-start | bytes 3145736 | tf_op jit(solution)/shard_map/ppermute | solution.py:29
  158.4 1.0 copy-start.4
  159.4 1.0 copy-start.14
  188.6 69.3 %collective-permute-start.12 = (bf16[16,128,256]{2,1,0:T(8,128)(2,1)}, bf16[16,128,256]{2,1,0:T(8,128)(2,1)}, u32[]{:S(2)}, u32[]{:S(2)}) collective-permute-start(bf16[16,128,256]{2,1,0:T(8,128)(2,1)} %get-tuple-element.89), channel_id=1, source_target_pairs={{0,8},{4,12},{8,0},{12,4},{1,9},{5,13},{9,1},{13,5},{2,10},{6,14},... | collective-permute-start | bytes 3145736 | tf_op jit(solution)/shard_map/ppermute | solution.py:29
  190.4 70.4 %collective-permute-start.24 = (bf16[16,128,256]{2,1,0:T(8,128)(2,1)}, bf16[16,128,256]{2,1,0:T(8,128)(2,1)}, u32[]{:S(2)}, u32[]{:S(2)}) collective-permute-start(bf16[16,128,256]{2,1,0:T(8,128)(2,1)} %get-tuple-element.112), channel_id=1, source_target_pairs={{0,4},{4,0},{8,12},{12,8},{1,5},{5,1},{9,13},{13,9},{2,6},{6,2},{1... | collective-permute-start | bytes 3145736 | tf_op jit(solution)/shard_map/ppermute | solution.py:29
  190.4 2.2 copy-start.1
  192.7 40.9 %copy-start.15 = (bf16[16,128,256]{2,1,0:T(8,128)(2,1)S(1)}, bf16[16,128,256]{2,1,0:T(8,128)(2,1)}, u32[]{:S(2)}) copy-start(bf16[16,128,256]{2,1,0:T(8,128)(2,1)} %copy-done.14) | copy-start | bytes 3145732
  198.7 1.0 copy-start.8
  206.2 57.4 %copy-start.6 = (bf16[16,128,256]{2,1,0:T(8,128)(2,1)}, bf16[16,128,256]{2,1,0:T(8,128)(2,1)S(1)}, u32[]{:S(2)}) copy-start(bf16[16,128,256]{2,1,0:T(8,128)(2,1)S(1)} %get-tuple-element.98.piece) | copy-start | bytes 3145732
  209.9 3.1 collective-permute-start.10
  213.0 43.7 %collective-permute-start.11 = (f32[64,320]{1,0:T(8,128)S(1)}, f32[64,320]{1,0:T(8,128)S(1)}, u32[]{:S(2)}, u32[]{:S(2)}) collective-permute-start(f32[64,320]{1,0:T(8,128)S(1)} %select_add_fusion), channel_id=1, source_target_pairs={{0,8},{4,12},{8,0},{12,4},{1,9},{5,13},{9,1},{13,5},{2,10},{6,14},... | collective-permute-start | bytes 245768 | tf_op jit(solution)/shard_map/ppermute | solution.py:29
  233.6 72.6 %collective-permute-start.23 = (bf16[16,128,256]{2,1,0:T(8,128)(2,1)S(1)}, bf16[16,128,256]{2,1,0:T(8,128)(2,1)S(1)}, u32[]{:S(2)}, u32[]{:S(2)}) collective-permute-start(bf16[16,128,256]{2,1,0:T(8,128)(2,1)S(1)} %copy-done.15), channel_id=1, source_target_pairs={{0,12},{4,8},{8,4},{12,0},{1,13},{5,9},{9,5},{13,1},{2,14},{6,10},... | collective-permute-start | bytes 3145736 | tf_op jit(solution)/shard_map/ppermute | solution.py:29
  233.6 72.6 %collective-permute-start.20 = (bf16[16,128,256]{2,1,0:T(8,128)(2,1)S(1)}, bf16[16,128,256]{2,1,0:T(8,128)(2,1)S(1)}, u32[]{:S(2)}, u32[]{:S(2)}) collective-permute-start(bf16[16,128,256]{2,1,0:T(8,128)(2,1)S(1)} %get-tuple-element.104), channel_id=1, source_target_pairs={{0,12},{4,8},{8,4},{12,0},{1,13},{5,9},{9,5},{13,1},{2,14},{6,10},... | collective-permute-start | bytes 3145736 | tf_op jit(solution)/shard_map/ppermute | solution.py:29
  256.7 67.4 %collective-permute-start.21 = (bf16[16,128,256]{2,1,0:T(8,128)(2,1)S(1)}, bf16[16,128,256]{2,1,0:T(8,128)(2,1)S(1)}, u32[]{:S(2)}, u32[]{:S(2)}) collective-permute-start(bf16[16,128,256]{2,1,0:T(8,128)(2,1)S(1)} %get-tuple-element.107), channel_id=1, source_target_pairs={{0,8},{4,12},{8,0},{12,4},{1,9},{5,13},{9,1},{13,5},{2,10},{6,14},... | collective-permute-start | bytes 3145736 | tf_op jit(solution)/shard_map/ppermute | solution.py:29
  257.9 69.9 %collective-permute-start.22 = (bf16[16,128,256]{2,1,0:T(8,128)(2,1)S(1)}, bf16[16,128,256]{2,1,0:T(8,128)(2,1)S(1)}, u32[]{:S(2)}, u32[]{:S(2)}) collective-permute-start(bf16[16,128,256]{2,1,0:T(8,128)(2,1)S(1)} %get-tuple-element.108), channel_id=1, source_target_pairs={{0,4},{4,0},{8,12},{12,8},{1,5},{5,1},{9,13},{13,9},{2,6},{6,2},{1... | collective-permute-start | bytes 3145736 | tf_op jit(solution)/shard_map/ppermute | solution.py:29
  260.8 2.4 collective-permute-start.13
  263.2 96.0 %collective-permute-start.18 = (bf16[16,128,256]{2,1,0:T(8,128)(2,1)}, bf16[16,128,256]{2,1,0:T(8,128)(2,1)}, u32[]{:S(2)}, u32[]{:S(2)}) collective-permute-start(bf16[16,128,256]{2,1,0:T(8,128)(2,1)} %get-tuple-element.97), channel_id=1, source_target_pairs={{0,4},{4,0},{8,12},{12,8},{1,5},{5,1},{9,13},{13,9},{2,6},{6,2},{1... | collective-permute-start | bytes 3145736 | tf_op jit(solution)/shard_map/ppermute | solution.py:29
  306.2 57.6 %collective-permute-start.16 = (bf16[64,16,256]{2,1,0:T(8,128)(2,1)}, bf16[64,16,256]{2,1,0:T(8,128)(2,1)}, u32[]{:S(2)}, u32[]{:S(2)}) collective-permute-start(bf16[64,16,256]{2,1,0:T(8,128)(2,1)} %get-tuple-element.95), channel_id=1, source_target_pairs={{0,8},{4,12},{8,0},{12,4},{1,9},{5,13},{9,1},{13,5},{2,10},{6,14},... | collective-permute-start | bytes 1572872 | tf_op jit(solution)/shard_map/ppermute | solution.py:29
  306.2 55.8 %collective-permute-start.17 = (bf16[64,16,256]{2,1,0:T(8,128)(2,1)}, bf16[64,16,256]{2,1,0:T(8,128)(2,1)}, u32[]{:S(2)}, u32[]{:S(2)}) collective-permute-start(bf16[64,16,256]{2,1,0:T(8,128)(2,1)} %get-tuple-element.96), channel_id=1, source_target_pairs={{0,8},{4,12},{8,0},{12,4},{1,9},{5,13},{9,1},{13,5},{2,10},{6,14},... | collective-permute-start | bytes 1572872 | tf_op jit(solution)/shard_map/ppermute | solution.py:29
  324.1 41.6 %collective-permute-start.15 = (bf16[64,16,256]{2,1,0:T(8,128)(2,1)}, bf16[64,16,256]{2,1,0:T(8,128)(2,1)}, u32[]{:S(2)}, u32[]{:S(2)}) collective-permute-start(bf16[64,16,256]{2,1,0:T(8,128)(2,1)} %get-tuple-element.93), channel_id=1, source_target_pairs={{0,12},{4,8},{8,4},{12,0},{1,13},{5,9},{9,5},{13,1},{2,14},{6,10},... | collective-permute-start | bytes 1572872 | tf_op jit(solution)/shard_map/ppermute | solution.py:29
  327.8 1.0 copy-start.10
  328.8 40.9 %collective-permute-start.14 = (bf16[64,16,256]{2,1,0:T(8,128)(2,1)}, bf16[64,16,256]{2,1,0:T(8,128)(2,1)}, u32[]{:S(2)}, u32[]{:S(2)}) collective-permute-start(bf16[64,16,256]{2,1,0:T(8,128)(2,1)} %get-tuple-element.92), channel_id=1, source_target_pairs={{0,12},{4,8},{8,4},{12,0},{1,13},{5,9},{9,5},{13,1},{2,14},{6,10},... | collective-permute-start | bytes 1572872 | tf_op jit(solution)/shard_map/ppermute | solution.py:29
  328.8 1.2 copy-start.13
  337.6 2.9 copy-start.5
  348.0 1.9 copy-start.9
  349.9 1.9 copy-start.11
  355.5 1.9 copy-start.7

commit v5 on v3

--- a/solution.py
+++ b/solution.py
@@ -10,6 +10,7 @@
 ROWS = 16
 LANES = 128
 PAD = 8
+STEP = 8
 BLOCK = 64
 VMEM_LIMIT = 20 * 1024 * 1024
 VMEM_LEAST = 8 * 1024 * 1024
@@ -39,10 +40,21 @@
     )
 
 
-def y_kernel(count, band, cuts, carry, walkers, kinetic, *rest):
-    outs, own, turned = rest[-2 - len(cuts) : -2], rest[-2], rest[-1]
+def y_kernel(count, band, cuts, carry, walkers, kinetic, fields, *rest):
+    outs, own, turned = rest[: len(cuts)], rest[len(cuts)], rest[len(cuts) + 1]
     me = lax.axis_index("site")
     depth = own.shape[0]
+    copies = []
+    if len(rest) > len(cuts) + 2:
+        lines, matrix, values, sems = rest[len(cuts) + 2 :]
+        pairs = [(kinetic, matrix), (fields, values)]
+        for r in range(0, ROWS, STEP):
+            pairs.append((walkers.at[pl.ds(r, STEP)], lines.at[pl.ds(r, STEP)]))
+        copies = [pltpu.make_async_copy(*pair, sems.at[k]) for k, pair in enumerate(pairs)]
+        for copy in copies:
+            copy.start()
+        copies[0].wait()
+        walkers, kinetic, fields = lines, matrix, values
 
     @pl.when(pl.program_id(0) == 0)
     def _():
@@ -53,10 +65,14 @@
             row += size
 
     for r in range(ROWS):
+        if copies and r % STEP == 0:
+            copies[2 + r // STEP].wait()
         line = jnp.dot(own[...], walkers[r], preferred_element_type=jnp.float32)
         for h in range(turned.shape[0]):
             part = line[:, h * LANES : (h + 1) * LANES]
             turned[h, pl.ds(r, depth, stride=ROWS + PAD), :] = part
+    if copies:
+        copies[1].wait()
     row = 0
     for (s, first, size), out in zip(cuts, outs):
         for h in range(turned.shape[0]):
@@ -69,9 +85,9 @@
             begin = partner(me, s, count) * band
             tile = pl.multiple_of(begin // window * window, LANES)
             across = out.shape[2] // band
-            for line in range(0, rest[0].shape[0], ROWS):
+            for line in range(0, fields.shape[0], ROWS):
                 place, part = size + line // ROWS // across, line // ROWS % across
-                values = rest[0][pl.ds(line, ROWS), pl.ds(tile, window)].astype(jnp.float32)
+                values = fields[pl.ds(line, ROWS), pl.ds(tile, window)].astype(jnp.float32)
                 own_values = values[:, :band]
                 for k in range(band, window, band):
                     own_values = jnp.where(begin - tile == k, values[:, k : k + band], own_values)
@@ -101,7 +117,9 @@
     return pl.pallas_call(
         functools.partial(y_kernel, count, width // count, cuts, carry),
         grid=(used // ROWS,),
-        in_specs=[
+        in_specs=[pl.BlockSpec(memory_space=pl.ANY)] * 3
+        if used == ROWS
+        else [
             pl.BlockSpec((ROWS, width, orbitals), lambda i: (i, 0, 0)),
             pl.BlockSpec((width, width), lambda i: (0, 0)),
             pl.BlockSpec((lines, width), lambda i: (0, 0)),
@@ -114,7 +132,17 @@
         scratch_shapes=[
             pltpu.VMEM((depth, width), jnp.bfloat16),
             pltpu.VMEM((orbitals // LANES, (depth + 1) * (ROWS + PAD), LANES), jnp.float32),
-        ],
+        ]
+        + (
+            [
+                pltpu.VMEM((ROWS, width, orbitals), jnp.bfloat16),
+                pltpu.VMEM((width, width), jnp.bfloat16),
+                pltpu.VMEM((lines, width), jnp.bfloat16),
+                pltpu.SemaphoreType.DMA((2 + ROWS // STEP,)),
+            ]
+            if used == ROWS
+            else []
+        ),
         **settings(VMEM_MOST),
     )(walkers, kinetic_y, fields)
 

time: 372 us -> 372 us (level)
  no operation moved by 1% of the time
where the time goes in v5:
time: 372 us; the launch traced here: 371 us
  waiting for transfers between devices  194 us (52%)
  Pallas kernels  128 us (34%)
  starting transfers between devices  30 us (8%)
  local copies, waits for them, and re-layouts  16.7 us (4%)
    ppermute x26, waiting for transfers between devices, trade(): lax.ppermute(piece, 'site', [(i, partner(i, step, count)) for i in range(...  194 us
    pallas_call x1, Pallas kernels, factor(): pl.pallas_call(functools.partial(factor_kernel, scale), out_shape=[jax.Sh...  38.4 us
    pallas_call x14, Pallas kernels, finish(): pl.pallas_call(last_kernel, grid_spec=pltpu.PrefetchScalarGridSpec(num_sc...  32.1 us
    ppermute x26, starting transfers between devices, trade(): lax.ppermute(piece, 'site', [(i, partner(i, step, count)) for i in range(...  30 us
    pallas_call x4, Pallas kernels, apply_x(): pl.pallas_call(functools.partial(x_kernel, count, group), grid=(part // g...  26.1 us
    pallas_call x2, Pallas kernels, apply_y(): pl.pallas_call(functools.partial(y_kernel, count, width // count, cuts, c...  20.2 us
    unnamed x34, local copies, waits for them, and re-layouts  11.9 us
  transfers between devices with their start and end apart: 26, of which 13 were waited for; matrix products, arithmetic and copies ran while one was open for 2% of the time, Pallas kernels for 33%

profile of v5, /device:TPU:1, one launch (start us, length us, event | category | flops | bytes accessed | tf_op | source)
XLA Modules:
  0.0 371.4 jit_solution(10842207094186014882)
XLA Ops:
  0.6 3.3 shard_map.59
  3.9 2.1 collective-permute-start.1
  6.7 16.9 %shard_map.60 = (bf16[32,112,256]{2,1,0:T(8,128)(2,1)}, bf16[32,112,256]{2,1,0:T(8,128)(2,1)}, bf16[32,112,256]{2,1,0:T(8,128)(2,1)}, bf16[32,112,256]{2,1,0:T(8...) custom-call(bf16[128,256,256]{2,1,0:T(8,128)(2,1)} %bitcast.58, ...), custom_call_target="tpu_custom_call" | custom-call | flops 1000 | bytes 1000 | tf_op jit(solution)/shard_map/pallas_call | solution.py:117
  25.5 5.7 %collective-permute-done.2.refs_4_ = bf16[66,16,256]{2,1,0:T(8,128)(2,1)S(1)} collective-permute-done((bf16[66,16,256]{2,1,0:T(8,128)(2,1)}, bf16[66,16,256]{2,1,0:T(8,128)(2,1)S(1)}, u32[]{:S(2)}, u32[]{:S(2)}) %collective-permute-start.2) | collective-permute-done | bytes 540704 | tf_op jit(solution)/shard_map/ppermute | solution.py:29
  39.3 29.9 %collective-permute-done.6.refs_3_ = bf16[32,112,256]{2,1,0:T(8,128)(2,1)} collective-permute-done((bf16[32,112,256]{2,1,0:T(8,128)(2,1)}, bf16[32,112,256]{2,1,0:T(8,128)(2,1)}, u32[]{:S(2)}, u32[]{:S(2)}) %collective-permute-start.6) | collective-permute-done | bytes 1835040 | tf_op jit(solution)/shard_map/ppermute | solution.py:29
  69.3 40.7 %collective-permute-done.7.refs_5_ = bf16[32,112,256]{2,1,0:T(8,128)(2,1)} collective-permute-done((bf16[32,112,256]{2,1,0:T(8,128)(2,1)}, bf16[32,112,256]{2,1,0:T(8,128)(2,1)}, u32[]{:S(2)}, u32[]{:S(2)}) %collective-permute-start.7) | collective-permute-done | bytes 1835040 | tf_op jit(solution)/shard_map/ppermute | solution.py:29
  111.5 2.2 copy-done
  114.9 6.7 %shard_map.61 = (bf16[16,128,256]{2,1,0:T(8,128)(2,1)S(1)}, bf16[16,128,256]{2,1,0:T(8,128)(2,1)}, bf16[16,128,256]{2,1,0:T(8,128)(2,1)}, bf16[16,128,256]{2,1,0:T(8,128)(2,1)}, f32[256,256]{1,0:T(8,128)S(1)}) custom-call(bf16[66,128,256]{2,1,0:T(8,128)(2,1)S(1)} %copy-done, bf16[18,128,256]{2,1,0:T(8,128)(2,1)S(1)} %copy-done.3, ...), custom_call_target="tpu_custom_call" | custom-call | flops 1000 | bytes 1000 | tf_op jit(solution)/shard_map/pallas_call | solution.py:185
  124.2 23.7 %collective-permute-done.3.refs_3_ = bf16[32,112,256]{2,1,0:T(8,128)(2,1)} collective-permute-done((bf16[32,112,256]{2,1,0:T(8,128)(2,1)}, bf16[32,112,256]{2,1,0:T(8,128)(2,1)}, u32[]{:S(2)}, u32[]{:S(2)}) %collective-permute-start.3) | collective-permute-done | bytes 1835040 | tf_op jit(solution)/shard_map/ppermute | solution.py:29
  147.9 3.7 %collective-permute-start.19 = (bf16[16,128,256]{2,1,0:T(8,128)(2,1)}, bf16[16,128,256]{2,1,0:T(8,128)(2,1)}, u32[]{:S(2)}, u32[]{:S(2)}) collective-permute-start(bf16[16,128,256]{2,1,0:T(8,128)(2,1)} %get-tuple-element.102), channel_id=1, source_target_pairs={{0,12},{4,8},{8,4},{12,0},{1,13},{5,9},{9,5},{13,1},{2,14},{6,10},... | collective-permute-start | bytes 3145736 | tf_op jit(solution)/shard_map/ppermute | solution.py:29
  151.6 6.8 %shard_map.62 = (bf16[16,128,256]{2,1,0:T(8,128)(2,1)S(1)}, bf16[16,128,256]{2,1,0:T(8,128)(2,1)}, bf16[16,128,256]{2,1,0:T(8,128)(2,1)}, bf16[16,128,256]{2,1,0:T(8,128)(2,1)S(1)}, f32[256,256]{1,0:T(8,128)S(1)}) custom-call(bf16[66,128,256]{2,1,0:T(8,128)(2,1)S(1)} %copy-done, bf16[16,128,256]{2,1,0:T(8,128)(2,1)} %collective-permute-done.8.refs_1_, ...), custom_call_target="tpu_custom_call" | custom-call | flops 1000 | bytes 1000 | tf_op jit(solution)/shard_map/pallas_call | solution.py:185
  160.4 28.2 %collective-permute-done.4.refs_5_ = bf16[32,112,256]{2,1,0:T(8,128)(2,1)} collective-permute-done((bf16[32,112,256]{2,1,0:T(8,128)(2,1)}, bf16[32,112,256]{2,1,0:T(8,128)(2,1)}, u32[]{:S(2)}, u32[]{:S(2)}) %collective-permute-start.4) | collective-permute-done | bytes 1835040 | tf_op jit(solution)/shard_map/ppermute | solution.py:29
  188.6 1.8 collective-permute-start.12
  190.4 2.2 copy-done.1
  192.6 6.1 %shard_map.63 = (bf16[16,128,256]{2,1,0:T(8,128)(2,1)S(1)}, bf16[16,128,256]{2,1,0:T(8,128)(2,1)S(1)}, bf16[16,128,256]{2,1,0:T(8,128)(2,1)S(1)}, bf16[16,128,256]{2,1,0:T(8,128)(2,1)S(1)}, f32[256,256]{1,0:T(8,128)S(1)}) custom-call(bf16[66,128,256]{2,1,0:T(8,128)(2,1)S(1)} %copy-done.1, bf16[32,128,256]{2,1,0:T(8,128)(2,1)} %collective-permute-done.refs_1_, ...), custom_call_target="tpu_custom_call" | custom-call | flops 1000 | bytes 1000 | tf_op jit(solution)/shard_map/pallas_call | solution.py:185
  199.7 6.6 %shard_map.64 = (bf16[16,128,256]{2,1,0:T(8,128)(2,1)S(1)}, bf16[16,128,256]{2,1,0:T(8,128)(2,1)}, bf16[16,128,256]{2,1,0:T(8,128)(2,1)S(1)}, bf16[16,128,256]{2,1,0:T(8,128)(2,1)S(1)}, f32[256,256]{1,0:T(8,128)S(1)}) custom-call(bf16[66,128,256]{2,1,0:T(8,128)(2,1)S(1)} %copy-done.1, bf16[32,128,256]{2,1,0:T(8,128)(2,1)} %collective-permute-done.refs_1_, ...), custom_call_target="tpu_custom_call" | custom-call | flops 1000 | bytes 1000 | tf_op jit(solution)/shard_map/pallas_call | solution.py:185
  206.2 3.5 collective-permute-done.9.piece
  209.8 2.1 collective-permute-start.10
  213.0 1.8 collective-permute-start.11
  214.8 18.7 %collective-permute-done.19.piece = bf16[16,128,256]{2,1,0:T(8,128)(2,1)} collective-permute-done((bf16[16,128,256]{2,1,0:T(8,128)(2,1)}, bf16[16,128,256]{2,1,0:T(8,128)(2,1)}, u32[]{:S(2)}, u32[]{:S(2)}) %collective-permute-start.19) | collective-permute-done | bytes 1048608 | tf_op jit(solution)/shard_map/ppermute | solution.py:29
  233.6 1.7 collective-permute-start.20
  235.3 21.4 %collective-permute-done.11 = f32[64,320]{1,0:T(8,128)S(1)} collective-permute-done((f32[64,320]{1,0:T(8,128)S(1)}, f32[64,320]{1,0:T(8,128)S(1)}, u32[]{:S(2)}, u32[]{:S(2)}) %collective-permute-start.11) | collective-permute-done | bytes 81952 | tf_op jit(solution)/shard_map/ppermute | solution.py:29
  257.9 2.9 collective-permute-start.22
  260.9 2.3 collective-permute-done.13
  263.6 38.4 %shard_map.65 = (f32[256,256]{1,0:T(8,128)}, bf16[256,256]{1,0:T(8,128)(2,1)S(1)}) custom-call(f32[64,320]{1,0:T(8,128)S(1)} %get-tuple-element.121.first, f32[64,320]{1,0:T(8,128)S(1)} %get-tuple-element.120.second), custom_call_target="tpu_custom_call" | custom-call | flops 1000 | bytes 1000 | tf_op jit(solution)/shard_map/pallas_call | solution.py:341
  302.0 2.1 shard_map.67
  304.1 2.0 shard_map.66
  307.6 16.4 %collective-permute-done.21.piece = bf16[16,128,256]{2,1,0:T(8,128)(2,1)S(1)} collective-permute-done((bf16[16,128,256]{2,1,0:T(8,128)(2,1)S(1)}, bf16[16,128,256]{2,1,0:T(8,128)(2,1)S(1)}, u32[]{:S(2)}, u32[]{:S(2)}) %collective-permute-start.21) | collective-permute-done | bytes 1048608 | tf_op jit(solution)/shard_map/ppermute | solution.py:29
  324.1 3.7 %collective-permute-start.15 = (bf16[64,16,256]{2,1,0:T(8,128)(2,1)}, bf16[64,16,256]{2,1,0:T(8,128)(2,1)}, u32[]{:S(2)}, u32[]{:S(2)}) collective-permute-start(bf16[64,16,256]{2,1,0:T(8,128)(2,1)} %get-tuple-element.93), channel_id=1, source_target_pairs={{0,12},{4,8},{8,4},{12,0},{1,13},{5,9},{9,5},{13,1},{2,14},{6,10},... | collective-permute-start | bytes 1572872 | tf_op jit(solution)/shard_map/ppermute | solution.py:29
  330.0 1.9 shard_map.68.rest_0_
  331.9 2.8 shard_map.69.rest_0_
  334.7 2.8 shard_map.70.rest_0_
  337.5 2.9 shard_map.71.rest_0_
  340.5 1.9 shard_map.72.rest_0_
  342.3 2.8 shard_map.73.rest_0_
  345.1 2.8 shard_map.74.rest_0_
  348.0 1.9 shard_map.75.rest_0_
  349.9 1.9 shard_map.76.rest_0_
  351.7 1.9 shard_map.77.rest_0_
  353.6 1.9 shard_map.78.rest_0_
  355.5 1.9 shard_map.79.rest_0_
  357.4 1.9 shard_map.80.rest_0_
  359.2 2.8 shard_map.81.result
  362.1 1.8 shard_map.82.result
  363.8 1.8 shard_map.83.result
  365.6 1.8 shard_map.84.result
  367.4 2.3 collective-permute-done.14.piece
  369.6 1.8 shard_map.85
  (101 shorter events, 25.5 us)
Async XLA Ops:
  0.6 32.8 %copy-start.16 = (bf16[512,512]{1,0:T(8,128)(2,1)S(1)}, bf16[512,512]{1,0:T(8,128)(2,1)}, u32[]{:S(2)}) copy-start(bf16[512,512]{1,0:T(8,128)(2,1)} %param.6) | copy-start | bytes 1572868
  3.9 21.6 %collective-permute-start.1 = (bf16[66,16,256]{2,1,0:T(8,128)(2,1)}, bf16[66,16,256]{2,1,0:T(8,128)(2,1)S(1)}, u32[]{:S(2)}, u32[]{:S(2)}) collective-permute-start(bf16[66,16,256]{2,1,0:T(8,128)(2,1)} %get-tuple-element.67), channel_id=1, source_target_pairs={{0,8},{4,12},{8,0},{12,4},{1,9},{5,13},{9,1},{13,5},{2,10},{6,14},... | collective-permute-start | bytes 1622024 | tf_op jit(solution)/shard_map/ppermute | solution.py:29
  6.0 25.2 %collective-permute-start.2 = (bf16[66,16,256]{2,1,0:T(8,128)(2,1)}, bf16[66,16,256]{2,1,0:T(8,128)(2,1)S(1)}, u32[]{:S(2)}, u32[]{:S(2)}) collective-permute-start(bf16[66,16,256]{2,1,0:T(8,128)(2,1)} %get-tuple-element.68), channel_id=1, source_target_pairs={{0,12},{4,8},{8,4},{12,0},{1,13},{5,9},{9,5},{13,1},{2,14},{6,10},... | collective-permute-start | bytes 1622024 | tf_op jit(solution)/shard_map/ppermute | solution.py:29
  23.6 45.7 %collective-permute-start.6 = (bf16[32,112,256]{2,1,0:T(8,128)(2,1)}, bf16[32,112,256]{2,1,0:T(8,128)(2,1)}, u32[]{:S(2)}, u32[]{:S(2)}) collective-permute-start(bf16[32,112,256]{2,1,0:T(8,128)(2,1)} %get-tuple-element.75), channel_id=1, source_target_pairs={{0,8},{4,12},{8,0},{12,4},{1,9},{5,13},{9,1},{13,5},{2,10},{6,14},... | collective-permute-start | bytes 5505032 | tf_op jit(solution)/shard_map/ppermute | solution.py:29
  25.2 84.7 %collective-permute-start.7 = (bf16[32,112,256]{2,1,0:T(8,128)(2,1)}, bf16[32,112,256]{2,1,0:T(8,128)(2,1)}, u32[]{:S(2)}, u32[]{:S(2)}) collective-permute-start(bf16[32,112,256]{2,1,0:T(8,128)(2,1)} %get-tuple-element.76), channel_id=1, source_target_pairs={{0,12},{4,8},{8,4},{12,0},{1,13},{5,9},{9,5},{13,1},{2,14},{6,10},... | collective-permute-start | bytes 5505032 | tf_op jit(solution)/shard_map/ppermute | solution.py:29
  31.2 3.1 collective-permute-start.5
  31.6 116.3 %collective-permute-start.3 = (bf16[32,112,256]{2,1,0:T(8,128)(2,1)}, bf16[32,112,256]{2,1,0:T(8,128)(2,1)}, u32[]{:S(2)}, u32[]{:S(2)}) collective-permute-start(bf16[32,112,256]{2,1,0:T(8,128)(2,1)} %get-tuple-element.70), channel_id=1, source_target_pairs={{0,8},{4,12},{8,0},{12,4},{1,9},{5,13},{9,1},{13,5},{2,10},{6,14},... | collective-permute-start | bytes 5505032 | tf_op jit(solution)/shard_map/ppermute | solution.py:29
  33.0 155.6 %collective-permute-start.4 = (bf16[32,112,256]{2,1,0:T(8,128)(2,1)}, bf16[32,112,256]{2,1,0:T(8,128)(2,1)}, u32[]{:S(2)}, u32[]{:S(2)}) collective-permute-start(bf16[32,112,256]{2,1,0:T(8,128)(2,1)} %get-tuple-element.72), channel_id=1, source_target_pairs={{0,12},{4,8},{8,4},{12,0},{1,13},{5,9},{9,5},{13,1},{2,14},{6,10},... | collective-permute-start | bytes 5505032 | tf_op jit(solution)/shard_map/ppermute | solution.py:29
  34.3 76.6 %copy-start.2 = (bf16[18,128,256]{2,1,0:T(8,128)(2,1)}, bf16[18,128,256]{2,1,0:T(8,128)(2,1)S(1)}, u32[]{:S(2)}) copy-start(bf16[18,128,256]{2,1,0:T(8,128)(2,1)S(1)} %collective-permute-done.5.refs_1_) | copy-start | bytes 3538948
  34.3 156.1 %collective-permute-start = (bf16[32,128,256]{2,1,0:T(8,128)(2,1)}, bf16[32,128,256]{2,1,0:T(8,128)(2,1)}, u32[]{:S(2)}, u32[]{:S(2)}) collective-permute-start(bf16[32,128,256]{2,1,0:T(8,128)(2,1)} %get-tuple-element.65), channel_id=1, source_target_pairs={{0,4},{4,0},{8,12},{12,8},{1,5},{5,1},{9,13},{13,9},{2,6},{6,2},{1... | collective-permute-start | bytes 6291464 | tf_op jit(solution)/shard_map/ppermute | solution.py:29
  109.9 41.7 %collective-permute-start.8 = (bf16[16,128,256]{2,1,0:T(8,128)(2,1)}, bf16[16,128,256]{2,1,0:T(8,128)(2,1)}, u32[]{:S(2)}, u32[]{:S(2)}) collective-permute-start(bf16[16,128,256]{2,1,0:T(8,128)(2,1)} %get-tuple-element.78), channel_id=1, source_target_pairs={{0,4},{4,0},{8,12},{12,8},{1,5},{5,1},{9,13},{13,9},{2,6},{6,2},{1... | collective-permute-start | bytes 3145736 | tf_op jit(solution)/shard_map/ppermute | solution.py:29
  111.4 2.2 copy-start
  113.7 1.3 copy-start.3
  121.7 1.0 copy-start.12
  122.7 87.0 %collective-permute-start.9 = (bf16[16,128,256]{2,1,0:T(8,128)(2,1)}, bf16[16,128,256]{2,1,0:T(8,128)(2,1)}, u32[]{:S(2)}, u32[]{:S(2)}) collective-permute-start(bf16[16,128,256]{2,1,0:T(8,128)(2,1)} %get-tuple-element.86), channel_id=1, source_target_pairs={{0,8},{4,12},{8,0},{12,4},{1,9},{5,13},{9,1},{13,5},{2,10},{6,14},... | collective-permute-start | bytes 3145736 | tf_op jit(solution)/shard_map/ppermute | solution.py:29
  147.9 85.6 %collective-permute-start.19 = (bf16[16,128,256]{2,1,0:T(8,128)(2,1)}, bf16[16,128,256]{2,1,0:T(8,128)(2,1)}, u32[]{:S(2)}, u32[]{:S(2)}) collective-permute-start(bf16[16,128,256]{2,1,0:T(8,128)(2,1)} %get-tuple-element.102), channel_id=1, source_target_pairs={{0,12},{4,8},{8,4},{12,0},{1,13},{5,9},{9,5},{13,1},{2,14},{6,10},... | collective-permute-start | bytes 3145736 | tf_op jit(solution)/shard_map/ppermute | solution.py:29
  151.6 82.0 %collective-permute-start.25 = (bf16[16,128,256]{2,1,0:T(8,128)(2,1)}, bf16[16,128,256]{2,1,0:T(8,128)(2,1)}, u32[]{:S(2)}, u32[]{:S(2)}) collective-permute-start(bf16[16,128,256]{2,1,0:T(8,128)(2,1)} %get-tuple-element.116), channel_id=1, source_target_pairs={{0,4},{4,0},{8,12},{12,8},{1,5},{5,1},{9,13},{13,9},{2,6},{6,2},{1... | collective-permute-start | bytes 3145736 | tf_op jit(solution)/shard_map/ppermute | solution.py:29
  158.4 1.0 copy-start.4
  159.4 1.0 copy-start.14
  188.6 69.3 %collective-permute-start.12 = (bf16[16,128,256]{2,1,0:T(8,128)(2,1)}, bf16[16,128,256]{2,1,0:T(8,128)(2,1)}, u32[]{:S(2)}, u32[]{:S(2)}) collective-permute-start(bf16[16,128,256]{2,1,0:T(8,128)(2,1)} %get-tuple-element.89), channel_id=1, source_target_pairs={{0,8},{4,12},{8,0},{12,4},{1,9},{5,13},{9,1},{13,5},{2,10},{6,14},... | collective-permute-start | bytes 3145736 | tf_op jit(solution)/shard_map/ppermute | solution.py:29
  190.4 70.4 %collective-permute-start.24 = (bf16[16,128,256]{2,1,0:T(8,128)(2,1)}, bf16[16,128,256]{2,1,0:T(8,128)(2,1)}, u32[]{:S(2)}, u32[]{:S(2)}) collective-permute-start(bf16[16,128,256]{2,1,0:T(8,128)(2,1)} %get-tuple-element.112), channel_id=1, source_target_pairs={{0,4},{4,0},{8,12},{12,8},{1,5},{5,1},{9,13},{13,9},{2,6},{6,2},{1... | collective-permute-start | bytes 3145736 | tf_op jit(solution)/shard_map/ppermute | solution.py:29
  190.4 2.2 copy-start.1
  192.6 40.9 %copy-start.15 = (bf16[16,128,256]{2,1,0:T(8,128)(2,1)S(1)}, bf16[16,128,256]{2,1,0:T(8,128)(2,1)}, u32[]{:S(2)}) copy-start(bf16[16,128,256]{2,1,0:T(8,128)(2,1)} %copy-done.14) | copy-start | bytes 3145732
  198.7 1.0 copy-start.8
  206.2 57.4 %copy-start.6 = (bf16[16,128,256]{2,1,0:T(8,128)(2,1)}, bf16[16,128,256]{2,1,0:T(8,128)(2,1)S(1)}, u32[]{:S(2)}) copy-start(bf16[16,128,256]{2,1,0:T(8,128)(2,1)S(1)} %get-tuple-element.98.piece) | copy-start | bytes 3145732
  209.8 3.1 collective-permute-start.10
  213.0 43.7 %collective-permute-start.11 = (f32[64,320]{1,0:T(8,128)S(1)}, f32[64,320]{1,0:T(8,128)S(1)}, u32[]{:S(2)}, u32[]{:S(2)}) collective-permute-start(f32[64,320]{1,0:T(8,128)S(1)} %select_add_fusion), channel_id=1, source_target_pairs={{0,8},{4,12},{8,0},{12,4},{1,9},{5,13},{9,1},{13,5},{2,10},{6,14},... | collective-permute-start | bytes 245768 | tf_op jit(solution)/shard_map/ppermute | solution.py:29
  233.5 72.6 %collective-permute-start.23 = (bf16[16,128,256]{2,1,0:T(8,128)(2,1)S(1)}, bf16[16,128,256]{2,1,0:T(8,128)(2,1)S(1)}, u32[]{:S(2)}, u32[]{:S(2)}) collective-permute-start(bf16[16,128,256]{2,1,0:T(8,128)(2,1)S(1)} %copy-done.15), channel_id=1, source_target_pairs={{0,12},{4,8},{8,4},{12,0},{1,13},{5,9},{9,5},{13,1},{2,14},{6,10},... | collective-permute-start | bytes 3145736 | tf_op jit(solution)/shard_map/ppermute | solution.py:29
  233.6 72.5 %collective-permute-start.20 = (bf16[16,128,256]{2,1,0:T(8,128)(2,1)S(1)}, bf16[16,128,256]{2,1,0:T(8,128)(2,1)S(1)}, u32[]{:S(2)}, u32[]{:S(2)}) collective-permute-start(bf16[16,128,256]{2,1,0:T(8,128)(2,1)S(1)} %get-tuple-element.104), channel_id=1, source_target_pairs={{0,12},{4,8},{8,4},{12,0},{1,13},{5,9},{9,5},{13,1},{2,14},{6,10},... | collective-permute-start | bytes 3145736 | tf_op jit(solution)/shard_map/ppermute | solution.py:29
  256.6 67.4 %collective-permute-start.21 = (bf16[16,128,256]{2,1,0:T(8,128)(2,1)S(1)}, bf16[16,128,256]{2,1,0:T(8,128)(2,1)S(1)}, u32[]{:S(2)}, u32[]{:S(2)}) collective-permute-start(bf16[16,128,256]{2,1,0:T(8,128)(2,1)S(1)} %get-tuple-element.107), channel_id=1, source_target_pairs={{0,8},{4,12},{8,0},{12,4},{1,9},{5,13},{9,1},{13,5},{2,10},{6,14},... | collective-permute-start | bytes 3145736 | tf_op jit(solution)/shard_map/ppermute | solution.py:29
  257.9 69.9 %collective-permute-start.22 = (bf16[16,128,256]{2,1,0:T(8,128)(2,1)S(1)}, bf16[16,128,256]{2,1,0:T(8,128)(2,1)S(1)}, u32[]{:S(2)}, u32[]{:S(2)}) collective-permute-start(bf16[16,128,256]{2,1,0:T(8,128)(2,1)S(1)} %get-tuple-element.108), channel_id=1, source_target_pairs={{0,4},{4,0},{8,12},{12,8},{1,5},{5,1},{9,13},{13,9},{2,6},{6,2},{1... | collective-permute-start | bytes 3145736 | tf_op jit(solution)/shard_map/ppermute | solution.py:29
  260.8 2.4 collective-permute-start.13
  263.2 96.0 %collective-permute-start.18 = (bf16[16,128,256]{2,1,0:T(8,128)(2,1)}, bf16[16,128,256]{2,1,0:T(8,128)(2,1)}, u32[]{:S(2)}, u32[]{:S(2)}) collective-permute-start(bf16[16,128,256]{2,1,0:T(8,128)(2,1)} %get-tuple-element.97), channel_id=1, source_target_pairs={{0,4},{4,0},{8,12},{12,8},{1,5},{5,1},{9,13},{13,9},{2,6},{6,2},{1... | collective-permute-start | bytes 3145736 | tf_op jit(solution)/shard_map/ppermute | solution.py:29
  306.1 55.9 %collective-permute-start.17 = (bf16[64,16,256]{2,1,0:T(8,128)(2,1)}, bf16[64,16,256]{2,1,0:T(8,128)(2,1)}, u32[]{:S(2)}, u32[]{:S(2)}) collective-permute-start(bf16[64,16,256]{2,1,0:T(8,128)(2,1)} %get-tuple-element.96), channel_id=1, source_target_pairs={{0,8},{4,12},{8,0},{12,4},{1,9},{5,13},{9,1},{13,5},{2,10},{6,14},... | collective-permute-start | bytes 1572872 | tf_op jit(solution)/shard_map/ppermute | solution.py:29
  306.2 57.7 %collective-permute-start.16 = (bf16[64,16,256]{2,1,0:T(8,128)(2,1)}, bf16[64,16,256]{2,1,0:T(8,128)(2,1)}, u32[]{:S(2)}, u32[]{:S(2)}) collective-permute-start(bf16[64,16,256]{2,1,0:T(8,128)(2,1)} %get-tuple-element.95), channel_id=1, source_target_pairs={{0,8},{4,12},{8,0},{12,4},{1,9},{5,13},{9,1},{13,5},{2,10},{6,14},... | collective-permute-start | bytes 1572872 | tf_op jit(solution)/shard_map/ppermute | solution.py:29
  324.1 41.5 %collective-permute-start.15 = (bf16[64,16,256]{2,1,0:T(8,128)(2,1)}, bf16[64,16,256]{2,1,0:T(8,128)(2,1)}, u32[]{:S(2)}, u32[]{:S(2)}) collective-permute-start(bf16[64,16,256]{2,1,0:T(8,128)(2,1)} %get-tuple-element.93), channel_id=1, source_target_pairs={{0,12},{4,8},{8,4},{12,0},{1,13},{5,9},{9,5},{13,1},{2,14},{6,10},... | collective-permute-start | bytes 1572872 | tf_op jit(solution)/shard_map/ppermute | solution.py:29
  327.8 1.0 copy-start.10
  328.8 40.9 %collective-permute-start.14 = (bf16[64,16,256]{2,1,0:T(8,128)(2,1)}, bf16[64,16,256]{2,1,0:T(8,128)(2,1)}, u32[]{:S(2)}, u32[]{:S(2)}) collective-permute-start(bf16[64,16,256]{2,1,0:T(8,128)(2,1)} %get-tuple-element.92), channel_id=1, source_target_pairs={{0,12},{4,8},{8,4},{12,0},{1,13},{5,9},{9,5},{13,1},{2,14},{6,10},... | collective-permute-start | bytes 1572872 | tf_op jit(solution)/shard_map/ppermute | solution.py:29
  328.8 1.2 copy-start.13
  337.5 2.9 copy-start.5
  348.0 1.9 copy-start.9
  349.9 1.9 copy-start.11
  355.5 1.9 copy-start.7
